TPU v7x, 256 devices: a whole 4x4x8 slice. The times are simulated.
256 devices in a mesh: lat: 8 (over x, y_hi), lon: 32 (over y_lo, z, core).
Axes of the slice: x: 4, y: 4 (y_hi: 2, y_lo: 2; y = y_hi * 2 + y_lo), z: 8, core: 2. Of those that a mesh axis runs over, the one named last changes fastest.
Arguments:
- tokens: bfloat16 [96, 384, 4, 512], P('lat', 'lon'), may hold values from -6 to 6
- norm_attn: float32 [512], replicated, may hold values from 0.1 to 1.9
- w_qkv: bfloat16 [512, 1536], replicated, may hold values from -0.25 to 0.25
- pos_bias: float32 [16, 144, 144], replicated, may hold values from -4 to 400
- w_out: bfloat16 [512, 512], replicated, may hold values from -0.25 to 0.25
- norm_mlp: float32 [512], replicated, may hold values from 0.1 to 1.9
- w_up: bfloat16 [512, 2048], replicated, may hold values from -0.25 to 0.25
- w_down: bfloat16 [2048, 512], replicated, may hold values from -0.125 to 0.125
- norm_merge: float32 [2048], replicated, may hold values from 0.1 to 1.9
- w_merge: bfloat16 [2048, 1024], P(None, 'lon'), may hold values from -0.125 to 0.125
Outputs:
- merged: bfloat16 [48, 192, 4, 1024], P('lat', None, None, 'lon')
All inputs are finite; a program needn't handle non-finite values.
Results may differ from a plain program's by a relative error of at most 0.015.
Values may be sent and summed in bfloat16 or wider, within the bound.
No kernel may reach another device: no remote copies, remote signals or barrier semaphores. Data moves between devices by JAX's collectives and lax.ppermute only.
A program may use at most 128 MiB of HBM per device.

v0:
```python
import jax
import jax.numpy as jnp
from jax import lax
from jax.sharding import PartitionSpec as P

HEADS = 16
WIN_LAT = 6
WIN_LON = 12
WIN_LEV = 2
WIN_TOK = 144


EPS = 1e-05


def with_halo(cells, sides, width):
    for axis, dim in sides:
        count = lax.axis_size(axis)
        ends = count - 1
        head = lax.slice_in_dim(cells, 0, width, axis=dim)
        tail = lax.slice_in_dim(cells, cells.shape[dim] - width, cells.shape[dim], axis=dim)
        cells = jnp.concatenate(
            [
                lax.ppermute(tail, axis, [(i, (i + 1) % count) for i in range(ends)]),
                cells,
                lax.ppermute(head, axis, [((i + 1) % count, i) for i in range(ends)]),
            ],
            axis=dim,
        )
    return cells


def from_behind(block, axis, distance):
    devices = range(lax.axis_size(axis))
    route = [((i - distance) % len(devices), i) for i in devices]
    return lax.ppermute(block, axis, route)


def layer_norm(values, gain):
    mean = jnp.mean(values, axis=-1, keepdims=True)
    centred = values - mean
    spread = jnp.mean(centred * centred, axis=-1, keepdims=True)
    return centred * lax.rsqrt(spread + EPS) * gain


def to_windows(grid):
    rows, cols, levels, width = grid.shape
    shaped = grid.reshape(
        rows // WIN_LAT, WIN_LAT, cols // WIN_LON, WIN_LON, levels // WIN_LEV, WIN_LEV, width
    )
    return shaped.transpose(0, 2, 4, 1, 3, 5, 6).reshape(-1, WIN_TOK, width)


def from_windows(windows, rows, cols, levels):
    width = windows.shape[-1]
    shaped = windows.reshape(
        rows // WIN_LAT, cols // WIN_LON, levels // WIN_LEV, WIN_LAT, WIN_LON, WIN_LEV, width
    )
    return shaped.transpose(0, 3, 1, 4, 2, 5, 6).reshape(rows, cols, levels, width)


def attend(windows, allowed, norm_attn, w_qkv, pos_bias, w_out):
    count, _, width = windows.shape
    head_size = width // HEADS
    normed = layer_norm(windows.astype(jnp.float32), norm_attn).astype(jnp.bfloat16)
    projected = jnp.einsum("nqf,fe->neq", normed, w_qkv, preferred_element_type=jnp.float32).astype(
        jnp.bfloat16
    )
    projected = projected.reshape(count, 3, HEADS, head_size, WIN_TOK)
    scores = jnp.einsum(
        "nhdq,nhdk->nhqk", projected[:, 0], projected[:, 1], preferred_element_type=jnp.float32
    )
    scores = scores * head_size ** (-0.5) + pos_bias[None]
    scores = jnp.where(allowed[:, None], scores, -1e30)
    highest = jnp.max(scores, axis=-1, keepdims=True)
    expd = jnp.exp(scores - highest)
    weights = (expd / jnp.sum(expd, axis=-1, keepdims=True)).astype(jnp.bfloat16)
    mixed = jnp.einsum(
        "nhqk,nhdk->nhdq", weights, projected[:, 2], preferred_element_type=jnp.float32
    ).astype(jnp.bfloat16)
    update = jnp.einsum(
        "ncq,cm->nqm",
        mixed.reshape(count, width, WIN_TOK),
        w_out,
        preferred_element_type=jnp.float32,
    )
    return (windows.astype(jnp.float32) + update).astype(jnp.bfloat16)


def pair_norm(block, norm_merge):
    width = block.shape[-1]
    values = block.astype(jnp.float32)
    mean = jnp.mean(values, axis=(1, 3, 5), keepdims=True)
    centred = values - mean
    spread = jnp.mean(centred * centred, axis=(1, 3, 5), keepdims=True)
    gain = norm_merge.reshape(2, 2, width).transpose(1, 0, 2)[None, :, None, :, None, :]
    return (centred * lax.rsqrt(spread + EPS) * gain).astype(jnp.bfloat16)


def on_device(
    tokens, norm_attn, w_qkv, pos_bias, w_out, norm_mlp, w_up, w_down, norm_merge, w_merge
):
    lat_dev, lon_dev, levels, width = tokens.shape
    half_lat = WIN_LAT // 2
    half_lon = WIN_LON // 2
    half_lev = WIN_LEV // 2
    row_total = lat_dev + 2 * half_lat
    padded = with_halo(tokens, (("lat", 0),), half_lat)
    beyond = from_behind(padded[:, :half_lon], "lon", -1)
    region = jnp.concatenate([padded[:, half_lon:], beyond], axis=1)
    region = jnp.roll(region, -half_lev, axis=2)
    lat_all = lat_dev * lax.axis_size("lat")
    rows = lax.axis_index("lat") * lat_dev - half_lat + jnp.arange(row_total, dtype=jnp.int32)
    row_ok = (rows >= 0) & (rows < lat_all)
    lev_group = ((jnp.arange(levels, dtype=jnp.int32) + half_lev) % levels + half_lev) // WIN_LEV
    tags = jnp.where(row_ok[:, None, None], lev_group[None, None, :], -1)
    tags = jnp.broadcast_to(tags, (row_total, lon_dev, levels))
    tag_win = to_windows(tags[..., None])[..., 0]
    allowed = tag_win[:, :, None] == tag_win[:, None, :]
    result = attend(to_windows(region), allowed, norm_attn, w_qkv, pos_bias, w_out)
    attended = from_windows(result, row_total, lon_dev, levels)
    attended = jnp.roll(attended, half_lev, axis=2)[half_lat : half_lat + lat_dev]
    returned = from_behind(attended[:, lon_dev - half_lon :], "lon", 1)
    attended = jnp.concatenate([returned, attended[:, : lon_dev - half_lon]], axis=1)
    flat = attended.reshape(lat_dev * lon_dev * levels, width)
    normed = layer_norm(flat.astype(jnp.float32), norm_mlp).astype(jnp.bfloat16)
    hidden = jax.nn.gelu(
        jnp.dot(normed, w_up, preferred_element_type=jnp.float32), approximate=False
    ).astype(jnp.bfloat16)
    block = (
        flat.astype(jnp.float32) + jnp.dot(hidden, w_down, preferred_element_type=jnp.float32)
    ).astype(jnp.bfloat16)
    block = block.reshape(lat_dev // 2, 2, lon_dev // 2, 2, levels, width)
    paired = pair_norm(block, norm_merge)
    piece = lax.all_gather(w_merge, "lon", axis=1, tiled=True)
    weight = piece.reshape(2, 2, width, piece.shape[1])
    complete = jnp.einsum(
        "aibjlw,jiwm->ablm", paired, weight, preferred_element_type=jnp.float32
    ).astype(jnp.bfloat16)
    merged = lax.all_to_all(complete, "lon", split_axis=3, concat_axis=1, tiled=True)
    return merged


def solution(mesh):
    in_specs = (P("lat", "lon", None, None), P(), P(), P(), P(), P(), P(), P(), P(), P(None, "lon"))
    out_specs = P("lat", None, None, "lon")
    return jax.shard_map(
        on_device, mesh=mesh, in_specs=in_specs, out_specs=out_specs, check_vma=False
    )
```

profile of v0, /device:TPU:18, one launch (start us, length us, event | category | flops | bytes accessed | tf_op | source)
XLA Modules:
  0.0 205.6 jit_solution(13824893783571540445)
XLA Ops:
  6.5 1.2 fusion.103
  7.8 3.2 %collective-permute-start = (bf16[3,12,4,512]{3,2,1,0:T(4,128)(2,1)S(1)}, bf16[3,12,4,512]{3,2,1,0:T(4,128)(2,1)S(1)}, u32[]{:S(2)}, u32[]{:S(2)}) collective-permute-start(bf16[3,12,4,512]{3,2,1,0:T(4,128)(2,1)S(1)} %get-tuple-element.10), channel_id=1, source_target_pairs={{0,32},{32,64},{64,96},{96,128},{128,160},{160,192},{192,224},{1,3... | collective-permute-start | bytes 442376 | tf_op jit(solution)/shard_map/ppermute | solution.py:24
  11.0 4.2 %collective-permute-start.1 = (bf16[3,12,4,512]{3,2,1,0:T(4,128)(2,1)S(1)}, bf16[3,12,4,512]{3,2,1,0:T(4,128)(2,1)S(1)}, u32[]{:S(2)}, u32[]{:S(2)}) collective-permute-start(bf16[3,12,4,512]{3,2,1,0:T(4,128)(2,1)S(1)} %get-tuple-element.9), channel_id=1, source_target_pairs={{32,0},{64,32},{96,64},{128,96},{160,128},{192,160},{224,192},{33,... | collective-permute-start | bytes 442376 | tf_op jit(solution)/shard_map/ppermute | solution.py:26
  15.2 3.5 %copy.44 = f32[16,144,144]{1,2,0:T(8,128)} copy(f32[16,144,144]{2,1,0:T(8,128)} %param.13) | data formatting | bytes 2654208 | tf_op args[3]
  18.8 0.3 constant_dynamic-update-slice_fusion.1
  19.1 1.4 collective-permute-done.1
  20.6 1.1 fusion.102
  21.7 5.9 %collective-permute-start.2 = (bf16[18,6,4,512]{3,2,1,0:T(4,128)(2,1)}, bf16[18,6,4,512]{3,2,1,0:T(4,128)(2,1)S(1)}, u32[]{:S(2)}, u32[]{:S(2)}) collective-permute-start(bf16[18,6,4,512]{3,2,1,0:T(4,128)(2,1)} %get-tuple-element.8), channel_id=1, source_target_pairs={{1,0},{2,1},{3,2},{4,3},{5,4},{6,5},{7,6},{8,7},{9,8},{10,9},{11,1... | collective-permute-start | bytes 1327112 | tf_op jit(solution)/shard_map/ppermute | solution.py:36
  27.6 0.2 eq.21
  27.8 0.2 broadcast_compare_fusion
  28.0 5.8 %collective-permute-done.2 = bf16[18,6,4,512]{3,2,1,0:T(4,128)(2,1)S(1)} collective-permute-done((bf16[18,6,4,512]{3,2,1,0:T(4,128)(2,1)}, bf16[18,6,4,512]{3,2,1,0:T(4,128)(2,1)S(1)}, u32[]{:S(2)}, u32[]{:S(2)}) %collective-permute-start.2) | collective-permute-done | bytes 442400 | tf_op jit(solution)/shard_map/ppermute | solution.py:36
  33.8 0.8 slice_maximum_fusion
  34.6 2.1 %fusion.44 = f32[18,12,4,512]{3,2,1,0:T(4,128)} fusion(bf16[18,6,4,512]{3,2,1,0:T(4,128)(2,1)S(1)} %collective-permute-done.2, bf16[18,6,4,512]{3,2,1,0:T(4,128)(2,1)S(1)} %get-tuple-element.7, bf16[18,12,3,512]{3,2,1,0:T(4,128)(2,1)S(1)} %slice_maximum_fusion), kind=kLoop, calls=%fused_computation.58 | loop fusion | flops 2654208 | bytes 3317760 | tf_op jit(solution)/shard_map/convert_element_type | solution.py:87
  36.6 3.6 %reshape.205 = f32[3,6,1,12,2,2,512]{6,5,4,3,1,0,2:T(2,128)} reshape(f32[18,12,4,512]{3,2,1,0:T(4,128)} %fusion.44) | data formatting | bytes 3538944 | tf_op jit(solution)/shard_map/convert_element_type | solution.py:87
  40.2 2.2 %fusion.99 = f32[3,2,6,12,2]{4,3,2,1,0:T(8,128)S(1)} fusion(f32[3,6,1,12,2,2,512]{6,5,4,3,1,0,2:T(2,128)} %reshape.205), kind=kLoop, calls=%fused_computation.133 | loop fusion | flops 441504 | bytes 1772928 | tf_op jit(solution)/shard_map/reduce_sum | solution.py:40
  42.4 3.6 %copy.88 = f32[3,6,1,12,2,2,512]{6,5,3,1,4,0,2:T(2,128)} copy(f32[3,6,1,12,2,2,512]{6,5,4,3,1,0,2:T(2,128)} %reshape.205) | data formatting | bytes 3538944 | tf_op jit(solution)/shard_map/convert_element_type | solution.py:87
  46.1 1.4 multiply_reduce_fusion
  47.5 0.2 div.41
  47.7 0.2 rsqrt.31
  47.9 3.3 %reshape.201 = f32[6,144,512]{2,1,0:T(8,128)} reshape(f32[3,1,2,6,12,2,512]{6,5,4,3,2,0,1:T(2,128)} %bitcast.82) | data formatting | bytes 3538944 | tf_op jit(solution)/shard_map/convert_element_type | solution.py:87
  51.3 5.1 %fusion.19 = bf16[6,1536,144]{1,2,0:T(8,128)(2,1)} fusion(bf16[512,1536]{1,0:T(8,128)(2,1)} %param.12, f32[6,144,512]{2,1,0:T(8,128)} %reshape.201, f32[512]{0:T(512)S(1)} %copy-done.7, f32[6,144]{1,0:T(8,128)S(1)} %rsqrt.31, f32[6,144]{1,0:T(8,128)S(1)} %div.41), kind=kOutput, calls=%fused_computation.32 | convolution fusion | flops 1362051072 | bytes 6005504 | tf_op jit(solution)/shard_map/nqf,fe->neq/dot_general | solution.py:66
  56.3 6.1 %copy.40 = bf16[6,1536,144]{2,1,0:T(8,128)(2,1)} copy(bf16[6,1536,144]{1,2,0:T(8,128)(2,1)} %fusion.19) | data formatting | bytes 5308416 | tf_op jit(solution)/shard_map/convert_element_type | solution.py:66
  62.4 10.6 %fusion.104 = (f32[6,16,144]{2,1,0:T(8,128)S(1)}, f32[6,16,144,144]{2,3,1,0:T(8,128)}) fusion(f32[16,144,144]{1,2,0:T(8,128)} %copy.44, pred[6,144,144]{1,2,0:T(8,128)(4,1)S(1)} %broadcast_compare_fusion, bf16[6,3,16,32,144]{4,3,2,1,0:T(8,128)(2,1)} %bitcast.83), kind=kOutput, calls=%fused_computation.137 | convolution fusion | flops 137355408 | bytes 13647360 | tf_op jit(solution)/shard_map/sub | solution.py:76
  73.0 6.8 %fusion.22 = bf16[6,16,32,144]{3,2,1,0:T(8,128)(2,1)S(1)} fusion(f32[6,16,144,144]{2,3,1,0:T(8,128)} %get-tuple-element.12, f32[6,16,144]{2,1,0:T(8,128)S(1)} %get-tuple-element.11, bf16[6,3,16,32,144]{4,3,2,1,0:T(8,128)(2,1)} %bitcast.84), kind=kOutput, calls=%fused_computation.38 | convolution fusion | flops 131825664 | bytes 16668672 | tf_op jit(solution)/shard_map/nhqk,nhdk->nhdq/dot_general | solution.py:78
  79.8 0.7 add_convert_fusion
  80.5 1.3 reshape.197
  81.8 3.0 %copy.89 = bf16[3,1,2,6,12,2,512]{6,5,2,4,3,0,1:T(2,128)(2,1)} copy(bf16[3,1,2,6,12,2,512]{6,5,4,3,2,0,1:T(2,128)(2,1)} %reshape.197) | data formatting | bytes 1769472 | tf_op jit(solution)/shard_map/reshape | solution.py:56
  84.7 2.6 %reshape.198 = bf16[18,12,4,512]{3,2,1,0:T(4,128)(2,1)S(1)} reshape(bf16[3,6,1,12,2,2,512]{6,5,4,3,1,0,2:T(2,128)(2,1)} %bitcast.88) | data formatting | bytes 1769472 | tf_op jit(solution)/shard_map/reshape | solution.py:59
  87.4 0.5 slice.66
  87.9 1.0 pad_maximum_fusion.2
  88.9 8.6 %collective-permute-done.3 = bf16[12,6,4,512]{3,2,1,0:T(4,128)(2,1)} collective-permute-done((bf16[12,6,4,512]{3,2,1,0:T(4,128)(2,1)}, bf16[12,6,4,512]{3,2,1,0:T(4,128)(2,1)}, u32[]{:S(2)}, u32[]{:S(2)}) %collective-permute-start.3) | collective-permute-done | bytes 294944 | tf_op jit(solution)/shard_map/ppermute | solution.py:36
  97.5 2.5 %fusion.100 = (f32[12,12,4]{2,1,0:T(8,128)S(1)}, f32[12,12,4,512]{3,2,1,0:T(4,128)}) fusion(bf16[18,12,3,512]{3,2,1,0:T(4,128)(2,1)S(1)} %bitcast.81, bf16[18,12,1,512]{3,2,1,0:T(2,128)(2,1)S(1)} %slice.66, bf16[12,6,4,512]{3,2,1,0:T(4,128)(2,1)} %collective-permute-done.3), kind=kLoop, calls=%fused_computation.134 | loop fusion | flops 2063808 | bytes 2361600 | tf_op jit(solution)/shard_map/reduce_sum | solution.py:40
  100.0 3.0 %reshape.202 = f32[576,512]{1,0:T(8,128)} reshape(f32[12,12,4,512]{3,2,1,0:T(4,128)} %get-tuple-element.6) | data formatting | bytes 2359296 | tf_op jit(solution)/shard_map/convert_element_type | solution.py:131
  103.2 1.7 multiply_reduce_fusion.2
  105.1 14.1 %fusion.105 = (f32[576]{0:T(1024)S(1)}, f32[576,512]{1,0:T(8,128)S(1)}) fusion(f32[576,512]{1,0:T(8,128)} %reshape.202, bf16[2048,512]{1,0:T(8,128)(2,1)S(1)} %copy-done, bf16[512,2048]{1,0:T(8,128)(2,1)} %param.16, f32[512]{0:T(512)S(1)} %copy-done.8, f32[576]{0:T(1024)S(1)} %rsqrt.33, f32[576]{0:T(1024)S(1)} %div.49), kind=kOutput, calls=%fused_computation.138 | convolution fusion | flops 2494955008 | bytes 6562560 | tf_op jit(solution)/shard_map/dot_general | solution.py:131
  119.2 0.2 reduce_sum.83
  119.7 0.3 reshape.203
  120.1 0.3 multiply_reduce_fusion.1
  120.3 0.2 reduce_sum.86
  120.7 6.4 %copy.52 = bf16[2048,1024]{1,0:T(8,128)(2,1)} copy(bf16[2048,1024]{0,1:T(8,128)(2,1)} %all-gather.2.cloned.1.call-done) | data formatting | bytes 8388608 | tf_op jit(solution)/shard_map/all_gather | solution.py:135
  127.1 4.7 %fusion.40 = bf16[6,6,4,1024]{3,1,2,0:T(8,128)(2,1)S(1)} fusion(bf16[2,2,512,1024,1,1]{3,2,1,0,5,4:T(8,128)(2,1)} %bitcast.87, f32[6,2,6,2,4,512]{5,4,3,2,1,0:T(4,128)S(1)} %reshape.203, f32[2,2,512]{2,1,0:T(2,128)S(1)} %copy.51, f32[6,6,4]{1,2,0:T(4,128)S(1)} %copy.50, f32[6,6,4]{1,2,0:T(4,128)S(1)} %copy.48), kind=kOutput, calls=%fused_computation.52 | convolution fusion | flops 605306880 | bytes 5678208 | tf_op jit(solution)/shard_map/aibjlw,jiwm->ablm/dot_general | solution.py:137
  131.8 7.5 %copy.54 = bf16[6,6,4,1024]{1,2,0,3:T(4,128)(2,1)} copy(bf16[6,6,4,1024]{3,1,2,0:T(8,128)(2,1)S(1)} %fusion.40) | data formatting | bytes 589824 | tf_op jit(solution)/shard_map/convert_element_type | solution.py:139
  139.3 10.2 %reshape.210 = bf16[32,2,2304]{2,1,0:T(2,128)(2,1)S(1)} reshape(bf16[1024,6,4,6]{3,2,1,0:T(4,128)(2,1)} %bitcast.78) | data formatting | bytes 589824
  149.5 18.8 %all_to_all.18 = bf16[32,2,2304]{2,1,0:T(2,128)(2,1)S(1)} all-to-all(bf16[32,2,2304]{2,1,0:T(2,128)(2,1)S(1)} %reshape.210), channel_id=1, replica_groups=mesh['lat'=8,'lon'=32] {'lon'}, dimensions={0} | all-to-all | bytes 589824 | tf_op jit(solution)/shard_map/all_to_all | solution.py:140
  168.3 15.5 %reshape.211 = bf16[1024,6,4,6]{3,2,1,0:T(4,128)(2,1)} reshape(bf16[32,2,2304]{2,1,0:T(2,128)(2,1)S(1)} %all_to_all.18) | data formatting | bytes 589824
  183.8 10.9 %copy.64 = bf16[6,6,4,32,32]{4,3,2,1,0:T(8,128)(2,1)S(1)} copy(bf16[6,6,4,32,32]{1,2,0,4,3:T(4,128)(2,1)} %bitcast.79) | data formatting | bytes 589824 | tf_op jit(solution)/shard_map/all_to_all | solution.py:140
  194.7 1.6 copy.56
  196.3 2.3 %copy.57 = bf16[6,192,4,32]{1,3,2,0:T(8,128)(2,1)} copy(bf16[6,192,4,32]{3,2,1,0:T(4,128)(2,1)} %bitcast.86) | data formatting | bytes 589824 | tf_op jit(solution)/shard_map/all_to_all | solution.py:140
  (45 shorter events, 1.2 us)
Async XLA Ops:
  6.5 98.5 %copy-start = (bf16[2048,512]{1,0:T(8,128)(2,1)S(1)}, bf16[2048,512]{1,0:T(8,128)(2,1)}, u32[]{:S(2)}) copy-start(bf16[2048,512]{1,0:T(8,128)(2,1)} %param.17) | copy-start | bytes 6291460
  6.5 12.3 %copy-start.4 = (bf16[12,12,4,512]{3,2,1,0:T(4,128)(2,1)S(1)}, bf16[12,12,4,512]{3,2,1,0:T(4,128)(2,1)}, u32[]{:S(2)}) copy-start(bf16[12,12,4,512]{3,2,1,0:T(4,128)(2,1)} %param.10) | copy-start | bytes 1769476
  6.5 114.2 %all-gather.2.cloned.1.call-start = ((), (), s32[]{:S(2)}) async-start(), calls=%async_computation.1 | async-start | bytes 4325376 | tf_op jit(solution)/shard_map/all_gather | solution.py:135
  7.8 11.0 %collective-permute-start = (bf16[3,12,4,512]{3,2,1,0:T(4,128)(2,1)S(1)}, bf16[3,12,4,512]{3,2,1,0:T(4,128)(2,1)S(1)}, u32[]{:S(2)}, u32[]{:S(2)}) collective-permute-start(bf16[3,12,4,512]{3,2,1,0:T(4,128)(2,1)S(1)} %get-tuple-element.10), channel_id=1, source_target_pairs={{0,32},{32,64},{64,96},{96,128},{128,160},{160,192},{192,224},{1,3... | collective-permute-start | bytes 442376 | tf_op jit(solution)/shard_map/ppermute | solution.py:24
  11.0 9.6 %collective-permute-start.1 = (bf16[3,12,4,512]{3,2,1,0:T(4,128)(2,1)S(1)}, bf16[3,12,4,512]{3,2,1,0:T(4,128)(2,1)S(1)}, u32[]{:S(2)}, u32[]{:S(2)}) collective-permute-start(bf16[3,12,4,512]{3,2,1,0:T(4,128)(2,1)S(1)} %get-tuple-element.9), channel_id=1, source_target_pairs={{32,0},{64,32},{96,64},{128,96},{160,128},{192,160},{224,192},{33,... | collective-permute-start | bytes 442376 | tf_op jit(solution)/shard_map/ppermute | solution.py:26
  21.7 12.1 %collective-permute-start.2 = (bf16[18,6,4,512]{3,2,1,0:T(4,128)(2,1)}, bf16[18,6,4,512]{3,2,1,0:T(4,128)(2,1)S(1)}, u32[]{:S(2)}, u32[]{:S(2)}) collective-permute-start(bf16[18,6,4,512]{3,2,1,0:T(4,128)(2,1)} %get-tuple-element.8), channel_id=1, source_target_pairs={{1,0},{2,1},{3,2},{4,3},{5,4},{6,5},{7,6},{8,7},{9,8},{10,9},{11,1... | collective-permute-start | bytes 1327112 | tf_op jit(solution)/shard_map/ppermute | solution.py:36
  40.2 5.9 %copy-start.2 = (f32[3,6,1,12,2,2,512]{6,5,4,3,1,0,2:T(2,128)S(1)}, f32[3,6,1,12,2,2,512]{6,5,4,3,1,0,2:T(2,128)}, u32[]{:S(2)}) copy-start(f32[3,6,1,12,2,2,512]{6,5,4,3,1,0,2:T(2,128)} %reshape.205) | copy-start | bytes 5308420
  46.1 5.2 %copy-start.7 = (f32[512]{0:T(512)S(1)}, f32[512]{0:T(512)}, u32[]{:S(2)}) copy-start(f32[512]{0:T(512)} %param.11) | copy-start | bytes 6148
  73.0 6.8 %copy-start.3 = (f32[6,144,512]{2,1,0:T(8,128)S(1)}, f32[6,144,512]{2,1,0:T(8,128)}, u32[]{:S(2)}) copy-start(f32[6,144,512]{2,1,0:T(8,128)} %reshape.201) | copy-start | bytes 5308420
  73.0 6.8 %copy-start.5 = (bf16[512,512]{1,0:T(8,128)(2,1)S(1)}, bf16[512,512]{1,0:T(8,128)(2,1)}, u32[]{:S(2)}) copy-start(bf16[512,512]{1,0:T(8,128)(2,1)} %param.14) | copy-start | bytes 1572868
  80.5 8.4 %copy-start.6 = (f32[2048]{0:T(1024)S(1)}, f32[2048]{0:T(1024)}, u32[]{:S(2)}) copy-start(f32[2048]{0:T(1024)} %param.18) | copy-start | bytes 24580
  87.4 17.7 %copy-start.8 = (f32[512]{0:T(512)S(1)}, f32[512]{0:T(512)}, u32[]{:S(2)}) copy-start(f32[512]{0:T(512)} %param.15) | copy-start | bytes 6148
  88.9 8.6 %collective-permute-start.3 = (bf16[12,6,4,512]{3,2,1,0:T(4,128)(2,1)}, bf16[12,6,4,512]{3,2,1,0:T(4,128)(2,1)}, u32[]{:S(2)}, u32[]{:S(2)}) collective-permute-start(bf16[12,6,4,512]{3,2,1,0:T(4,128)(2,1)} %pad_maximum_fusion.2), channel_id=1, source_target_pairs={{31,0},{0,1},{1,2},{2,3},{3,4},{4,5},{5,6},{6,7},{7,8},{8,9},{9,10... | collective-permute-start | bytes 884744 | tf_op jit(solution)/shard_map/ppermute | solution.py:36
  183.8 14.8 %copy-start.1 = (bf16[2048,512]{1,0:T(8,128)(2,1)S(1)}, bf16[2048,512]{1,0:T(8,128)(2,1)}, u32[]{:S(2)}) copy-start(bf16[2048,512]{1,0:T(8,128)(2,1)} %param.17) | copy-start | bytes 6291460
Sparse Core Ops, SparseCore 0:
  15.3 71.1 all-gather.1
where the time goes:
time: 209 us; the launch traced here: 206 us
  local copies, waits for them, and re-layouts  89.3 us (43%)
  matrix products  41.9 us (20%)
  blocking collectives  18.8 us (9%)
  waiting for transfers between devices  15.9 us (8%)
  between operations  13.9 us (7%)
  starting transfers between devices  13.2 us (6%)
  other arithmetic  12.6 us (6%)
    unnamed x23, local copies, waits for them, and re-layouts  29.5 us
    all_to_all x1, blocking collectives, on_device(): lax.all_to_all(complete, 'lon', split_axis=3, concat_axis=1, tiled=True)  18.8 us
    all_to_all x3, local copies, waits for them, and re-layouts, on_device(): lax.all_to_all(complete, 'lon', split_axis=3, concat_axis=1, tiled=True)  14.8 us
    ppermute x2, waiting for transfers between devices, from_behind(): return lax.ppermute(block, axis, route)  14.4 us
    dot_general x1, matrix products, on_device(): jnp.dot(hidden, w_down, preferred_element_type=jnp.float32)  14.1 us
    sub x1, matrix products, attend(): expd = jnp.exp(scores - highest)  10.6 us
    convert_element_type x3, local copies, waits for them, and re-layouts, attend(): return (windows.astype(jnp.float32) + update).astype(jnp.bfloat16)  10.6 us
    convert_element_type x1, local copies, waits for them, and re-layouts, on_device(): complete = jnp.einsum('aibjlw,jiwm->ablm', paired, weight, preferred_elem...  7.53 us
  transfers between devices with their start and end apart: 5, of which 3 were waited for; matrix products, arithmetic and copies ran while one was open for 41% of the time, Pallas kernels for 0%

commit v1 on v0

v1 whole, which is shorter than its diff:
```python
import functools

import jax
import jax.numpy as jnp
import numpy as np
from jax import lax
from jax.experimental import pallas as pl
from jax.experimental.pallas import tpu as pltpu
from jax.sharding import PartitionSpec as P

HEADS = 16
HEAD_DIM = 32
WIDTH = 512
FFN = 2048
ROWS = 12
HALF = 6
WIN = 144
HALF_WIN = 72
BAND = 288
LOG2E = 1.4426950408889634
EPS = 1e-05
BIG = -1e30
BF = jnp.bfloat16
F32 = jnp.float32
LEVELS = ((1, 2), (3, 0))
MERGE_PAD = 40


def dot(a, b, dims=((1,), (0,))):
    return lax.dot_general(a, b, (dims, ((), ())), preferred_element_type=F32)


NT = ((1,), (1,))


def window_order():
    order = []
    for ihalf in range(2):
        for k in range(2):
            for i3 in range(3):
                for j in range(12):
                    order.append(((ihalf * 3 + i3) * 12 + j) * 2 + k)
    return order


def bias_permutation():
    out = np.zeros((WIN, WIN), np.float32)
    out[np.arange(WIN), window_order()] = 1
    return out


def band_permutation():
    out = np.zeros((BAND, BAND), np.float32)
    n = 0
    for t in range(2):
        for ihalf in range(2):
            for k in range(2):
                for i3 in range(3):
                    for j in range(12):
                        i, half, c = ihalf * 3 + i3, j // 6, j % 6
                        out[n, half * 144 + i * 24 + c * 4 + LEVELS[t][k]] = 1
                        n += 1
    return out


def merge_permutation():
    first = np.zeros((4, 4, MERGE_PAD, BAND), np.float32)
    second = np.zeros((4, 4, MERGE_PAD, BAND), np.float32)
    place = {LEVELS[t][k]: (t, k) for t in range(2) for k in range(2)}
    for dj in range(2):
        for di in range(2):
            for lev in range(4):
                t, k = place[lev]
                for b in range(6):
                    for a in range(6):
                        r, j = 2 * a + di, 2 * b + dj
                        row = (dj * 2 + di, lev, b * 6 + a)
                        if 3 <= r < 9:
                            i = r - 3
                            first[row + (t * 144 + (i // 3) * 72 + k * 36 + (i % 3) * 12 + j,)] = 1
                        else:
                            band = int(r >= 9)
                            i3 = r - 9 if band else r
                            second[row + ((band * 2 + t) * 72 + k * 36 + i3 * 12 + j,)] = 1
    shape = (4, 4 * MERGE_PAD, BAND)
    return first.reshape(shape), second.reshape(shape)


def normalise(x, gain):
    mean = jnp.sum(x, axis=-1, keepdims=True) * (1.0 / WIDTH)
    centred = x - mean
    spread = jnp.sum(centred * centred, axis=-1, keepdims=True) * (1.0 / WIDTH)
    return centred * lax.rsqrt(spread + EPS) * gain


def split3(x):
    hi = x.astype(BF)
    rest = x - hi.astype(F32)
    mid = rest.astype(BF)
    return hi, mid, (rest - mid.astype(F32)).astype(BF)


def prepare_kernel(bias_ref, wqkv_ref, perm_ref, eye_ref, bias_out, wvt_out):
    perm = perm_ref[...]

    def head(h, carry):
        b = bias_ref[h] * LOG2E
        y = sum(dot(perm, part, NT) for part in split3(b))
        bias_out[h] = sum(dot(part, perm, NT) for part in split3(y))
        return carry

    lax.fori_loop(0, HEADS, head, 0, unroll=4)
    wvt_out[...] = dot(eye_ref[...], wqkv_ref[:, 2 * WIDTH :], NT).astype(BF)


def attend_window(x, normed, q, k, vt_ref, mixt_ref, bias_ref, kaug, qaug, wvt, q_from, q_count):
    q = q[q_from : q_from + q_count].astype(BF)
    k = k.astype(BF)
    vt_ref[...] = dot(wvt, normed, NT).astype(BF)
    lane = lax.broadcasted_iota(jnp.int32, (q_count, 128), 1) // HEAD_DIM
    for h in range(HEADS):
        tile = slice(h // 4 * 128, h // 4 * 128 + 128)
        kx = jnp.concatenate([k[:, tile], kaug], axis=1)
        qm = jnp.where(lane == h % 4, q[:, tile], jnp.zeros((), BF))
        qx = jnp.concatenate([qm, qaug], axis=1)
        s = dot(kx, qx, NT) + bias_ref[h, :, q_from : q_from + q_count]
        p = jnp.exp2(s - jnp.max(s, axis=0, keepdims=True))
        total = jnp.sum(p, axis=0, keepdims=True)
        rows = slice(h * HEAD_DIM, (h + 1) * HEAD_DIM)
        o = dot(vt_ref[rows, :], p.astype(BF))
        mixt_ref[rows, :] = (o * (1.0 / total)).astype(BF)


def feed_forward(attended, norm_mlp, up_ref, down_ref):
    normed = normalise(attended, norm_mlp).astype(BF)
    acc = attended
    step = 512
    for c in range(0, FFN, step):
        h = dot(normed, up_ref[:, c : c + step])
        h = 0.5 * h * (1.0 + lax.erf(h * 0.7071067811865476))
        acc = acc + dot(h.astype(BF), down_ref[c : c + step, :])
    return acc


def group_lanes(count):
    row = lax.broadcasted_iota(jnp.int32, (count, 128), 0)
    lane = lax.broadcasted_iota(jnp.int32, (count, 128), 1)
    return (row % HALF_WIN) // 36, row // HALF_WIN, lane


class Copies:
    def __init__(self, sems):
        self.sems = sems
        self.made = {}

    def start(self, name, src, dst):
        copy = pltpu.make_async_copy(src, dst, self.sems.at[len(self.made)])
        copy.start()
        self.made[name] = copy

    def wait(self, name):
        self.made[name].wait()


def middle_kernel(
    left_ref, right_ref, perm_ref, eye_ref, ga_ref, gm_ref, wqkv_hbm, wvt_hbm, bias_hbm, wout_hbm, up_hbm, down_hbm,
    out_ref, wqk_ref, wvt_ref, bias_ref, wout_ref, up_ref, down_ref, vt_ref, mixt_ref, sems,
):
    copies = Copies(sems)
    copies.start("qk", wqkv_hbm.at[:, : 2 * WIDTH], wqk_ref)
    copies.start("v", wvt_hbm, wvt_ref)
    copies.start("bias", bias_hbm, bias_ref)
    copies.start("out", wout_hbm, wout_ref)
    copies.start("up", up_hbm, up_ref)
    copies.start("down", down_hbm, down_ref)
    x = dot(perm_ref[0], left_ref[...]) + dot(perm_ref[1], right_ref[...])
    normed = normalise(x, ga_ref[...]).astype(BF)
    copies.wait("qk")
    qk = dot(normed, wqk_ref[...])
    q = qk[:, :WIDTH] * (LOG2E * HEAD_DIM**-0.5)
    k = qk[:, WIDTH:]
    group, _, lane = group_lanes(WIN)
    qaug = jnp.where(lane == group, 1.0, 0.0).astype(BF)
    copies.wait("v")
    copies.wait("bias")
    pieces = []
    for t in range(2):
        rows = slice(t * WIN, (t + 1) * WIN)
        kaug = jnp.where((lane < 2) & (lane != group), BIG if t else 0.0, 0.0).astype(BF)
        attend_window(
            x, normed[rows], q[rows], k[rows], vt_ref.at[t], mixt_ref.at[t], bias_ref, kaug, qaug, wvt_ref[...], 0, WIN
        )
        pieces.append(dot(eye_ref[...], mixt_ref[t], NT).astype(BF))
    copies.wait("out")
    update = dot(jnp.concatenate(pieces, axis=0), wout_ref[...])
    attended = (x + update).astype(BF).astype(F32)
    copies.wait("up")
    copies.wait("down")
    out_ref[...] = feed_forward(attended, gm_ref[...], up_ref, down_ref).astype(BF)


def edge_kernel(
    lt_ref, rt_ref, lb_ref, rb_ref, top_ref, bottom_ref, blk1_ref, perm_ref, eye_ref, ga_ref, gm_ref, gg_ref, s1_ref, s2_ref,
    wqkv_hbm, wvt_hbm, bias_hbm, wout_hbm, up_hbm, down_hbm,
    out_ref, wqk_ref, wvt_ref, bias_ref, wout_ref, up_ref, down_ref, vt_ref, mixt_ref, sems,
):
    copies = Copies(sems)
    copies.start("qk", wqkv_hbm.at[:, : 2 * WIDTH], wqk_ref)
    copies.start("v", wvt_hbm, wvt_ref)
    copies.start("bias", bias_hbm, bias_ref)
    copies.start("out", wout_hbm, wout_ref)
    copies.start("up", up_hbm, up_ref)
    copies.start("down", down_hbm, down_ref)
    bands = (
        (top_ref[0], lt_ref[...], top_ref[1], rt_ref[...]),
        (lb_ref[...], bottom_ref[0], rb_ref[...], bottom_ref[1]),
    )
    x = jnp.concatenate([sum(dot(perm_ref[n], piece) for n, piece in enumerate(band)) for band in bands], axis=0)
    normed = normalise(x, ga_ref[...]).astype(BF)
    copies.wait("qk")
    qk = dot(normed, wqk_ref[...])
    q = qk[:, :WIDTH] * (LOG2E * HEAD_DIM**-0.5)
    k = qk[:, WIDTH:]
    group, half, lane = group_lanes(WIN)
    lat = lax.axis_index("lat")
    qgroup, _, qlane = group_lanes(HALF_WIN)
    qaug = jnp.where(qlane == qgroup, 1.0, 0.0).astype(BF)
    copies.wait("v")
    copies.wait("bias")
    pieces = []
    kept = []
    for n in range(2):
        outside = half == n
        off = jnp.where(lat == (lax.axis_size("lat") - 1 if n else 0), BIG, 0.0)
        q_from = 0 if n else HALF_WIN
        for t in range(2):
            w = n * 2 + t
            rows = slice(w * WIN, (w + 1) * WIN)
            other = jnp.where(lane != group, BIG if t else 0.0, 0.0)
            kaug = jnp.where(lane < 2, jnp.where(outside, jnp.minimum(off, other), other), 0.0).astype(BF)
            attend_window(
                x, normed[rows], q[rows], k[rows], vt_ref.at[w], mixt_ref.at[w], bias_ref, kaug, qaug, wvt_ref[...],
                q_from, HALF_WIN,
            )
            pieces.append(dot(eye_ref[...], mixt_ref[w], NT))
            kept.append(x[w * WIN + q_from : w * WIN + q_from + HALF_WIN])
    copies.wait("out")
    update = dot(jnp.concatenate(pieces, axis=0).astype(BF), wout_ref[...])
    attended = (jnp.concatenate(kept, axis=0) + update).astype(BF).astype(F32)
    copies.wait("up")
    copies.wait("down")
    block = feed_forward(attended, gm_ref[...], up_ref, down_ref).astype(BF)
    first = blk1_ref[...]
    patches = [dot(s1_ref[p], first) + dot(s2_ref[p], block) for p in range(4)]
    mean = sum(jnp.sum(v, axis=-1, keepdims=True) for v in patches) * (1.0 / (4 * WIDTH))
    centred = [v - mean for v in patches]
    spread = sum(jnp.sum(v * v, axis=-1, keepdims=True) for v in centred) * (1.0 / (4 * WIDTH))
    scale = lax.rsqrt(spread + EPS)
    for p in range(4):
        out_ref[p] = (centred[p] * scale * gg_ref[p]).astype(BF)


def merge_kernel(own_ref, other_ref, w_ref, out_ref, merged_ref, message_ref):
    core = lax.rem(lax.axis_index("lon"), 2)
    for n, ref in enumerate((own_ref, other_ref)):
        total = sum(dot(ref[p], w_ref[:, p * WIDTH : (p + 1) * WIDTH], NT) for p in range(4))
        merged_ref[core if n == 0 else 1 - core] = total
    chunk = lax.broadcasted_iota(jnp.int32, (MERGE_PAD, 128), 1) // 32
    for tile in range(4):
        for c in range(2):
            parts = [
                merged_ref[c, lev * MERGE_PAD : (lev + 1) * MERGE_PAD, tile * 128 : (tile + 1) * 128] for lev in range(4)
            ]
            for d in range(4):
                value = jnp.zeros((MERGE_PAD, 128), F32)
                for lev in range(4):
                    shift = (lev - d) % 4 * 32
                    moved = pltpu.roll(parts[lev], shift, 1) if shift else parts[lev]
                    value = jnp.where(chunk == lev, moved, value)
                message_ref[tile * 4 + d, c * 36 : c * 36 + 36, :] = value[:36]
    for block in range(16):
        z, y = block // 2, block % 2
        out_ref[y * 8 + z] = message_ref[block].astype(BF)


def unpack_kernel(in_ref, out_ref, rows_ref):
    for n in range(16):
        rows_ref[n * 72 : (n + 1) * 72, :] = in_ref[n].astype(F32)
    for a in range(6):
        piece = rows_ref[pl.ds(a, 192, stride=6), :]
        out_ref[a] = pltpu.roll(piece, 3, 0).T.astype(BF)


VMEM = pl.BlockSpec(memory_space=pltpu.VMEM)
ANY = pl.BlockSpec(memory_space=pl.ANY)


def call(kernel, out_shape, in_specs, scratch, flops, limit, name):
    out_specs = jax.tree.map(lambda _: VMEM, out_shape)
    return pl.pallas_call(
        kernel,
        out_shape=out_shape,
        in_specs=in_specs,
        out_specs=out_specs,
        scratch_shapes=scratch,
        compiler_params=pltpu.CompilerParams(vmem_limit_bytes=limit),
        cost_estimate=pl.CostEstimate(flops=flops, bytes_accessed=8 << 20, transcendentals=0),
        name=name,
    )


def weight_scratch():
    return [
        pltpu.VMEM((WIDTH, 2 * WIDTH), BF),
        pltpu.VMEM((WIDTH, WIDTH), BF),
        pltpu.VMEM((HEADS, WIN, WIN), F32),
        pltpu.VMEM((WIDTH, WIDTH), BF),
        pltpu.VMEM((WIDTH, FFN), BF),
        pltpu.VMEM((FFN, WIDTH), BF),
    ]


def on_device(tokens, norm_attn, w_qkv, pos_bias, w_out, norm_mlp, w_up, w_down, norm_merge, w_merge):
    shape = lambda s, d=BF: jax.ShapeDtypeStruct(s, d)
    lat_count = lax.axis_size("lat")
    lon_count = lax.axis_size("lon")
    chips = lon_count // 2
    half = lon_count // 2
    zs = chips // 2

    right_own = tokens[:, :HALF].reshape(BAND, WIDTH)
    left = tokens[:, HALF:].reshape(BAND, WIDTH)
    right = lax.ppermute(right_own, "lon", [((i + 1) % lon_count, i) for i in range(lon_count)])

    w_own = w_merge.T
    w_pair = lax.ppermute(w_own, "lon", [(i, (i + half) % lon_count) for i in range(lon_count)])
    first = lax.axis_index("lon") < half
    w_two = jnp.concatenate([jnp.where(first, w_own, w_pair), jnp.where(first, w_pair, w_own)], axis=0)
    rings = [[y * half + 2 * z + c for z in range(zs)] for y in range(2) for c in range(2)]
    w_cols = lax.all_gather(w_two, "lon", axis=0, tiled=True, axis_index_groups=rings)

    bias_perm = jnp.asarray(bias_permutation(), BF)
    eye = jnp.asarray(np.eye(WIDTH, dtype=np.float32), BF)
    bias, wvt = call(
        prepare_kernel, (shape((HEADS, WIN, WIN), F32), shape((WIDTH, WIDTH))), [VMEM] * 4, [], 4 * 10**9, 24 << 20, "prepare"
    )(pos_bias, w_qkv, bias_perm, eye)

    top_rows = jnp.stack([left[:HALF_WIN], right[:HALF_WIN]])
    bottom_rows = jnp.stack([left[-HALF_WIN:], right[-HALF_WIN:]])
    from_above = lax.ppermute(bottom_rows, "lat", [(i, i + 1) for i in range(lat_count - 1)])
    from_below = lax.ppermute(top_rows, "lat", [(i + 1, i) for i in range(lat_count - 1)])

    band = band_permutation()
    middle = np.zeros((2, BAND, BAND), np.float32)
    for n in range(2):
        middle[n, :, 72:216] = band[:, n * 144 : (n + 1) * 144]
    edges = np.stack([band[:, n * 72 : (n + 1) * 72] for n in range(4)])
    eye_win = jnp.asarray(np.eye(WIN, dtype=np.float32), BF)
    eye_half = jnp.asarray(np.eye(HALF_WIN, dtype=np.float32), BF)
    ga, gm = norm_attn.reshape(1, WIDTH), norm_mlp.reshape(1, WIDTH)
    weights = (w_qkv, wvt, bias, w_out, w_up, w_down)

    block1 = call(
        middle_kernel,
        shape((BAND, WIDTH)),
        [VMEM] * 6 + [ANY] * 6,
        weight_scratch()
        + [pltpu.VMEM((2, WIDTH, WIN), BF), pltpu.VMEM((2, WIDTH, WIN), BF), pltpu.SemaphoreType.DMA((6,))],
        9 * 10**9,
        40 << 20,
        "middle",
    )(left, right, jnp.asarray(middle, BF), eye_win, ga, gm, *weights)

    s1, s2 = merge_permutation()
    joined = call(
        edge_kernel,
        shape((4, 4 * MERGE_PAD, WIDTH)),
        [VMEM] * 14 + [ANY] * 6,
        weight_scratch()
        + [pltpu.VMEM((4, WIDTH, WIN), BF), pltpu.VMEM((4, WIDTH, HALF_WIN), BF), pltpu.SemaphoreType.DMA((6,))],
        10 * 10**9,
        40 << 20,
        "edges",
    )(
        top_rows[0], top_rows[1], bottom_rows[0], bottom_rows[1], from_above, from_below, block1, jnp.asarray(edges, BF),
        eye_half, ga, gm, norm_merge.reshape(4, 1, WIDTH), jnp.asarray(s1, BF), jnp.asarray(s2, BF), *weights,
    )

    neighbour = lax.ppermute(joined, "lon", [(i, i ^ 1) for i in range(lon_count)])
    messages = call(
        merge_kernel,
        shape((16, 72, 128)),
        [VMEM] * 3,
        [pltpu.VMEM((2, 4 * MERGE_PAD, WIDTH), F32), pltpu.VMEM((16, 72, 128), F32)],
        10**9,
        32 << 20,
        "merge",
    )(joined, neighbour, w_cols)
    cores = [[2 * i + c for i in range(chips)] for c in range(2)]
    received = lax.all_to_all(messages, "lon", 0, 0, tiled=True, axis_index_groups=cores)
    out = call(
        unpack_kernel, shape((6, 128, 192)), [VMEM], [pltpu.VMEM((1152, 128), F32)], 10**8, 16 << 20, "unpack"
    )(received)
    return out.reshape(6, 4, 32, 192).transpose(0, 3, 1, 2)


def solution(mesh):
    in_specs = (P("lat", "lon", None, None), P(), P(), P(), P(), P(), P(), P(), P(), P(None, "lon"))
    out_specs = P("lat", None, None, "lon")
    return jax.shard_map(on_device, mesh=mesh, in_specs=in_specs, out_specs=out_specs, check_vma=False)
```

time: 209 us -> 94.4 us (0.45)
  local copies, waits for them, and re-layouts: 89.3 us -> 8.01 us
  matrix products: 41.9 us -> 0 us
  Pallas kernels: 0 us -> 34.3 us
  other arithmetic: 12.6 us -> 1.68 us
  waiting for transfers between devices: 15.9 us -> 6.27 us
  blocking collectives: 18.8 us -> 15 us
    pallas_call x0 -> x5, Pallas kernels: none -> 34.3 us  [the longest x1 17.9 us: on_device(): call(edge_kernel, shape((4, 4 * MERGE_PAD, WIDTH)), [VMEM] * 14 + [ANY] *...]
    dot_general x5 -> x0, matrix products: 31.3 us -> none  [the longest x1 14.1 us: on_device(): jnp.dot(hidden, w_down, preferred_element_type=jnp.float32)]
    convert_element_type x7 -> x0, local copies, waits for them, and re-layouts: 27.5 us -> none  [the longest x3 10.6 us: attend(): return (windows.astype(jnp.float32) + update).astype(jnp.bfloat16)]
    unnamed x23 -> x38, local copies, waits for them, and re-layouts: 29.5 us -> 4.13 us
    all_to_all x3 -> x0, local copies, waits for them, and re-layouts: 14.8 us -> none  [on_device(): lax.all_to_all(complete, 'lon', split_axis=3, concat_axis=1, tiled=True)]
    sub x1 -> x0, matrix products: 10.6 us -> none  [attend(): expd = jnp.exp(scores - highest)]
    ppermute x4 -> x5, waiting for transfers between devices: 15.8 us -> 6.26 us  [the longest x1 4.16 us: on_device(): lax.ppermute(w_own, 'lon', [(i, (i + half) % lon_count) for i in range(lo...]
    reduce_sum x7 -> x0, other arithmetic: 8.27 us -> none  [the longest x2 4.69 us: layer_norm(): mean = jnp.mean(values, axis=-1, keepdims=True)]
  transfers between devices with their start and end apart: 5 -> 6, of which waited for: 3 -> 2; matrix products, arithmetic and copies ran while one was open for 41% -> 4% of each run, Pallas kernels for 0% -> 34%
where the time goes in v1:
time: 94.4 us; the launch traced here: 92.9 us
  Pallas kernels  34.3 us (36%)
  blocking collectives  15 us (16%)
  starting transfers between devices  13.9 us (15%)
  between operations  13.7 us (15%)
  local copies, waits for them, and re-layouts  8.01 us (8%)
  waiting for transfers between devices  6.27 us (7%)
  other arithmetic  1.68 us (2%)
    pallas_call x1, Pallas kernels, on_device(): call(edge_kernel, shape((4, 4 * MERGE_PAD, WIDTH)), [VMEM] * 14 + [ANY] *...  17.9 us
    all_to_all x1, blocking collectives, on_device(): lax.all_to_all(messages, 'lon', 0, 0, tiled=True, axis_index_groups=cores)  15 us
    pallas_call x1, Pallas kernels, on_device(): call(middle_kernel, shape((BAND, WIDTH)), [VMEM] * 6 + [ANY] * 6, weight_...  9.52 us
    ppermute x1, starting transfers between devices, on_device(): lax.ppermute(right_own, 'lon', [((i + 1) % lon_count, i) for i in range(l...  5.14 us
    ppermute x1, waiting for transfers between devices, on_device(): lax.ppermute(w_own, 'lon', [(i, (i + half) % lon_count) for i in range(lo...  4.16 us
    unnamed x38, local copies, waits for them, and re-layouts  4.13 us
    ppermute x1, starting transfers between devices, on_device(): lax.ppermute(top_rows, 'lat', [(i + 1, i) for i in range(lat_count - 1)])  3.88 us
    pallas_call x1, Pallas kernels, on_device(): call(prepare_kernel, (shape((HEADS, WIN, WIN), F32), shape((WIDTH, WIDTH)...  3.71 us
  transfers between devices with their start and end apart: 6, of which 2 were waited for; matrix products, arithmetic and copies ran while one was open for 4% of the time, Pallas kernels for 34%

profile of v1, /device:TPU:18, one launch (start us, length us, event | category | flops | bytes accessed | tf_op | source)
XLA Modules:
  0.0 92.9 jit_solution(1402333752361690148)
XLA Ops:
  6.5 0.0 all-gather.2.cloned.1.call-start
  6.5 1.3 %collective-permute-start.4 = (bf16[32,2048]{1,0:T(8,128)(2,1)}, bf16[32,2048]{1,0:T(8,128)(2,1)S(1)}, u32[]{:S(2)}, u32[]{:S(2)}) collective-permute-start(bf16[32,2048]{1,0:T(8,128)(2,1)} %bitcast.18), channel_id=1, source_target_pairs={{0,16},{1,17},{2,18},{3,19},{4,20},{5,21},{6,22},{7,23},{8,24},{9,... | collective-permute-start | bytes 393224 | tf_op jit(solution)/shard_map/ppermute | solution.py:336
  7.8 4.2 %collective-permute-done.4 = bf16[32,2048]{1,0:T(8,128)(2,1)S(1)} collective-permute-done((bf16[32,2048]{1,0:T(8,128)(2,1)}, bf16[32,2048]{1,0:T(8,128)(2,1)S(1)}, u32[]{:S(2)}, u32[]{:S(2)}) %collective-permute-start.4) | collective-permute-done | bytes 131104 | tf_op jit(solution)/shard_map/ppermute | solution.py:336
  12.0 0.9 broadcast_select_fusion.1
  12.9 0.0 copy-start.1
  12.9 0.0 copy-start.16
  12.9 0.7 pad_maximum_fusion
  13.7 0.0 all-gather.2.cloned.1.call-update
  13.7 1.3 %fusion = (bf16[12,6,4,512]{3,2,1,0:T(4,128)(2,1)S(1)}, bf16[12,6,4,512]{3,2,1,0:T(4,128)(2,1)S(1)}) fusion(bf16[12,12,4,512]{3,2,1,0:T(4,128)(2,1)} %param.18), kind=kLoop, calls=%fused_computation.7 | loop fusion | bytes 1179648 | tf_op jit(solution)/shard_map/slice | solution.py:332
  15.0 0.8 reshape.22
  15.8 5.1 %collective-permute-start = (bf16[288,512]{1,0:T(8,128)(2,1)}, bf16[288,512]{1,0:T(8,128)(2,1)S(1)}, u32[]{:S(2)}, u32[]{:S(2)}) collective-permute-start(bf16[288,512]{1,0:T(8,128)(2,1)} %reshape.22), channel_id=1, source_target_pairs={{1,0},{2,1},{3,2},{4,3},{5,4},{6,5},{7,6},{8,7},{9,8},{10,9},{11,1... | collective-permute-start | bytes 884744 | tf_op jit(solution)/shard_map/ppermute | solution.py:333
  20.9 1.0 %fusion.1 = (bf16[3,6,4,512]{3,2,1,0:T(4,128)(2,1)S(1)}, bf16[3,6,4,512]{3,2,1,0:T(4,128)(2,1)S(1)}) fusion(bf16[12,12,4,512]{3,2,1,0:T(4,128)(2,1)} %param.18), kind=kLoop, calls=%fused_computation.8 | loop fusion | bytes 294912 | tf_op jit(solution)/shard_map/slice | solution.py:349
  22.0 0.6 stack.18
  22.6 0.1 reshape.23.left_ref
  22.7 0.0 copy-done.1
  22.7 0.0 copy-done.16
  22.7 0.0 copy-start.4
  22.7 1.4 %copy-done.4 = bf16[512,1536]{1,0:T(8,128)(2,1)S(1)} copy-done((bf16[512,1536]{1,0:T(8,128)(2,1)S(1)}, bf16[512,1536]{1,0:T(8,128)(2,1)}, u32[]{:S(2)}) %copy-start.4) | copy-done | bytes 1572888
  24.1 1.0 %copy-done.10 = bf16[512,512]{1,0:T(8,128)(2,1)S(1)} copy-done((bf16[512,512]{1,0:T(8,128)(2,1)S(1)}, bf16[512,512]{1,0:T(8,128)(2,1)}, u32[]{:S(2)}) %copy-start.10) | copy-done | bytes 524312
  25.2 0.0 copy-start.6
  25.2 0.0 copy-start.8
  25.2 0.0 copy-start.9
  25.2 0.0 copy-start.13
  25.2 0.0 copy-start.15
  25.3 3.7 %prepare.1 = (f32[16,144,144]{2,1,0:T(8,128)S(1)}, bf16[512,512]{1,0:T(8,128)(2,1)S(1)}) custom-call(f32[16,144,144]{2,1,0:T(8,128)S(1)} %copy-done.1, bf16[512,1536]{1,0:T(8,128)(2,1)S(1)} %copy-done.4, bf16[144,144]{1,0:T(8,128)(2,1)S(1)} %copy-done.16, bf16[512,512]{1,0:T(8,128)(2,1)S(1)} %copy-done.10), custom_call_target="tpu_custom_call" | custom-call | flops 4000000000 | bytes 8388608 | tf_op jit(solution)/shard_map/prepare/pallas_call | solution.py:344
  29.0 0.0 collective-permute-done.right_ref
  29.0 0.0 copy-done.18
  29.0 3.5 %collective-permute-start.1 = (bf16[2,72,512]{2,1,0:T(8,128)(2,1)S(1)}, bf16[2,72,512]{2,1,0:T(8,128)(2,1)S(1)}, u32[]{:S(2)}, u32[]{:S(2)}) collective-permute-start(bf16[2,72,512]{2,1,0:T(8,128)(2,1)S(1)} %pad_maximum_fusion.1), channel_id=1, source_target_pairs={{0,32},{32,64},{64,96},{96,128},{128,160},{160,192},{192,224},{1,3... | collective-permute-start | bytes 442376 | tf_op jit(solution)/shard_map/ppermute | solution.py:350
  32.5 3.9 %collective-permute-start.2 = (bf16[2,72,512]{2,1,0:T(8,128)(2,1)S(1)}, bf16[2,72,512]{2,1,0:T(8,128)(2,1)S(1)}, u32[]{:S(2)}, u32[]{:S(2)}) collective-permute-start(bf16[2,72,512]{2,1,0:T(8,128)(2,1)S(1)} %pad_maximum_fusion.2), channel_id=1, source_target_pairs={{32,0},{64,32},{96,64},{128,96},{160,128},{192,160},{224,192},{33,... | collective-permute-start | bytes 442376 | tf_op jit(solution)/shard_map/ppermute | solution.py:351
  36.4 0.0 copy-done.2
  36.4 0.0 copy-done.3
  36.4 0.0 copy-done.5
  36.5 0.0 copy-done.6
  36.5 0.0 copy-start.7
  36.5 0.0 copy-start.11
  36.5 0.0 copy-start.12
  36.5 0.0 copy-start.14
  36.6 0.0 copy-start.17
  36.6 9.5 %middle.1.blk1_ref = bf16[288,512]{1,0:T(8,128)(2,1)S(1)} custom-call(bf16[288,512]{1,0:T(8,128)(2,1)S(1)} %reshape.23.left_ref, bf16[288,512]{1,0:T(8,128)(2,1)S(1)} %collective-permute-done.right_ref, bf16[2,288,288]{2,1,0:T(8,128)(2,1)S(1)} %copy-done.13, bf16[144,144]{1,0:T(8,128)(2,1)S(1)} %copy-done.15, f32[1,512]{1,0:T(1,128)S(1)} %bitcast.14, ...), custom_call_target="tpu_custom_call" | custom-call | flops 8999999488 | bytes 8388608 | tf_op jit(solution)/shard_map/middle/pallas_call | solution.py:363
  46.1 0.0 collective-permute-done.1.top_ref
  46.1 0.0 collective-permute-done.2.bottom_ref
  46.2 17.9 %edges.1.own_ref = bf16[4,160,512]{2,1,0:T(8,128)(2,1)S(1)} custom-call(bf16[72,512]{1,0:T(8,128)(2,1)S(1)} %slice.27.lt_ref, bf16[72,512]{1,0:T(8,128)(2,1)S(1)} %get-tuple-element.16.rt_ref, bf16[72,512]{1,0:T(8,128)(2,1)S(1)} %slice.31.lb_ref, bf16[72,512]{1,0:T(8,128)(2,1)S(1)} %get-tuple-element.15.rb_ref, ...), custom_call_target="tpu_custom_call" | custom-call | flops 10000000000 | bytes 8388608 | tf_op jit(solution)/shard_map/edges/pallas_call | solution.py:375
  64.1 0.1 collective-permute-start.3
  64.2 2.1 %collective-permute-done.3.other_ref = bf16[4,160,512]{2,1,0:T(8,128)(2,1)S(1)} collective-permute-done((bf16[4,160,512]{2,1,0:T(8,128)(2,1)S(1)}, bf16[4,160,512]{2,1,0:T(8,128)(2,1)S(1)}, u32[]{:S(2)}, u32[]{:S(2)}) %collective-permute-start.3) | collective-permute-done | bytes 655392 | tf_op jit(solution)/shard_map/ppermute | solution.py:389
  66.3 1.6 %copy-done = bf16[512,2048]{1,0:T(8,128)(2,1)S(1)} copy-done((bf16[512,2048]{1,0:T(8,128)(2,1)S(1)}, bf16[512,2048]{1,0:T(8,128)(2,1)}, u32[]{:S(2)}) %copy-start) | copy-done | bytes 2097176
  67.9 2.1 %merge.1 = bf16[16,72,128]{2,1,0:T(8,128)(2,1)S(1)} custom-call(bf16[4,160,512]{2,1,0:T(8,128)(2,1)S(1)} %edges.1.own_ref, bf16[4,160,512]{2,1,0:T(8,128)(2,1)S(1)} %collective-permute-done.3.other_ref, bf16[512,2048]{1,0:T(8,128)(2,1)S(1)} %copy-done), custom_call_target="tpu_custom_call" | custom-call | flops 1000000000 | bytes 8388608 | tf_op jit(solution)/shard_map/merge/pallas_call | solution.py:390
  70.0 15.0 %all_to_all.5.in_ref = bf16[16,72,128]{2,1,0:T(8,128)(2,1)S(1)} all-to-all(bf16[16,72,128]{2,1,0:T(8,128)(2,1)S(1)} %merge.1), channel_id=1, replica_groups={{0,2,4,6,8,10,12,14,16,18,20,22,24,26,28,30},{1,3,5,7,9,11,13,15,17,19,..., dimensions={0} | all-to-all | bytes 589824 | tf_op jit(solution)/shard_map/all_to_all | solution.py:400
  85.1 1.0 %unpack.1 = bf16[6,128,192]{2,1,0:T(8,128)(2,1)} custom-call(bf16[16,72,128]{2,1,0:T(8,128)(2,1)S(1)} %all_to_all.5.in_ref), custom_call_target="tpu_custom_call" | custom-call | flops 100000000 | bytes 8388608 | tf_op jit(solution)/shard_map/unpack/pallas_call | solution.py:401
  (22 shorter events, 0.2 us)
Async XLA Ops:
  6.5 59.8 %all-gather.2.cloned.1.call-start = ((), (), s32[]{:S(2)}) async-start(), calls=%async_computation.1 | async-start | bytes 2359296 | tf_op jit(solution)/shard_map/all_gather | solution.py:340
  6.5 5.4 %collective-permute-start.4 = (bf16[32,2048]{1,0:T(8,128)(2,1)}, bf16[32,2048]{1,0:T(8,128)(2,1)S(1)}, u32[]{:S(2)}, u32[]{:S(2)}) collective-permute-start(bf16[32,2048]{1,0:T(8,128)(2,1)} %bitcast.18), channel_id=1, source_target_pairs={{0,16},{1,17},{2,18},{3,19},{4,20},{5,21},{6,22},{7,23},{8,24},{9,... | collective-permute-start | bytes 393224 | tf_op jit(solution)/shard_map/ppermute | solution.py:336
  12.9 9.8 %copy-start.1 = (f32[16,144,144]{2,1,0:T(8,128)S(1)}, f32[16,144,144]{2,1,0:T(8,128)}, u32[]{:S(2)}) copy-start(f32[16,144,144]{2,1,0:T(8,128)} %bias_ref.1) | copy-start | bytes 3981316
  12.9 9.8 %copy-start.16 = (bf16[144,144]{1,0:T(8,128)(2,1)S(1)}, bf16[144,144]{1,0:T(8,128)(2,1)}, u32[]{:S(2)}) copy-start(bf16[144,144]{1,0:T(8,128)(2,1)} %constant.22.clone.perm_ref) | copy-start | bytes 124420
  15.8 13.2 %collective-permute-start = (bf16[288,512]{1,0:T(8,128)(2,1)}, bf16[288,512]{1,0:T(8,128)(2,1)S(1)}, u32[]{:S(2)}, u32[]{:S(2)}) collective-permute-start(bf16[288,512]{1,0:T(8,128)(2,1)} %reshape.22), channel_id=1, source_target_pairs={{1,0},{2,1},{3,2},{4,3},{5,4},{6,5},{7,6},{8,7},{9,8},{10,9},{11,1... | collective-permute-start | bytes 884744 | tf_op jit(solution)/shard_map/ppermute | solution.py:333
  22.7 1.4 %copy-start.4 = (bf16[512,1536]{1,0:T(8,128)(2,1)S(1)}, bf16[512,1536]{1,0:T(8,128)(2,1)}, u32[]{:S(2)}) copy-start(bf16[512,1536]{1,0:T(8,128)(2,1)} %wqkv_hbm.3) | copy-start | bytes 4718596
  24.1 1.0 %copy-start.10 = (bf16[512,512]{1,0:T(8,128)(2,1)S(1)}, bf16[512,512]{1,0:T(8,128)(2,1)}, u32[]{:S(2)}) copy-start(bf16[512,512]{1,0:T(8,128)(2,1)} %constant.23.clone.eye_ref) | copy-start | bytes 1572868
  25.2 3.8 %copy-start.18 = (bf16[1,72,512]{2,1,0:T(8,128)(2,1)S(1)}, bf16[1,72,512]{2,1,0:T(8,128)(2,1)}, u32[]{:S(2)}) copy-start(bf16[1,72,512]{2,1,0:T(8,128)(2,1)} %stack.18) | copy-start | bytes 221188
  25.2 11.3 %copy-start.2 = (bf16[512,2048]{1,0:T(8,128)(2,1)S(1)}, bf16[512,2048]{1,0:T(8,128)(2,1)}, u32[]{:S(2)}) copy-start(bf16[512,2048]{1,0:T(8,128)(2,1)} %up_hbm.3) | copy-start | bytes 6291460
  25.2 11.3 %copy-start.3 = (bf16[2048,512]{1,0:T(8,128)(2,1)S(1)}, bf16[2048,512]{1,0:T(8,128)(2,1)}, u32[]{:S(2)}) copy-start(bf16[2048,512]{1,0:T(8,128)(2,1)} %down_hbm.3) | copy-start | bytes 6291460
  25.2 11.3 %copy-start.5 = (bf16[512,1536]{1,0:T(8,128)(2,1)S(1)}, bf16[512,1536]{1,0:T(8,128)(2,1)}, u32[]{:S(2)}) copy-start(bf16[512,1536]{1,0:T(8,128)(2,1)} %wqkv_hbm.3) | copy-start | bytes 4718596
  25.2 11.3 %copy-start.6 = (bf16[512,512]{1,0:T(8,128)(2,1)S(1)}, bf16[512,512]{1,0:T(8,128)(2,1)}, u32[]{:S(2)}) copy-start(bf16[512,512]{1,0:T(8,128)(2,1)} %wout_hbm.3) | copy-start | bytes 1572868
  25.2 11.3 %copy-start.8 = (f32[512]{0:T(512)S(1)}, f32[512]{0:T(512)}, u32[]{:S(2)}) copy-start(f32[512]{0:T(512)} %param.19) | copy-start | bytes 6148
  25.2 11.3 %copy-start.9 = (f32[512]{0:T(512)S(1)}, f32[512]{0:T(512)}, u32[]{:S(2)}) copy-start(f32[512]{0:T(512)} %param.23) | copy-start | bytes 6148
  25.2 11.3 %copy-start.13 = (bf16[2,288,288]{2,1,0:T(8,128)(2,1)S(1)}, bf16[2,288,288]{2,1,0:T(8,128)(2,1)}, u32[]{:S(2)}) copy-start(bf16[2,288,288]{2,1,0:T(8,128)(2,1)} %constant.26.clone.perm_ref) | copy-start | bytes 995332
  25.2 11.3 %copy-start.15 = (bf16[144,144]{1,0:T(8,128)(2,1)S(1)}, bf16[144,144]{1,0:T(8,128)(2,1)}, u32[]{:S(2)}) copy-start(bf16[144,144]{1,0:T(8,128)(2,1)} %constant.24.clone.eye_ref) | copy-start | bytes 124420
  29.0 17.1 %collective-permute-start.1 = (bf16[2,72,512]{2,1,0:T(8,128)(2,1)S(1)}, bf16[2,72,512]{2,1,0:T(8,128)(2,1)S(1)}, u32[]{:S(2)}, u32[]{:S(2)}) collective-permute-start(bf16[2,72,512]{2,1,0:T(8,128)(2,1)S(1)} %pad_maximum_fusion.1), channel_id=1, source_target_pairs={{0,32},{32,64},{64,96},{96,128},{128,160},{160,192},{192,224},{1,3... | collective-permute-start | bytes 442376 | tf_op jit(solution)/shard_map/ppermute | solution.py:350
  32.5 13.6 %collective-permute-start.2 = (bf16[2,72,512]{2,1,0:T(8,128)(2,1)S(1)}, bf16[2,72,512]{2,1,0:T(8,128)(2,1)S(1)}, u32[]{:S(2)}, u32[]{:S(2)}) collective-permute-start(bf16[2,72,512]{2,1,0:T(8,128)(2,1)S(1)} %pad_maximum_fusion.2), channel_id=1, source_target_pairs={{32,0},{64,32},{96,64},{128,96},{160,128},{192,160},{224,192},{33,... | collective-permute-start | bytes 442376 | tf_op jit(solution)/shard_map/ppermute | solution.py:351
  36.5 9.6 %copy-start.7 = (f32[2048]{0:T(1024)S(1)}, f32[2048]{0:T(1024)}, u32[]{:S(2)}) copy-start(f32[2048]{0:T(1024)} %param.26) | copy-start | bytes 24580
  36.5 9.6 %copy-start.11 = (bf16[4,160,288]{2,1,0:T(8,128)(2,1)S(1)}, bf16[4,160,288]{2,1,0:T(8,128)(2,1)}, u32[]{:S(2)}) copy-start(bf16[4,160,288]{2,1,0:T(8,128)(2,1)} %constant.28.clone.s1_ref) | copy-start | bytes 1105924
  36.5 9.6 %copy-start.12 = (bf16[4,160,288]{2,1,0:T(8,128)(2,1)S(1)}, bf16[4,160,288]{2,1,0:T(8,128)(2,1)}, u32[]{:S(2)}) copy-start(bf16[4,160,288]{2,1,0:T(8,128)(2,1)} %constant.29.clone.s2_ref) | copy-start | bytes 1105924
  36.5 9.6 %copy-start.14 = (bf16[4,288,72]{2,1,0:T(8,128)(2,1)S(1)}, bf16[4,288,72]{2,1,0:T(8,128)(2,1)}, u32[]{:S(2)}) copy-start(bf16[4,288,72]{2,1,0:T(8,128)(2,1)} %constant.27.clone.perm_ref) | copy-start | bytes 497668
  36.6 9.6 %copy-start.17 = (bf16[72,72]{1,0:T(8,128)(2,1)S(1)}, bf16[72,72]{1,0:T(8,128)(2,1)}, u32[]{:S(2)}) copy-start(bf16[72,72]{1,0:T(8,128)(2,1)} %constant.25.clone.eye_ref) | copy-start | bytes 31108
  64.1 2.2 %collective-permute-start.3 = (bf16[4,160,512]{2,1,0:T(8,128)(2,1)S(1)}, bf16[4,160,512]{2,1,0:T(8,128)(2,1)S(1)}, u32[]{:S(2)}, u32[]{:S(2)}) collective-permute-start(bf16[4,160,512]{2,1,0:T(8,128)(2,1)S(1)} %edges.1.own_ref), channel_id=1, source_target_pairs={{0,1},{1,0},{2,3},{3,2},{4,5},{5,4},{6,7},{7,6},{8,9},{9,8},{10,11... | collective-permute-start | bytes 1966088 | tf_op jit(solution)/shard_map/ppermute | solution.py:389
  66.3 1.6 %copy-start = (bf16[512,2048]{1,0:T(8,128)(2,1)S(1)}, bf16[512,2048]{1,0:T(8,128)(2,1)}, u32[]{:S(2)}) copy-start(bf16[512,2048]{1,0:T(8,128)(2,1)} %all-gather.2.cloned.1.call-done.w_ref) | copy-start | bytes 6291460
Sparse Core Ops, SparseCore 0:
  13.8 44.0 all-gather.1

commit v2 on v1

v2 whole, which is shorter than its diff:
```python
import jax
import jax.numpy as jnp
from jax import lax
from jax.experimental import pallas as pl
from jax.experimental.pallas import tpu as pltpu
from jax.sharding import PartitionSpec as P

HEADS = 16
HEAD_DIM = 32
WIDTH = 512
FFN = 2048
ROWS = 12
HALF = 6
WIN = 144
HALF_WIN = 72
BAND = 288
LOG2E = 1.4426950408889634
EPS = 1e-05
BIG = -1e30
BF = jnp.bfloat16
F32 = jnp.float32
LEVELS = ((1, 2), (3, 0))
MERGE_PAD = 40
Z_STEPS = (0, -1, -2, -3, 1, 2, 3, 4)


def dot(a, b, dims=((1,), (0,))):
    return lax.dot_general(a, b, (dims, ((), ())), preferred_element_type=F32)


NT = ((1,), (1,))


def count_steps(value, starts):
    return sum((value >= start).astype(jnp.int32) for start in starts)


def one_hot(column, width):
    lane = lax.broadcasted_iota(jnp.int32, (column.shape[0], width), 1)
    return jnp.where(lane == column, 1.0, 0.0).astype(BF)


def row_numbers(count):
    return lax.broadcasted_iota(jnp.int32, (count, 1), 0)


def split_window(n):
    ihalf = count_steps(n, (72,))
    k = count_steps(n - 72 * ihalf, (36,))
    rest = n - 72 * ihalf - 36 * k
    i3 = count_steps(rest, (12, 24))
    return ihalf, k, i3, rest - 12 * i3


def bias_permutation():
    ihalf, k, i3, j = split_window(row_numbers(WIN))
    return one_hot(2 * (36 * ihalf + 12 * i3 + j) + k, WIN)


def band_places():
    n = row_numbers(BAND)
    t = count_steps(n, (WIN,))
    ihalf, k, i3, j = split_window(n - WIN * t)
    half = count_steps(j, (6,))
    level = jnp.where(t == 0, 1 + k, 3 - 3 * k)
    return half, ihalf, 24 * i3 + 4 * (j - 6 * half) + level


def merge_places(dj, di):
    n = row_numbers(4 * MERGE_PAD)
    level = count_steps(n, (MERGE_PAD, 2 * MERGE_PAD, 3 * MERGE_PAD))
    q = n - MERGE_PAD * level
    b = count_steps(q, (6, 12, 18, 24, 30))
    r, j = 2 * (q - 6 * b) + di, 2 * b + dj
    t = jnp.where((level == 0) | (level == 3), 1, 0)
    k = jnp.where((level == 0) | (level == 2), 1, 0)
    place = 36 * k + j
    ihalf = count_steps(r, (6,))
    band = count_steps(r, (9,))
    middle = 144 * t + 72 * ihalf + 12 * (r - 3 - 3 * ihalf) + place
    edge = 72 * (2 * band + t) + 12 * (r - 9 * band) + place
    inside = (r >= 3) & (r < 9)
    real = q < 36
    return jnp.where(real & inside, middle, -1), jnp.where(real & ~inside, edge, -1)


def normalise(x, gain):
    mean = jnp.sum(x, axis=-1, keepdims=True) * (1.0 / WIDTH)
    centred = x - mean
    spread = jnp.sum(centred * centred, axis=-1, keepdims=True) * (1.0 / WIDTH)
    return centred * lax.rsqrt(spread + EPS) * gain


def split3(x):
    hi = x.astype(BF)
    rest = x - hi.astype(F32)
    mid = rest.astype(BF)
    return hi, mid, (rest - mid.astype(F32)).astype(BF)


def split_kernel(tokens_hbm, right_out, left_out, right_ref, left_ref, sems):
    parts = ((right_ref, 0, right_out), (left_ref, HALF, left_out))
    copies = []
    for n, (held, start, _) in enumerate(parts):
        copies.append(pltpu.make_async_copy(tokens_hbm.at[:, start : start + HALF], held, sems.at[n]))
        copies[-1].start()
    for copy, (held, _, out) in zip(copies, parts):
        copy.wait()
        out[...] = held[...].astype(F32).reshape(BAND, WIDTH).astype(BF)


def prepare_kernel(bias_ref, middle_out, edges_out):
    perm = bias_permutation()
    for h in range(HEADS):
        b = bias_ref[h] * LOG2E
        y = sum(dot(perm, part, NT) for part in split3(b))
        t = sum(dot(part, perm, NT) for part in split3(y))
        tile, n = h // 4, h % 4
        middle_out[tile, :, n * WIN : (n + 1) * WIN] = t
        for half in range(2):
            edges_out[half, tile, :, n * HALF_WIN : (n + 1) * HALF_WIN] = t[:, half * HALF_WIN : (half + 1) * HALF_WIN]


def attend_window(normed, q, k, bias, kaug, qaug, wvt):
    count = q.shape[0]
    k = k.astype(BF)
    vt = dot(wvt, normed, NT).astype(BF)
    lane = lax.broadcasted_iota(jnp.int32, (count, 128), 1) // HEAD_DIM
    scores = []
    for tile in range(4):
        lanes = slice(tile * 128, tile * 128 + 128)
        part = q[:, lanes]
        qm = jnp.concatenate([jnp.where(lane == n, part, 0.0) for n in range(4)], axis=0).astype(BF)
        kx = jnp.concatenate([k[:, lanes], kaug], axis=1)
        qx = jnp.concatenate([qm, qaug], axis=1)
        scores.append(dot(kx, qx, NT) + bias(tile))
    row_head = lax.broadcasted_iota(jnp.int32, (128, 4 * count), 0) // HEAD_DIM
    column = lax.broadcasted_iota(jnp.int32, (128, 4 * count), 1)
    column_head = sum((column >= n * count).astype(jnp.int32) for n in range(1, 4))
    own = row_head == column_head
    pick_row = lax.broadcasted_iota(jnp.int32, (count, 4 * count), 0)
    pick_column = lax.broadcasted_iota(jnp.int32, (count, 4 * count), 1)
    pick = sum((pick_column == pick_row + n * count).astype(F32) for n in range(4)).astype(BF)
    mixed = []
    for tile in range(4):
        s = scores[tile]
        p = jnp.exp2(s - jnp.max(s, axis=0, keepdims=True))
        inverse = 1.0 / jnp.sum(p, axis=0, keepdims=True)
        o = dot(vt[tile * 128 : tile * 128 + 128], p.astype(BF))
        mixed.append(dot(pick, jnp.where(own, o * inverse, 0.0).astype(BF), NT))
    return jnp.concatenate(mixed, axis=1)


def feed_forward(attended, norm_mlp, up_ref, down_ref):
    normed = normalise(attended, norm_mlp).astype(BF)
    acc = attended
    step = 512
    for c in range(0, FFN, step):
        h = dot(normed, up_ref[:, c : c + step])
        h = 0.5 * h * (1.0 + lax.erf(h * 0.7071067811865476))
        acc = acc + dot(h.astype(BF), down_ref[c : c + step, :])
    return acc


def group_lanes(count):
    row = lax.broadcasted_iota(jnp.int32, (count, 128), 0)
    lane = lax.broadcasted_iota(jnp.int32, (count, 128), 1)
    return (row % HALF_WIN) // 36, row // HALF_WIN, lane


def query_key(x, gain, wqkv_ref):
    normed = normalise(x, gain).astype(BF)
    qk = dot(normed, wqkv_ref[:, : 2 * WIDTH])
    return normed, qk[:, :WIDTH] * (LOG2E * HEAD_DIM**-0.5), qk[:, WIDTH:]


def middle_attention_kernel(left_ref, right_ref, ga_ref, wqkv_ref, bias_ref, wout_ref, out_ref, wvt_ref):
    half, ihalf, place = band_places()
    place = 72 + 72 * ihalf + place
    x = dot(one_hot(jnp.where(half == 0, place, -1), BAND), left_ref[...])
    x = x + dot(one_hot(jnp.where(half == 1, place, -1), BAND), right_ref[...])
    normed, q, k = query_key(x, ga_ref[...], wqkv_ref)
    group, _, lane = group_lanes(WIN)
    qgroup, _, qlane = group_lanes(4 * WIN)
    qaug = jnp.where(qlane == qgroup, 1.0, 0.0).astype(BF)
    wvt = dot(one_hot(row_numbers(WIDTH), WIDTH), wqkv_ref[:, 2 * WIDTH :], NT).astype(BF)
    wvt_ref[...] = wvt
    pieces = []
    for t in range(2):
        rows = slice(t * WIN, (t + 1) * WIN)
        kaug = jnp.where((lane < 2) & (lane != group), BIG if t else 0.0, 0.0).astype(BF)
        pieces.append(attend_window(normed[rows], q[rows], k[rows], lambda n: bias_ref[n], kaug, qaug, wvt))
    update = dot(jnp.concatenate(pieces, axis=0).astype(BF), wout_ref[...])
    out_ref[...] = (x + update).astype(BF)


def middle_mlp_kernel(x_ref, gm_ref, up_ref, down_ref, out_ref):
    out_ref[...] = feed_forward(x_ref[...].astype(F32), gm_ref[...], up_ref, down_ref).astype(BF)


def edge_attention_kernel(
    lt_ref, rt_ref, lb_ref, rb_ref, top_ref, bottom_ref, ga_ref, wqkv_ref, wvt_ref, bias_ref, wout_ref, out_ref
):
    bands = (
        (top_ref[0], lt_ref[...], top_ref[1], rt_ref[...]),
        (lb_ref[...], bottom_ref[0], rb_ref[...], bottom_ref[1]),
    )
    half, ihalf, place = band_places()
    perm = [one_hot(jnp.where(2 * half + ihalf == n, place, -1), HALF_WIN) for n in range(4)]
    x = jnp.concatenate([sum(dot(perm[n], piece) for n, piece in enumerate(band)) for band in bands], axis=0)
    normed, q, k = query_key(x, ga_ref[...], wqkv_ref)
    group, half, lane = group_lanes(WIN)
    qgroup, _, qlane = group_lanes(4 * HALF_WIN)
    qaug = jnp.where(qlane == qgroup, 1.0, 0.0).astype(BF)
    lat = lax.axis_index("lat")
    wvt = wvt_ref[...]
    pieces = []
    kept = []
    for n in range(2):
        outside = half == n
        off = jnp.where(lat == (lax.axis_size("lat") - 1 if n else 0), BIG, 0.0)
        for t in range(2):
            first = (n * 2 + t) * WIN
            rows = slice(first, first + WIN)
            queries = slice(first, first + HALF_WIN) if n else slice(first + HALF_WIN, first + WIN)
            other = jnp.where(lane != group, BIG if t else 0.0, 0.0)
            kaug = jnp.where(lane < 2, jnp.where(outside, jnp.minimum(off, other), other), 0.0).astype(BF)
            pieces.append(
                attend_window(normed[rows], q[queries], k[rows], lambda m: bias_ref[1 - n, m], kaug, qaug, wvt)
            )
            kept.append(x[queries])
    update = dot(jnp.concatenate(pieces, axis=0).astype(BF), wout_ref[...])
    out_ref[...] = (jnp.concatenate(kept, axis=0) + update).astype(BF)


def edge_mlp_kernel(x_ref, blk1_ref, gm_ref, up_ref, down_ref, gg_ref, out_ref):
    block = feed_forward(x_ref[...].astype(F32), gm_ref[...], up_ref, down_ref).astype(BF)
    first = blk1_ref[...]
    patches = []
    for p in range(4):
        middle, edge = merge_places(p // 2, p % 2)
        patches.append(dot(one_hot(middle, BAND), first) + dot(one_hot(edge, BAND), block))
    mean = sum(jnp.sum(v, axis=-1, keepdims=True) for v in patches) * (1.0 / (4 * WIDTH))
    centred = [v - mean for v in patches]
    spread = sum(jnp.sum(v * v, axis=-1, keepdims=True) for v in centred) * (1.0 / (4 * WIDTH))
    scale = lax.rsqrt(spread + EPS)
    for p in range(4):
        out_ref[p] = (centred[p] * scale * gg_ref[p]).astype(BF)


def merge_columns(joined_ref, w_refs):
    total = 0.0
    for p in range(4):
        lanes = slice(p * WIDTH, (p + 1) * WIDTH)
        w = jnp.concatenate([r[:, lanes] for r in w_refs], axis=0)
        total = total + dot(joined_ref[p], w, NT)
    return total


def merge_own_kernel(joined_ref, *refs):
    w_refs, out_ref = refs[:-1], refs[-1]
    out_ref[:, :256] = merge_columns(joined_ref, w_refs[:5])
    out_ref[:, 256:] = merge_columns(joined_ref, w_refs[5:])


def merge_kernel(joined_ref, own_ref, *refs):
    w_refs, (out_ref, merged_ref, message_ref) = refs[:-3], refs[-3:]
    lon = lax.axis_index("lon")
    chips = lax.axis_size("lon") // 2
    core = lax.rem(lon, 2)
    z = lax.rem(lon // 2, 8)
    y = lon // chips
    merged_ref[core] = own_ref[...]
    merged_ref[1 - core, :, :256] = merge_columns(joined_ref, w_refs[:5])
    merged_ref[1 - core, :, 256:] = merge_columns(joined_ref, w_refs[5:])
    chunk = lax.broadcasted_iota(jnp.int32, (MERGE_PAD, 128), 1) // 32
    for tile in range(4):
        for c in range(2):
            parts = [
                merged_ref[c, lev * MERGE_PAD : (lev + 1) * MERGE_PAD, tile * 128 : (tile + 1) * 128] for lev in range(4)
            ]
            for d in range(4):
                value = jnp.zeros((MERGE_PAD, 128), F32)
                for lev in range(4):
                    shift = (lev - d) % 4 * 32
                    moved = pltpu.roll(parts[lev], shift, 1) if shift else parts[lev]
                    value = jnp.where(chunk == lev, moved, value)
                message_ref[tile * 4 + d, c * 36 : c * 36 + 36, :] = value[:36]
    for block in range(16):
        zd = lax.rem(z + Z_STEPS[block // 2] + 8, 8)
        yd = 1 - y if block % 2 else y
        out_ref[yd * 8 + zd] = message_ref[block].astype(BF)


def unpack_kernel(in_ref, out_ref, rows_ref):
    for n in range(16):
        rows_ref[n * 72 : (n + 1) * 72, :] = in_ref[n].astype(F32)
    for a in range(6):
        piece = rows_ref[pl.ds(a, 192, stride=6), :]
        out_ref[a] = pltpu.roll(piece, 3, 0).T.astype(BF)


VMEM = pl.BlockSpec(memory_space=pltpu.VMEM)
ANY = pl.BlockSpec(memory_space=pl.ANY)


def call(kernel, out_shape, in_specs, scratch, name, limit=28):
    out_specs = jax.tree.map(lambda _: VMEM, out_shape)
    return pl.pallas_call(
        kernel,
        out_shape=out_shape,
        in_specs=in_specs,
        out_specs=out_specs,
        scratch_shapes=scratch,
        compiler_params=pltpu.CompilerParams(vmem_limit_bytes=limit << 20),
        cost_estimate=pl.CostEstimate(flops=1 << 20, bytes_accessed=1 << 16, transcendentals=0),
        name=name,
    )


def on_device(tokens, norm_attn, w_qkv, pos_bias, w_out, norm_mlp, w_up, w_down, norm_merge, w_merge):
    shape = lambda s, d=BF: jax.ShapeDtypeStruct(s, d)
    barrier = lax.optimization_barrier
    lat_count = lax.axis_size("lat")
    lon_count = lax.axis_size("lon")
    chips = lon_count // 2
    held = pltpu.VMEM((ROWS, HALF, 4, WIDTH), BF)

    def around(block, step):
        route = []
        for i in range(lon_count):
            y, z, c = i // chips, i // 2 % 8, i % 2
            route.append((i, y * chips + (z + step) % 8 * 2 + c))
        return lax.ppermute(block, "lon", route)

    w_own = w_merge.T
    w_pair = lax.ppermute(w_own, "lon", [(i, (i + chips) % lon_count) for i in range(lon_count)])
    right_own, left = call(
        split_kernel, (shape((BAND, WIDTH)),) * 2, [ANY], [held, held, pltpu.SemaphoreType.DMA((2,))], "split", 28
    )(tokens)
    right = lax.ppermute(right_own, "lon", [((i + 1) % lon_count, i) for i in range(lon_count)])
    own_up, own_down = around(w_own, 1), around(w_own, -1)
    bias_middle, bias_edges = call(
        prepare_kernel,
        (shape((4, WIN, 4 * WIN), F32), shape((2, 4, WIN, 4 * HALF_WIN), F32)),
        [VMEM],
        [],
        "prepare",
    )(pos_bias)
    bias_middle, w_pair = barrier((bias_middle, w_pair))
    pair_up, pair_down = around(w_pair, 1), around(w_pair, -1)

    top_rows = jnp.stack([left[:HALF_WIN], right[:HALF_WIN]])
    bottom_rows = jnp.stack([left[-HALF_WIN:], right[-HALF_WIN:]])
    from_above = lax.ppermute(bottom_rows, "lat", [(i, i + 1) for i in range(lat_count - 1)])
    top_rows, own_up, own_down, pair_up, pair_down = barrier((top_rows, own_up, own_down, pair_up, pair_down))
    up, down = [jnp.concatenate([own_up, pair_up], axis=0)], [jnp.concatenate([own_down, pair_down], axis=0)]
    up.append(around(up[-1], 1))
    down.append(around(down[-1], -1))
    from_below = lax.ppermute(top_rows, "lat", [(i + 1, i) for i in range(lat_count - 1)])

    ga, gm = norm_attn.reshape(1, WIDTH), norm_mlp.reshape(1, WIDTH)
    attended1, wvt = call(
        middle_attention_kernel, (shape((BAND, WIDTH)), shape((WIDTH, WIDTH))), [VMEM] * 6, [], "middle_attention"
    )(left, right, ga, w_qkv, bias_middle, w_out)
    attended1, wvt, from_above, u, d = barrier((attended1, wvt, from_above, up[-1], down[-1]))
    up.append(around(u, 1))
    down.append(around(d, -1))
    block1 = call(middle_mlp_kernel, shape((BAND, WIDTH)), [VMEM] * 4, [], "middle_mlp")(attended1, gm, w_up, w_down)
    attended2 = call(edge_attention_kernel, shape((BAND, WIDTH)), [VMEM] * 11, [], "edge_attention")(
        top_rows[0], top_rows[1], bottom_rows[0], bottom_rows[1], from_above, from_below, ga, w_qkv, wvt, bias_edges, w_out
    )
    attended2, block1, u, d = barrier((attended2, block1, up[-1], down[-1]))
    far_up, far_down = around(u[:32], 1), around(d[32:], -1)
    joined = call(edge_mlp_kernel, shape((4, 4 * MERGE_PAD, WIDTH)), [VMEM] * 6, [], "edge_mlp")(
        attended2, block1, gm, w_up, w_down, norm_merge.reshape(4, 1, WIDTH)
    )
    joined, far_up, far_down = barrier((joined, far_up, far_down))
    neighbour = lax.ppermute(joined, "lon", [(i, i ^ 1) for i in range(lon_count)])
    w_cols = [w_own, w_pair] + up + down + [far_up, far_down]
    own = call(merge_own_kernel, shape((4 * MERGE_PAD, WIDTH), F32), [VMEM] * 11, [], "merge_own")(joined, *w_cols)
    messages = call(
        merge_kernel,
        shape((16, 72, 128)),
        [VMEM] * 12,
        [pltpu.VMEM((2, 4 * MERGE_PAD, WIDTH), F32), pltpu.VMEM((16, 72, 128), F32)],
        "merge",
    )(neighbour, own, *w_cols)
    cores = [[2 * i + c for i in range(chips)] for c in range(2)]
    received = lax.all_to_all(messages, "lon", 0, 0, tiled=True, axis_index_groups=cores)
    out = call(unpack_kernel, shape((6, 128, 192)), [VMEM], [pltpu.VMEM((1152, 128), F32)],  "unpack")(received)
    return out.reshape(6, 4, 32, 192).transpose(0, 3, 1, 2)


def solution(mesh):
    in_specs = (P("lat", "lon", None, None), P(), P(), P(), P(), P(), P(), P(), P(), P(None, "lon"))
    out_specs = P("lat", None, None, "lon")
    return jax.shard_map(on_device, mesh=mesh, in_specs=in_specs, out_specs=out_specs, check_vma=False)
```

time: 94.4 us -> 76.4 us (0.81); the launches traced: 92.9 us -> 75.9 us
  Pallas kernels: 34.3 us -> 20 us
  between operations: 13.7 us -> 0.29 us
  starting transfers between devices: 13.9 us -> 25.4 us
  waiting for transfers between devices: 6.27 us -> 13.5 us
  local copies, waits for them, and re-layouts: 8.01 us -> 2.87 us
  other arithmetic: 1.68 us -> 0.03 us
  blocking collectives: 15 us -> 13.8 us
    pallas_call x4 -> x8, Pallas kernels: 33.3 us -> 19 us  [the longest x1 5.14 us: on_device(): call(edge_attention_kernel, shape((BAND, WIDTH)), [VMEM] * 11, [], 'edge_...]
    ppermute x1 -> x11, starting transfers between devices: 1.28 us -> 12.4 us  [the longest x10 11.7 us: around(): return lax.ppermute(block, 'lon', route)]
    ppermute x1, waiting for transfers between devices: 0.01 us -> 3.91 us  [on_device(): lax.ppermute(top_rows, 'lat', [(i + 1, i) for i in range(lat_count - 1)])]
    ppermute x1 -> x11, waiting for transfers between devices: 4.16 us -> 7.2 us  [the longest x10 7.2 us: around(): return lax.ppermute(block, 'lon', route)]
    slice x4 -> x2, local copies, waits for them, and re-layouts: 2.33 us -> 0.02 us  [on_device(): far_up, far_down = (around(u[:32], 1), around(d[32:], -1))]
    unnamed x38 -> x22, local copies, waits for them, and re-layouts: 4.13 us -> 2.79 us
    all_to_all x1, blocking collectives: 15 us -> 13.8 us  [on_device(): lax.all_to_all(messages, 'lon', 0, 0, tiled=True, axis_index_groups=cores)]
    ppermute x1, waiting for transfers between devices: 0.01 us -> 1.2 us  [on_device(): lax.ppermute(bottom_rows, 'lat', [(i, i + 1) for i in range(lat_count - 1)])]
  transfers between devices with their start and end apart: 6 -> 15, of which waited for: 2 -> 6; matrix products, arithmetic and copies ran while one was open for 4% -> 0% of each run, Pallas kernels for 34% -> 23%
where the time goes in v2:
time: 76.4 us; the launch traced here: 75.9 us
  starting transfers between devices  25.4 us (33%)
  Pallas kernels  20 us (26%)
  blocking collectives  13.8 us (18%)
  waiting for transfers between devices  13.5 us (18%)
  local copies, waits for them, and re-layouts  2.87 us (4%)
    all_to_all x1, blocking collectives, on_device(): lax.all_to_all(messages, 'lon', 0, 0, tiled=True, axis_index_groups=cores)  13.8 us
    ppermute x10, starting transfers between devices, around(): return lax.ppermute(block, 'lon', route)  11.7 us
    ppermute x10, waiting for transfers between devices, around(): return lax.ppermute(block, 'lon', route)  7.2 us
    ppermute x1, starting transfers between devices, on_device(): lax.ppermute(right_own, 'lon', [((i + 1) % lon_count, i) for i in range(l...  6.09 us
    pallas_call x1, Pallas kernels, on_device(): call(edge_attention_kernel, shape((BAND, WIDTH)), [VMEM] * 11, [], 'edge_...  5.14 us
    ppermute x1, waiting for transfers between devices, on_device(): lax.ppermute(top_rows, 'lat', [(i + 1, i) for i in range(lat_count - 1)])  3.91 us
    pallas_call x1, Pallas kernels, on_device(): call(middle_attention_kernel, (shape((BAND, WIDTH)), shape((WIDTH, WIDTH)...  3.8 us
    ppermute x1, starting transfers between devices, on_device(): lax.ppermute(bottom_rows, 'lat', [(i, i + 1) for i in range(lat_count - 1)])  3.46 us
  transfers between devices with their start and end apart: 15, of which 6 were waited for; matrix products, arithmetic and copies ran while one was open for 0% of the time, Pallas kernels for 23%

profile of v2, /device:TPU:18, one launch (start us, length us, event | category | flops | bytes accessed | tf_op | source)
XLA Modules:
  0.0 75.9 jit_solution(3716000088284678868)
XLA Ops:
  0.0 1.1 %copy-done.5 = bf16[12,12,4,512]{3,2,1,0:T(4,128)(2,1)S(1)} copy-done((bf16[12,12,4,512]{3,2,1,0:T(4,128)(2,1)S(1)}, bf16[12,12,4,512]{3,2,1,0:T(4,128)(2,1)}, u32[]{:S(2)}) %copy-start.5) | copy-done | bytes 589848
  1.1 0.2 split.1
  1.3 6.1 %collective-permute-start = (bf16[288,512]{1,0:T(8,128)(2,1)S(1)}, bf16[288,512]{1,0:T(8,128)(2,1)S(1)}, u32[]{:S(2)}, u32[]{:S(2)}) collective-permute-start(bf16[288,512]{1,0:T(8,128)(2,1)S(1)} %get-tuple-element.31), channel_id=1, source_target_pairs={{1,0},{2,1},{3,2},{4,3},{5,4},{6,5},{7,6},{8,7},{9,8},{10,9},{11,1... | collective-permute-start | bytes 884744 | tf_op jit(solution)/shard_map/ppermute | solution.py:341
  7.4 0.7 collective-permute-start.3
  8.1 0.8 %collective-permute-start.2 = (bf16[32,2048]{1,0:T(8,128)(2,1)}, bf16[32,2048]{1,0:T(8,128)(2,1)S(1)}, u32[]{:S(2)}, u32[]{:S(2)}) collective-permute-start(bf16[32,2048]{1,0:T(8,128)(2,1)} %bitcast.20), channel_id=1, source_target_pairs={{0,14},{1,15},{2,0},{3,1},{4,2},{5,3},{6,4},{7,5},{8,6},{9,7},{10,... | collective-permute-start | bytes 393224 | tf_op jit(solution)/shard_map/ppermute | solution.py:334
  8.9 1.2 %collective-permute-start.1 = (bf16[32,2048]{1,0:T(8,128)(2,1)}, bf16[32,2048]{1,0:T(8,128)(2,1)S(1)}, u32[]{:S(2)}, u32[]{:S(2)}) collective-permute-start(bf16[32,2048]{1,0:T(8,128)(2,1)} %bitcast.21), channel_id=1, source_target_pairs={{0,2},{1,3},{2,4},{3,5},{4,6},{5,7},{6,8},{7,9},{8,10},{9,11},{10,... | collective-permute-start | bytes 393224 | tf_op jit(solution)/shard_map/ppermute | solution.py:334
  10.1 1.7 %copy-done.3 = f32[16,144,144]{2,1,0:T(8,128)S(1)} copy-done((f32[16,144,144]{2,1,0:T(8,128)S(1)}, f32[16,144,144]{2,1,0:T(8,128)}, u32[]{:S(2)}) %copy-start.3) | copy-done | bytes 1327128
  11.8 2.4 %prepare.1 = (f32[4,144,576]{2,1,0:T(8,128)S(1)}, f32[2,4,144,288]{3,2,1,0:T(8,128)S(1)}) custom-call(f32[16,144,144]{2,1,0:T(8,128)S(1)} %copy-done.3), custom_call_target="tpu_custom_call" | custom-call | flops 1048576 | bytes 65536 | tf_op jit(solution)/shard_map/prepare/pallas_call | solution.py:343
  14.2 0.0 collective-permute-done.3.refs_1_
  14.2 2.1 %collective-permute-start.5 = (bf16[32,2048]{1,0:T(8,128)(2,1)S(1)}, bf16[32,2048]{1,0:T(8,128)(2,1)S(1)}, u32[]{:S(2)}, u32[]{:S(2)}) collective-permute-start(bf16[32,2048]{1,0:T(8,128)(2,1)S(1)} %collective-permute-done.3.refs_1_), channel_id=1, source_target_pairs={{0,14},{1,15},{2,0},{3,1},{4,2},{5,3},{6,4},{7,5},{8,6},{9,7},{10,... | collective-permute-start | bytes 393224 | tf_op jit(solution)/shard_map/ppermute | solution.py:334
  16.4 0.0 collective-permute-start.4
  16.4 0.0 collective-permute-done.right_ref
  16.4 0.0 collective-permute-done.2
  16.4 0.0 collective-permute-done.1
  16.4 2.9 %collective-permute-done.5 = bf16[32,2048]{1,0:T(8,128)(2,1)S(1)} collective-permute-done((bf16[32,2048]{1,0:T(8,128)(2,1)S(1)}, bf16[32,2048]{1,0:T(8,128)(2,1)S(1)}, u32[]{:S(2)}, u32[]{:S(2)}) %collective-permute-start.5) | collective-permute-done | bytes 131104 | tf_op jit(solution)/shard_map/ppermute | solution.py:334
  19.3 3.2 %collective-permute-done.4 = bf16[32,2048]{1,0:T(8,128)(2,1)S(1)} collective-permute-done((bf16[32,2048]{1,0:T(8,128)(2,1)S(1)}, bf16[32,2048]{1,0:T(8,128)(2,1)S(1)}, u32[]{:S(2)}, u32[]{:S(2)}) %collective-permute-start.4) | collective-permute-done | bytes 131104 | tf_op jit(solution)/shard_map/ppermute | solution.py:334
  22.6 0.1 collective-permute-start.8
  22.7 2.1 %collective-permute-start.7 = (bf16[64,2048]{1,0:T(8,128)(2,1)S(1)}, bf16[64,2048]{1,0:T(8,128)(2,1)S(1)}, u32[]{:S(2)}, u32[]{:S(2)}) collective-permute-start(bf16[64,2048]{1,0:T(8,128)(2,1)S(1)} %constant_dynamic-update-slice_fusion.refs_2_), channel_id=1, source_target_pairs={{0,2},{1,3},{2,4},{3,5},{4,6},{5,7},{6,8},{7,9},{8,10},{9,11},{10,... | collective-permute-start | bytes 786440 | tf_op jit(solution)/shard_map/ppermute | solution.py:334
  24.8 3.5 %collective-permute-start.6 = (bf16[2,72,512]{2,1,0:T(8,128)(2,1)S(1)}, bf16[2,72,512]{2,1,0:T(8,128)(2,1)S(1)}, u32[]{:S(2)}, u32[]{:S(2)}) collective-permute-start(bf16[2,72,512]{2,1,0:T(8,128)(2,1)S(1)} %pad_maximum_fusion.1), channel_id=1, source_target_pairs={{0,32},{32,64},{64,96},{96,128},{128,160},{160,192},{192,224},{1,3... | collective-permute-start | bytes 442376 | tf_op jit(solution)/shard_map/ppermute | solution.py:355
  28.3 0.0 copy-done.2
  28.3 0.0 copy-done.4
  28.3 0.0 copy-start
  28.3 0.0 copy-start.1
  28.3 0.0 copy-start.7
  28.3 3.8 %middle_attention.1 = (bf16[288,512]{1,0:T(8,128)(2,1)S(1)}, bf16[512,512]{1,0:T(8,128)(2,1)S(1)}) custom-call(bf16[288,512]{1,0:T(8,128)(2,1)S(1)} %get-tuple-element.30.left_ref, bf16[288,512]{1,0:T(8,128)(2,1)S(1)} %collective-permute-done.right_ref, f32[1,512]{1,0:T(1,128)S(1)} %bitcast.27, bf16[512,1536]{1,0:T(8,128)(2,1)S(1)} %copy-done.2, ...), custom_call_target="tpu_custom_call" | custom-call | flops 1048576 | bytes 65536 | tf_op jit(solution)/shard_map/middle_attention/pallas_call | solution.py:363
  32.1 1.2 %collective-permute-done.6.top_ref = bf16[2,72,512]{2,1,0:T(8,128)(2,1)S(1)} collective-permute-done((bf16[2,72,512]{2,1,0:T(8,128)(2,1)S(1)}, bf16[2,72,512]{2,1,0:T(8,128)(2,1)S(1)}, u32[]{:S(2)}, u32[]{:S(2)}) %collective-permute-start.6) | collective-permute-done | bytes 147488 | tf_op jit(solution)/shard_map/ppermute | solution.py:355
  33.3 0.0 collective-permute-done.8.refs_6_
  33.3 0.0 collective-permute-done.7.refs_3_
  33.4 0.0 collective-permute-start.10
  33.4 3.2 %collective-permute-start.11 = (bf16[64,2048]{1,0:T(8,128)(2,1)S(1)}, bf16[64,2048]{1,0:T(8,128)(2,1)S(1)}, u32[]{:S(2)}, u32[]{:S(2)}) collective-permute-start(bf16[64,2048]{1,0:T(8,128)(2,1)S(1)} %collective-permute-done.8.refs_6_), channel_id=1, source_target_pairs={{0,14},{1,15},{2,0},{3,1},{4,2},{5,3},{6,4},{7,5},{8,6},{9,7},{10,... | collective-permute-start | bytes 786440 | tf_op jit(solution)/shard_map/ppermute | solution.py:334
  36.6 3.4 %collective-permute-start.9 = (bf16[2,72,512]{2,1,0:T(8,128)(2,1)S(1)}, bf16[2,72,512]{2,1,0:T(8,128)(2,1)S(1)}, u32[]{:S(2)}, u32[]{:S(2)}) collective-permute-start(bf16[2,72,512]{2,1,0:T(8,128)(2,1)S(1)} %pad_maximum_fusion), channel_id=1, source_target_pairs={{32,0},{64,32},{96,64},{128,96},{160,128},{192,160},{224,192},{33,... | collective-permute-start | bytes 442376 | tf_op jit(solution)/shard_map/ppermute | solution.py:360
  40.1 2.0 %middle_mlp.1.blk1_ref = bf16[288,512]{1,0:T(8,128)(2,1)S(1)} custom-call(bf16[288,512]{1,0:T(8,128)(2,1)S(1)} %get-tuple-element.45.x_ref, f32[1,512]{1,0:T(1,128)S(1)} %bitcast.24, bf16[512,2048]{1,0:T(8,128)(2,1)S(1)} %copy-done, bf16[2048,512]{1,0:T(8,128)(2,1)S(1)} %copy-done.1), custom_call_target="tpu_custom_call" | custom-call | flops 1048576 | bytes 65536 | tf_op jit(solution)/shard_map/middle_mlp/pallas_call | solution.py:369
  42.1 3.9 %collective-permute-done.9.bottom_ref = bf16[2,72,512]{2,1,0:T(8,128)(2,1)S(1)} collective-permute-done((bf16[2,72,512]{2,1,0:T(8,128)(2,1)S(1)}, bf16[2,72,512]{2,1,0:T(8,128)(2,1)S(1)}, u32[]{:S(2)}, u32[]{:S(2)}) %collective-permute-start.9) | collective-permute-done | bytes 147488 | tf_op jit(solution)/shard_map/ppermute | solution.py:360
  46.0 5.1 %edge_attention.1.x_ref = bf16[288,512]{1,0:T(8,128)(2,1)S(1)} custom-call(bf16[72,512]{1,0:T(8,128)(2,1)S(1)} %get-tuple-element.62.lt_ref, bf16[72,512]{1,0:T(8,128)(2,1)S(1)} %get-tuple-element.61.rt_ref, bf16[72,512]{1,0:T(8,128)(2,1)S(1)} %get-tuple-element.56.lb_ref, bf16[72,512]{1,0:T(8,128)(2,1)S(1)} %get-tuple-element.59.rb_ref, ...), custom_call_target="tpu_custom_call" | custom-call | flops 1048576 | bytes 65536 | tf_op jit(solution)/shard_map/edge_attention/pallas_call | solution.py:370
  51.2 0.0 collective-permute-done.10.refs_4_
  51.2 0.0 collective-permute-done.11.refs_7_
  51.2 0.1 collective-permute-start.13
  51.3 2.0 %collective-permute-start.12 = (bf16[32,2048]{1,0:T(8,128)(2,1)S(1)}, bf16[32,2048]{1,0:T(8,128)(2,1)S(1)}, u32[]{:S(2)}, u32[]{:S(2)}) collective-permute-start(bf16[32,2048]{1,0:T(8,128)(2,1)S(1)} %slice.30), channel_id=1, source_target_pairs={{0,2},{1,3},{2,4},{3,5},{4,6},{5,7},{6,8},{7,9},{8,10},{9,11},{10,... | collective-permute-start | bytes 393224 | tf_op jit(solution)/shard_map/ppermute | solution.py:334
  53.3 0.0 copy-done.8
  53.3 3.1 %edge_mlp.1.joined_ref = bf16[4,160,512]{2,1,0:T(8,128)(2,1)S(1)} custom-call(bf16[288,512]{1,0:T(8,128)(2,1)S(1)} %edge_attention.1.x_ref, bf16[288,512]{1,0:T(8,128)(2,1)S(1)} %middle_mlp.1.blk1_ref, f32[1,512]{1,0:T(1,128)S(1)} %bitcast.25, bf16[512,2048]{1,0:T(8,128)(2,1)S(1)} %copy-done, bf16[2048,512]{1,0:T(8,128)(2,1)S(1)} %copy-done.1, ...), custom_call_target="tpu_custom_call" | custom-call | flops 1048576 | bytes 65536 | tf_op jit(solution)/shard_map/edge_mlp/pallas_call | solution.py:375
  56.5 0.0 collective-permute-done.13.refs_9_
  56.5 1.1 %collective-permute-done.12.refs_8_ = bf16[32,2048]{1,0:T(8,128)(2,1)S(1)} collective-permute-done((bf16[32,2048]{1,0:T(8,128)(2,1)S(1)}, bf16[32,2048]{1,0:T(8,128)(2,1)S(1)}, u32[]{:S(2)}, u32[]{:S(2)}) %collective-permute-start.12) | collective-permute-done | bytes 131104 | tf_op jit(solution)/shard_map/ppermute | solution.py:334
  57.6 0.0 collective-permute-start.14
  57.6 0.9 %merge_own.1.own_ref = f32[160,512]{1,0:T(8,128)S(1)} custom-call(bf16[4,160,512]{2,1,0:T(8,128)(2,1)S(1)} %edge_mlp.1.joined_ref, bf16[32,2048]{1,0:T(8,128)(2,1)S(1)} %bitcast.22, bf16[32,2048]{1,0:T(8,128)(2,1)S(1)} %collective-permute-done.3.refs_1_, bf16[64,2048]{1,0:T(8,128)(2,1)S(1)} %constant_dynamic-update-slice_fusion.refs_2_, ...), custom_call_target="tpu_custom_call" | custom-call | flops 1048576 | bytes 65536 | tf_op jit(solution)/shard_map/merge_own/pallas_call | solution.py:381
  58.4 1.2 %collective-permute-done.14.joined_ref = bf16[4,160,512]{2,1,0:T(8,128)(2,1)S(1)} collective-permute-done((bf16[4,160,512]{2,1,0:T(8,128)(2,1)S(1)}, bf16[4,160,512]{2,1,0:T(8,128)(2,1)S(1)}, u32[]{:S(2)}, u32[]{:S(2)}) %collective-permute-start.14) | collective-permute-done | bytes 655392 | tf_op jit(solution)/shard_map/ppermute | solution.py:379
  59.7 1.4 %merge.1 = bf16[16,72,128]{2,1,0:T(8,128)(2,1)S(1)} custom-call(bf16[4,160,512]{2,1,0:T(8,128)(2,1)S(1)} %collective-permute-done.14.joined_ref, f32[160,512]{1,0:T(8,128)S(1)} %merge_own.1.own_ref, bf16[32,2048]{1,0:T(8,128)(2,1)S(1)} %bitcast.23, bf16[32,2048]{1,0:T(8,128)(2,1)S(1)} %collective-permute-done.3.refs_1_, ...), custom_call_target="tpu_custom_call" | custom-call | flops 1048576 | bytes 65536 | tf_op jit(solution)/shard_map/merge/pallas_call | solution.py:382
  61.1 13.8 %all_to_all.5.in_ref = bf16[16,72,128]{2,1,0:T(8,128)(2,1)S(1)} all-to-all(bf16[16,72,128]{2,1,0:T(8,128)(2,1)S(1)} %merge.1), channel_id=1, replica_groups={{0,2,4,6,8,10,12,14,16,18,20,22,24,26,28,30},{1,3,5,7,9,11,13,15,17,19,..., dimensions={0} | all-to-all | bytes 589824 | tf_op jit(solution)/shard_map/all_to_all | solution.py:390
  74.9 1.0 %unpack.1 = bf16[6,128,192]{2,1,0:T(8,128)(2,1)} custom-call(bf16[16,72,128]{2,1,0:T(8,128)(2,1)S(1)} %all_to_all.5.in_ref), custom_call_target="tpu_custom_call" | custom-call | flops 1048576 | bytes 65536 | tf_op jit(solution)/shard_map/unpack/pallas_call | solution.py:391
  (23 shorter events, 0.2 us)
Async XLA Ops:
  0.0 1.1 %copy-start.5 = (bf16[12,12,4,512]{3,2,1,0:T(4,128)(2,1)S(1)}, bf16[12,12,4,512]{3,2,1,0:T(4,128)(2,1)}, u32[]{:S(2)}) copy-start(bf16[12,12,4,512]{3,2,1,0:T(4,128)(2,1)} %tokens_hbm.1) | copy-start | bytes 1769476
  1.3 15.1 %collective-permute-start = (bf16[288,512]{1,0:T(8,128)(2,1)S(1)}, bf16[288,512]{1,0:T(8,128)(2,1)S(1)}, u32[]{:S(2)}, u32[]{:S(2)}) collective-permute-start(bf16[288,512]{1,0:T(8,128)(2,1)S(1)} %get-tuple-element.31), channel_id=1, source_target_pairs={{1,0},{2,1},{3,2},{4,3},{5,4},{6,5},{7,6},{8,7},{9,8},{10,9},{11,1... | collective-permute-start | bytes 884744 | tf_op jit(solution)/shard_map/ppermute | solution.py:341
  7.4 20.9 %copy-start.2 = (bf16[512,1536]{1,0:T(8,128)(2,1)S(1)}, bf16[512,1536]{1,0:T(8,128)(2,1)}, u32[]{:S(2)}) copy-start(bf16[512,1536]{1,0:T(8,128)(2,1)} %wqkv_ref.3) | copy-start | bytes 4718596
  7.4 6.9 %collective-permute-start.3 = (bf16[32,2048]{1,0:T(8,128)(2,1)}, bf16[32,2048]{1,0:T(8,128)(2,1)S(1)}, u32[]{:S(2)}, u32[]{:S(2)}) collective-permute-start(bf16[32,2048]{1,0:T(8,128)(2,1)} %bitcast.19), channel_id=1, source_target_pairs={{0,16},{1,17},{2,18},{3,19},{4,20},{5,21},{6,22},{7,23},{8,24},{9,... | collective-permute-start | bytes 393224 | tf_op jit(solution)/shard_map/ppermute | solution.py:337
  8.1 8.3 %collective-permute-start.2 = (bf16[32,2048]{1,0:T(8,128)(2,1)}, bf16[32,2048]{1,0:T(8,128)(2,1)S(1)}, u32[]{:S(2)}, u32[]{:S(2)}) collective-permute-start(bf16[32,2048]{1,0:T(8,128)(2,1)} %bitcast.20), channel_id=1, source_target_pairs={{0,14},{1,15},{2,0},{3,1},{4,2},{5,3},{6,4},{7,5},{8,6},{9,7},{10,... | collective-permute-start | bytes 393224 | tf_op jit(solution)/shard_map/ppermute | solution.py:334
  8.9 7.5 %collective-permute-start.1 = (bf16[32,2048]{1,0:T(8,128)(2,1)}, bf16[32,2048]{1,0:T(8,128)(2,1)S(1)}, u32[]{:S(2)}, u32[]{:S(2)}) collective-permute-start(bf16[32,2048]{1,0:T(8,128)(2,1)} %bitcast.21), channel_id=1, source_target_pairs={{0,2},{1,3},{2,4},{3,5},{4,6},{5,7},{6,8},{7,9},{8,10},{9,11},{10,... | collective-permute-start | bytes 393224 | tf_op jit(solution)/shard_map/ppermute | solution.py:334
  10.1 1.7 %copy-start.3 = (f32[16,144,144]{2,1,0:T(8,128)S(1)}, f32[16,144,144]{2,1,0:T(8,128)}, u32[]{:S(2)}) copy-start(f32[16,144,144]{2,1,0:T(8,128)} %bias_ref.1) | copy-start | bytes 3981316
  11.8 16.5 %copy-start.4 = (bf16[512,512]{1,0:T(8,128)(2,1)S(1)}, bf16[512,512]{1,0:T(8,128)(2,1)}, u32[]{:S(2)}) copy-start(bf16[512,512]{1,0:T(8,128)(2,1)} %wout_ref.3) | copy-start | bytes 1572868
  11.8 16.5 %copy-start.9 = (f32[512]{0:T(512)S(1)}, f32[512]{0:T(512)}, u32[]{:S(2)}) copy-start(f32[512]{0:T(512)} %param.11) | copy-start | bytes 6148
  14.2 5.0 %collective-permute-start.5 = (bf16[32,2048]{1,0:T(8,128)(2,1)S(1)}, bf16[32,2048]{1,0:T(8,128)(2,1)S(1)}, u32[]{:S(2)}, u32[]{:S(2)}) collective-permute-start(bf16[32,2048]{1,0:T(8,128)(2,1)S(1)} %collective-permute-done.3.refs_1_), channel_id=1, source_target_pairs={{0,14},{1,15},{2,0},{3,1},{4,2},{5,3},{6,4},{7,5},{8,6},{9,7},{10,... | collective-permute-start | bytes 393224 | tf_op jit(solution)/shard_map/ppermute | solution.py:334
  16.4 6.2 %collective-permute-start.4 = (bf16[32,2048]{1,0:T(8,128)(2,1)S(1)}, bf16[32,2048]{1,0:T(8,128)(2,1)S(1)}, u32[]{:S(2)}, u32[]{:S(2)}) collective-permute-start(bf16[32,2048]{1,0:T(8,128)(2,1)S(1)} %collective-permute-done.3.refs_1_), channel_id=1, source_target_pairs={{0,2},{1,3},{2,4},{3,5},{4,6},{5,7},{6,8},{7,9},{8,10},{9,11},{10,... | collective-permute-start | bytes 393224 | tf_op jit(solution)/shard_map/ppermute | solution.py:334
  22.6 10.8 %collective-permute-start.8 = (bf16[64,2048]{1,0:T(8,128)(2,1)S(1)}, bf16[64,2048]{1,0:T(8,128)(2,1)S(1)}, u32[]{:S(2)}, u32[]{:S(2)}) collective-permute-start(bf16[64,2048]{1,0:T(8,128)(2,1)S(1)} %constant_dynamic-update-slice_fusion.2.refs_5_), channel_id=1, source_target_pairs={{0,14},{1,15},{2,0},{3,1},{4,2},{5,3},{6,4},{7,5},{8,6},{9,7},{10,... | collective-permute-start | bytes 786440 | tf_op jit(solution)/shard_map/ppermute | solution.py:334
  22.7 10.6 %collective-permute-start.7 = (bf16[64,2048]{1,0:T(8,128)(2,1)S(1)}, bf16[64,2048]{1,0:T(8,128)(2,1)S(1)}, u32[]{:S(2)}, u32[]{:S(2)}) collective-permute-start(bf16[64,2048]{1,0:T(8,128)(2,1)S(1)} %constant_dynamic-update-slice_fusion.refs_2_), channel_id=1, source_target_pairs={{0,2},{1,3},{2,4},{3,5},{4,6},{5,7},{6,8},{7,9},{8,10},{9,11},{10,... | collective-permute-start | bytes 786440 | tf_op jit(solution)/shard_map/ppermute | solution.py:334
  24.8 8.5 %collective-permute-start.6 = (bf16[2,72,512]{2,1,0:T(8,128)(2,1)S(1)}, bf16[2,72,512]{2,1,0:T(8,128)(2,1)S(1)}, u32[]{:S(2)}, u32[]{:S(2)}) collective-permute-start(bf16[2,72,512]{2,1,0:T(8,128)(2,1)S(1)} %pad_maximum_fusion.1), channel_id=1, source_target_pairs={{0,32},{32,64},{64,96},{96,128},{128,160},{160,192},{192,224},{1,3... | collective-permute-start | bytes 442376 | tf_op jit(solution)/shard_map/ppermute | solution.py:355
  28.3 11.7 %copy-start = (bf16[512,2048]{1,0:T(8,128)(2,1)S(1)}, bf16[512,2048]{1,0:T(8,128)(2,1)}, u32[]{:S(2)}) copy-start(bf16[512,2048]{1,0:T(8,128)(2,1)} %up_ref.3) | copy-start | bytes 6291460
  28.3 11.7 %copy-start.1 = (bf16[2048,512]{1,0:T(8,128)(2,1)S(1)}, bf16[2048,512]{1,0:T(8,128)(2,1)}, u32[]{:S(2)}) copy-start(bf16[2048,512]{1,0:T(8,128)(2,1)} %down_ref.3) | copy-start | bytes 6291460
  28.3 11.7 %copy-start.7 = (f32[512]{0:T(512)S(1)}, f32[512]{0:T(512)}, u32[]{:S(2)}) copy-start(f32[512]{0:T(512)} %param.15) | copy-start | bytes 6148
  33.4 17.8 %collective-permute-start.10 = (bf16[64,2048]{1,0:T(8,128)(2,1)S(1)}, bf16[64,2048]{1,0:T(8,128)(2,1)S(1)}, u32[]{:S(2)}, u32[]{:S(2)}) collective-permute-start(bf16[64,2048]{1,0:T(8,128)(2,1)S(1)} %collective-permute-done.7.refs_3_), channel_id=1, source_target_pairs={{0,2},{1,3},{2,4},{3,5},{4,6},{5,7},{6,8},{7,9},{8,10},{9,11},{10,... | collective-permute-start | bytes 786440 | tf_op jit(solution)/shard_map/ppermute | solution.py:334
  33.4 17.8 %collective-permute-start.11 = (bf16[64,2048]{1,0:T(8,128)(2,1)S(1)}, bf16[64,2048]{1,0:T(8,128)(2,1)S(1)}, u32[]{:S(2)}, u32[]{:S(2)}) collective-permute-start(bf16[64,2048]{1,0:T(8,128)(2,1)S(1)} %collective-permute-done.8.refs_6_), channel_id=1, source_target_pairs={{0,14},{1,15},{2,0},{3,1},{4,2},{5,3},{6,4},{7,5},{8,6},{9,7},{10,... | collective-permute-start | bytes 786440 | tf_op jit(solution)/shard_map/ppermute | solution.py:334
  36.6 9.4 %collective-permute-start.9 = (bf16[2,72,512]{2,1,0:T(8,128)(2,1)S(1)}, bf16[2,72,512]{2,1,0:T(8,128)(2,1)S(1)}, u32[]{:S(2)}, u32[]{:S(2)}) collective-permute-start(bf16[2,72,512]{2,1,0:T(8,128)(2,1)S(1)} %pad_maximum_fusion), channel_id=1, source_target_pairs={{32,0},{64,32},{96,64},{128,96},{160,128},{192,160},{224,192},{33,... | collective-permute-start | bytes 442376 | tf_op jit(solution)/shard_map/ppermute | solution.py:360
  46.0 7.3 %copy-start.8 = (f32[2048]{0:T(1024)S(1)}, f32[2048]{0:T(1024)}, u32[]{:S(2)}) copy-start(f32[2048]{0:T(1024)} %param.18) | copy-start | bytes 24580
  51.2 5.3 %collective-permute-start.13 = (bf16[32,2048]{1,0:T(8,128)(2,1)S(1)}, bf16[32,2048]{1,0:T(8,128)(2,1)S(1)}, u32[]{:S(2)}, u32[]{:S(2)}) collective-permute-start(bf16[32,2048]{1,0:T(8,128)(2,1)S(1)} %slice.31), channel_id=1, source_target_pairs={{0,14},{1,15},{2,0},{3,1},{4,2},{5,3},{6,4},{7,5},{8,6},{9,7},{10,... | collective-permute-start | bytes 393224 | tf_op jit(solution)/shard_map/ppermute | solution.py:334
  51.3 6.3 %collective-permute-start.12 = (bf16[32,2048]{1,0:T(8,128)(2,1)S(1)}, bf16[32,2048]{1,0:T(8,128)(2,1)S(1)}, u32[]{:S(2)}, u32[]{:S(2)}) collective-permute-start(bf16[32,2048]{1,0:T(8,128)(2,1)S(1)} %slice.30), channel_id=1, source_target_pairs={{0,2},{1,3},{2,4},{3,5},{4,6},{5,7},{6,8},{7,9},{8,10},{9,11},{10,... | collective-permute-start | bytes 393224 | tf_op jit(solution)/shard_map/ppermute | solution.py:334
  53.3 4.2 %copy-start.6 = (bf16[2048,32]{0,1:T(8,128)(2,1)S(1)}, bf16[2048,32]{0,1:T(8,128)(2,1)}, u32[]{:S(2)}) copy-start(bf16[2048,32]{0,1:T(8,128)(2,1)} %param.19) | copy-start | bytes 393220
  57.6 2.1 %collective-permute-start.14 = (bf16[4,160,512]{2,1,0:T(8,128)(2,1)S(1)}, bf16[4,160,512]{2,1,0:T(8,128)(2,1)S(1)}, u32[]{:S(2)}, u32[]{:S(2)}) collective-permute-start(bf16[4,160,512]{2,1,0:T(8,128)(2,1)S(1)} %edge_mlp.1.joined_ref), channel_id=1, source_target_pairs={{0,1},{1,0},{2,3},{3,2},{4,5},{5,4},{6,7},{7,6},{8,9},{9,8},{10,11... | collective-permute-start | bytes 1966088 | tf_op jit(solution)/shard_map/ppermute | solution.py:379

commit v3 on v2

--- a/solution.py
+++ b/solution.py
@@ -109,46 +109,29 @@
         out[...] = held[...].astype(F32).reshape(BAND, WIDTH).astype(BF)
 
 
-def prepare_kernel(bias_ref, middle_out, edges_out):
+def prepare_kernel(bias_ref, out_ref):
     perm = bias_permutation()
     for h in range(HEADS):
-        b = bias_ref[h] * LOG2E
-        y = sum(dot(perm, part, NT) for part in split3(b))
-        t = sum(dot(part, perm, NT) for part in split3(y))
-        tile, n = h // 4, h % 4
-        middle_out[tile, :, n * WIN : (n + 1) * WIN] = t
-        for half in range(2):
-            edges_out[half, tile, :, n * HALF_WIN : (n + 1) * HALF_WIN] = t[:, half * HALF_WIN : (half + 1) * HALF_WIN]
-
-
-def attend_window(normed, q, k, bias, kaug, qaug, wvt):
+        parts = split3(bias_ref[h] * LOG2E)
+        out_ref[h] = sum(dot(dot(perm, part).astype(BF), perm, NT) for part in parts)
+
+
+def attend_window(q, k, v, bias, kaug, qaug):
     count = q.shape[0]
-    k = k.astype(BF)
-    vt = dot(wvt, normed, NT).astype(BF)
-    lane = lax.broadcasted_iota(jnp.int32, (count, 128), 1) // HEAD_DIM
-    scores = []
+    k, v = k.astype(BF), v.astype(BF)
+    lane_head = lax.broadcasted_iota(jnp.int32, (count, 128), 1) // HEAD_DIM
+    ones = jnp.ones((WIN, 128), BF)
+    mixed = []
     for tile in range(4):
         lanes = slice(tile * 128, tile * 128 + 128)
         part = q[:, lanes]
-        qm = jnp.concatenate([jnp.where(lane == n, part, 0.0) for n in range(4)], axis=0).astype(BF)
-        kx = jnp.concatenate([k[:, lanes], kaug], axis=1)
-        qx = jnp.concatenate([qm, qaug], axis=1)
-        scores.append(dot(kx, qx, NT) + bias(tile))
-    row_head = lax.broadcasted_iota(jnp.int32, (128, 4 * count), 0) // HEAD_DIM
-    column = lax.broadcasted_iota(jnp.int32, (128, 4 * count), 1)
-    column_head = sum((column >= n * count).astype(jnp.int32) for n in range(1, 4))
-    own = row_head == column_head
-    pick_row = lax.broadcasted_iota(jnp.int32, (count, 4 * count), 0)
-    pick_column = lax.broadcasted_iota(jnp.int32, (count, 4 * count), 1)
-    pick = sum((pick_column == pick_row + n * count).astype(F32) for n in range(4)).astype(BF)
-    mixed = []
-    for tile in range(4):
-        s = scores[tile]
-        p = jnp.exp2(s - jnp.max(s, axis=0, keepdims=True))
-        inverse = 1.0 / jnp.sum(p, axis=0, keepdims=True)
-        o = dot(vt[tile * 128 : tile * 128 + 128], p.astype(BF))
-        mixed.append(dot(pick, jnp.where(own, o * inverse, 0.0).astype(BF), NT))
-    return jnp.concatenate(mixed, axis=1)
+        qm = jnp.concatenate([jnp.where(lane_head == n, part, 0.0) for n in range(4)], axis=0).astype(BF)
+        s = dot(jnp.concatenate([qm, qaug], axis=1), jnp.concatenate([k[:, lanes], kaug], axis=1), NT) + bias(tile)
+        p = jnp.exp2(s - jnp.max(s, axis=1, keepdims=True)).astype(BF)
+        o = dot(p, jnp.concatenate([v[:, lanes], ones], axis=1))
+        o = o[:, :128] * (1.0 / o[:, 128:])
+        mixed.append(sum(jnp.where(lane_head == n, o[n * count : (n + 1) * count], 0.0) for n in range(4)))
+    return jnp.concatenate(mixed, axis=1).astype(BF)
 
 
 def feed_forward(attended, norm_mlp, up_ref, down_ref):
@@ -168,29 +151,26 @@
     return (row % HALF_WIN) // 36, row // HALF_WIN, lane
 
 
-def query_key(x, gain, wqkv_ref):
-    normed = normalise(x, gain).astype(BF)
-    qk = dot(normed, wqkv_ref[:, : 2 * WIDTH])
-    return normed, qk[:, :WIDTH] * (LOG2E * HEAD_DIM**-0.5), qk[:, WIDTH:]
-
-
-def middle_attention_kernel(left_ref, right_ref, ga_ref, wqkv_ref, bias_ref, wout_ref, out_ref, wvt_ref):
+def middle_attention_kernel(left_ref, right_ref, ga_ref, wqkv_ref, bias_ref, wout_ref, out_ref):
     half, ihalf, place = band_places()
     place = 72 + 72 * ihalf + place
     x = dot(one_hot(jnp.where(half == 0, place, -1), BAND), left_ref[...])
     x = x + dot(one_hot(jnp.where(half == 1, place, -1), BAND), right_ref[...])
-    normed, q, k = query_key(x, ga_ref[...], wqkv_ref)
+    qkv = dot(normalise(x, ga_ref[...]).astype(BF), wqkv_ref[...])
+    q = qkv[:, :WIDTH] * (LOG2E * HEAD_DIM**-0.5)
     group, _, lane = group_lanes(WIN)
     qgroup, _, qlane = group_lanes(4 * WIN)
     qaug = jnp.where(qlane == qgroup, 1.0, 0.0).astype(BF)
-    wvt = dot(one_hot(row_numbers(WIDTH), WIDTH), wqkv_ref[:, 2 * WIDTH :], NT).astype(BF)
-    wvt_ref[...] = wvt
+
+    def bias(tile):
+        return jnp.concatenate([bias_ref[4 * tile + n] for n in range(4)], axis=0)
+
     pieces = []
     for t in range(2):
         rows = slice(t * WIN, (t + 1) * WIN)
         kaug = jnp.where((lane < 2) & (lane != group), BIG if t else 0.0, 0.0).astype(BF)
-        pieces.append(attend_window(normed[rows], q[rows], k[rows], lambda n: bias_ref[n], kaug, qaug, wvt))
-    update = dot(jnp.concatenate(pieces, axis=0).astype(BF), wout_ref[...])
+        pieces.append(attend_window(q[rows], qkv[rows, WIDTH : 2 * WIDTH], qkv[rows, 2 * WIDTH :], bias, kaug, qaug))
+    update = dot(jnp.concatenate(pieces, axis=0), wout_ref[...])
     out_ref[...] = (x + update).astype(BF)
 
 
@@ -199,7 +179,7 @@
 
 
 def edge_attention_kernel(
-    lt_ref, rt_ref, lb_ref, rb_ref, top_ref, bottom_ref, ga_ref, wqkv_ref, wvt_ref, bias_ref, wout_ref, out_ref
+    lt_ref, rt_ref, lb_ref, rb_ref, top_ref, bottom_ref, ga_ref, wqkv_ref, bias_ref, wout_ref, out_ref
 ):
     bands = (
         (top_ref[0], lt_ref[...], top_ref[1], rt_ref[...]),
@@ -208,29 +188,32 @@
     half, ihalf, place = band_places()
     perm = [one_hot(jnp.where(2 * half + ihalf == n, place, -1), HALF_WIN) for n in range(4)]
     x = jnp.concatenate([sum(dot(perm[n], piece) for n, piece in enumerate(band)) for band in bands], axis=0)
-    normed, q, k = query_key(x, ga_ref[...], wqkv_ref)
+    normed = normalise(x, ga_ref[...])
+    kv = dot(normed.astype(BF), wqkv_ref[:, WIDTH:])
     group, half, lane = group_lanes(WIN)
     qgroup, _, qlane = group_lanes(4 * HALF_WIN)
     qaug = jnp.where(qlane == qgroup, 1.0, 0.0).astype(BF)
     lat = lax.axis_index("lat")
-    wvt = wvt_ref[...]
+    starts = [(n * 2 + t) * WIN + (1 - n) * HALF_WIN for n in range(2) for t in range(2)]
+    asked = jnp.concatenate([normed[start : start + HALF_WIN] for start in starts], axis=0).astype(BF)
+    q = dot(asked, wqkv_ref[:, :WIDTH]) * (LOG2E * HEAD_DIM**-0.5)
     pieces = []
-    kept = []
-    for n in range(2):
-        outside = half == n
+    for w, start in enumerate(starts):
+        n, t = w // 2, w % 2
         off = jnp.where(lat == (lax.axis_size("lat") - 1 if n else 0), BIG, 0.0)
-        for t in range(2):
-            first = (n * 2 + t) * WIN
-            rows = slice(first, first + WIN)
-            queries = slice(first, first + HALF_WIN) if n else slice(first + HALF_WIN, first + WIN)
-            other = jnp.where(lane != group, BIG if t else 0.0, 0.0)
-            kaug = jnp.where(lane < 2, jnp.where(outside, jnp.minimum(off, other), other), 0.0).astype(BF)
-            pieces.append(
-                attend_window(normed[rows], q[queries], k[rows], lambda m: bias_ref[1 - n, m], kaug, qaug, wvt)
-            )
-            kept.append(x[queries])
+        other = jnp.where(lane != group, BIG if t else 0.0, 0.0)
+        kaug = jnp.where(lane < 2, jnp.where(half == n, jnp.minimum(off, other), other), 0.0).astype(BF)
+        rows = slice(w * WIN, (w + 1) * WIN)
+
+        def bias(tile):
+            asked_rows = slice((1 - n) * HALF_WIN, (2 - n) * HALF_WIN)
+            return jnp.concatenate([bias_ref[4 * tile + m, asked_rows, :] for m in range(4)], axis=0)
+
+        mixed = attend_window(q[w * HALF_WIN : (w + 1) * HALF_WIN], kv[rows, :WIDTH], kv[rows, WIDTH:], bias, kaug, qaug)
+        pieces.append(mixed.astype(F32))
     update = dot(jnp.concatenate(pieces, axis=0).astype(BF), wout_ref[...])
-    out_ref[...] = (jnp.concatenate(kept, axis=0) + update).astype(BF)
+    kept = jnp.concatenate([x[start : start + HALF_WIN] for start in starts], axis=0)
+    out_ref[...] = (kept + update).astype(BF)
 
 
 def edge_mlp_kernel(x_ref, blk1_ref, gm_ref, up_ref, down_ref, gg_ref, out_ref):
@@ -340,42 +323,35 @@
     )(tokens)
     right = lax.ppermute(right_own, "lon", [((i + 1) % lon_count, i) for i in range(lon_count)])
     own_up, own_down = around(w_own, 1), around(w_own, -1)
-    bias_middle, bias_edges = call(
-        prepare_kernel,
-        (shape((4, WIN, 4 * WIN), F32), shape((2, 4, WIN, 4 * HALF_WIN), F32)),
-        [VMEM],
-        [],
-        "prepare",
-    )(pos_bias)
-    bias_middle, w_pair = barrier((bias_middle, w_pair))
+    w_pair, pos_bias = barrier((w_pair, pos_bias))
     pair_up, pair_down = around(w_pair, 1), around(w_pair, -1)
-
+    bias = call(prepare_kernel, shape((HEADS, WIN, WIN), F32), [VMEM], [], "prepare")(pos_bias)
+
+    bias, right, own_up, own_down, pair_up, pair_down = barrier((bias, right, own_up, own_down, pair_up, pair_down))
+    up, down = [jnp.concatenate([own_up, pair_up], axis=0)], [jnp.concatenate([own_down, pair_down], axis=0)]
+    up.append(around(up[-1], 1))
+    down.append(around(down[-1], -1))
     top_rows = jnp.stack([left[:HALF_WIN], right[:HALF_WIN]])
     bottom_rows = jnp.stack([left[-HALF_WIN:], right[-HALF_WIN:]])
     from_above = lax.ppermute(bottom_rows, "lat", [(i, i + 1) for i in range(lat_count - 1)])
-    top_rows, own_up, own_down, pair_up, pair_down = barrier((top_rows, own_up, own_down, pair_up, pair_down))
-    up, down = [jnp.concatenate([own_up, pair_up], axis=0)], [jnp.concatenate([own_down, pair_down], axis=0)]
-    up.append(around(up[-1], 1))
-    down.append(around(down[-1], -1))
     from_below = lax.ppermute(top_rows, "lat", [(i + 1, i) for i in range(lat_count - 1)])
-
     ga, gm = norm_attn.reshape(1, WIDTH), norm_mlp.reshape(1, WIDTH)
-    attended1, wvt = call(
-        middle_attention_kernel, (shape((BAND, WIDTH)), shape((WIDTH, WIDTH))), [VMEM] * 6, [], "middle_attention"
-    )(left, right, ga, w_qkv, bias_middle, w_out)
-    attended1, wvt, from_above, u, d = barrier((attended1, wvt, from_above, up[-1], down[-1]))
+    attended1 = call(middle_attention_kernel, shape((BAND, WIDTH)), [VMEM] * 6, [], "middle_attention")(
+        left, right, ga, w_qkv, bias, w_out
+    )
+    block1 = call(middle_mlp_kernel, shape((BAND, WIDTH)), [VMEM] * 4, [], "middle_mlp")(attended1, gm, w_up, w_down)
+
+    block1, from_above, from_below, u, d = barrier((block1, from_above, from_below, up[-1], down[-1]))
     up.append(around(u, 1))
     down.append(around(d, -1))
-    block1 = call(middle_mlp_kernel, shape((BAND, WIDTH)), [VMEM] * 4, [], "middle_mlp")(attended1, gm, w_up, w_down)
-    attended2 = call(edge_attention_kernel, shape((BAND, WIDTH)), [VMEM] * 11, [], "edge_attention")(
-        top_rows[0], top_rows[1], bottom_rows[0], bottom_rows[1], from_above, from_below, ga, w_qkv, wvt, bias_edges, w_out
-    )
-    attended2, block1, u, d = barrier((attended2, block1, up[-1], down[-1]))
-    far_up, far_down = around(u[:32], 1), around(d[32:], -1)
+    far_up, far_down = around(u[:32], 2), around(d[32:], -2)
+    attended2 = call(edge_attention_kernel, shape((BAND, WIDTH)), [VMEM] * 10, [], "edge_attention")(
+        top_rows[0], top_rows[1], bottom_rows[0], bottom_rows[1], from_above, from_below, ga, w_qkv, bias, w_out
+    )
     joined = call(edge_mlp_kernel, shape((4, 4 * MERGE_PAD, WIDTH)), [VMEM] * 6, [], "edge_mlp")(
         attended2, block1, gm, w_up, w_down, norm_merge.reshape(4, 1, WIDTH)
     )
-    joined, far_up, far_down = barrier((joined, far_up, far_down))
+    joined, far_up, far_down, up[-1], down[-1] = barrier((joined, far_up, far_down, up[-1], down[-1]))
     neighbour = lax.ppermute(joined, "lon", [(i, i ^ 1) for i in range(lon_count)])
     w_cols = [w_own, w_pair] + up + down + [far_up, far_down]
     own = call(merge_own_kernel, shape((4 * MERGE_PAD, WIDTH), F32), [VMEM] * 11, [], "merge_own")(joined, *w_cols)

time: 76.4 us -> 69.5 us (0.910)
  waiting for transfers between devices: 13.5 us -> 4.23 us
  Pallas kernels: 20 us -> 17.6 us
  starting transfers between devices: 25.4 us -> 27.7 us
  blocking collectives: 13.8 us -> 16 us
    ppermute x10, waiting for transfers between devices: 7.2 us -> 2.98 us  [around(): return lax.ppermute(block, 'lon', route)]
    ppermute x1, waiting for transfers between devices: 3.91 us -> 0.01 us  [on_device(): lax.ppermute(top_rows, 'lat', [(i + 1, i) for i in range(lat_count - 1)])]
    pallas_call x3, Pallas kernels: 11.3 us -> 8.95 us  [the longest x1 3.62 us: on_device(): call(edge_attention_kernel, shape((BAND, WIDTH)), [VMEM] * 10, [], 'edge_...]
    all_to_all x1, blocking collectives: 13.8 us -> 16 us  [on_device(): lax.all_to_all(messages, 'lon', 0, 0, tiled=True, axis_index_groups=cores)]
    ppermute x10, starting transfers between devices: 11.7 us -> 13.6 us  [around(): return lax.ppermute(block, 'lon', route)]
    ppermute x1, waiting for transfers between devices: 1.2 us -> 0.01 us  [on_device(): lax.ppermute(bottom_rows, 'lat', [(i, i + 1) for i in range(lat_count - 1)])]
    ppermute x1, starting transfers between devices: 3.42 us -> 4.35 us  [on_device(): lax.ppermute(top_rows, 'lat', [(i + 1, i) for i in range(lat_count - 1)])]
    ppermute x1, starting transfers between devices: 6.09 us -> 5.27 us  [on_device(): lax.ppermute(right_own, 'lon', [((i + 1) % lon_count, i) for i in range(l...]
  transfers between devices with their start and end apart: 15 -> 15, of which waited for: 6 -> 5; matrix products, arithmetic and copies ran while one was open for 0% -> 0% of each run, Pallas kernels for 23% -> 22%
where the time goes in v3:
time: 69.5 us; the launch traced here: 68.7 us
  starting transfers between devices  27.7 us (40%)
  Pallas kernels  17.6 us (25%)
  blocking collectives  16 us (23%)
  waiting for transfers between devices  4.23 us (6%)
  local copies, waits for them, and re-layouts  2.87 us (4%)
    all_to_all x1, blocking collectives, on_device(): lax.all_to_all(messages, 'lon', 0, 0, tiled=True, axis_index_groups=cores)  16 us
    ppermute x10, starting transfers between devices, around(): return lax.ppermute(block, 'lon', route)  13.6 us
    ppermute x1, starting transfers between devices, on_device(): lax.ppermute(right_own, 'lon', [((i + 1) % lon_count, i) for i in range(l...  5.27 us
    ppermute x1, starting transfers between devices, on_device(): lax.ppermute(top_rows, 'lat', [(i + 1, i) for i in range(lat_count - 1)])  4.35 us
    pallas_call x1, Pallas kernels, on_device(): call(edge_attention_kernel, shape((BAND, WIDTH)), [VMEM] * 10, [], 'edge_...  3.62 us
    ppermute x1, starting transfers between devices, on_device(): lax.ppermute(bottom_rows, 'lat', [(i, i + 1) for i in range(lat_count - 1)])  3.17 us
    pallas_call x1, Pallas kernels, on_device(): call(edge_mlp_kernel, shape((4, 4 * MERGE_PAD, WIDTH)), [VMEM] * 6, [], '...  3.15 us
    pallas_call x1, Pallas kernels, on_device(): call(middle_attention_kernel, shape((BAND, WIDTH)), [VMEM] * 6, [], 'midd...  3.06 us
  transfers between devices with their start and end apart: 15, of which 5 were waited for; matrix products, arithmetic and copies ran while one was open for 0% of the time, Pallas kernels for 22%

profile of v3, /device:TPU:18, one launch (start us, length us, event | category | flops | bytes accessed | tf_op | source)
XLA Modules:
  0.0 68.7 jit_solution(2371177465391708565)
XLA Ops:
  0.0 1.3 %collective-permute-start = (bf16[32,2048]{1,0:T(8,128)(2,1)}, bf16[32,2048]{1,0:T(8,128)(2,1)S(1)}, u32[]{:S(2)}, u32[]{:S(2)}) collective-permute-start(bf16[32,2048]{1,0:T(8,128)(2,1)} %bitcast.15), channel_id=1, source_target_pairs={{0,16},{1,17},{2,18},{3,19},{4,20},{5,21},{6,22},{7,23},{8,24},{9,... | collective-permute-start | bytes 393224 | tf_op jit(solution)/shard_map/ppermute | solution.py:320
  1.3 1.1 %copy-done.5 = bf16[12,12,4,512]{3,2,1,0:T(4,128)(2,1)S(1)} copy-done((bf16[12,12,4,512]{3,2,1,0:T(4,128)(2,1)S(1)}, bf16[12,12,4,512]{3,2,1,0:T(4,128)(2,1)}, u32[]{:S(2)}) %copy-start.5) | copy-done | bytes 589848
  2.3 0.2 split.1
  2.6 5.3 %collective-permute-start.1 = (bf16[288,512]{1,0:T(8,128)(2,1)S(1)}, bf16[288,512]{1,0:T(8,128)(2,1)S(1)}, u32[]{:S(2)}, u32[]{:S(2)}) collective-permute-start(bf16[288,512]{1,0:T(8,128)(2,1)S(1)} %get-tuple-element.27), channel_id=1, source_target_pairs={{1,0},{2,1},{3,2},{4,3},{5,4},{6,5},{7,6},{8,7},{9,8},{10,9},{11,1... | collective-permute-start | bytes 884744 | tf_op jit(solution)/shard_map/ppermute | solution.py:324
  7.8 0.8 %collective-permute-start.3 = (bf16[32,2048]{1,0:T(8,128)(2,1)}, bf16[32,2048]{1,0:T(8,128)(2,1)S(1)}, u32[]{:S(2)}, u32[]{:S(2)}) collective-permute-start(bf16[32,2048]{1,0:T(8,128)(2,1)} %bitcast.16), channel_id=1, source_target_pairs={{0,14},{1,15},{2,0},{3,1},{4,2},{5,3},{6,4},{7,5},{8,6},{9,7},{10,... | collective-permute-start | bytes 393224 | tf_op jit(solution)/shard_map/ppermute | solution.py:317
  8.7 1.2 %collective-permute-start.2 = (bf16[32,2048]{1,0:T(8,128)(2,1)}, bf16[32,2048]{1,0:T(8,128)(2,1)S(1)}, u32[]{:S(2)}, u32[]{:S(2)}) collective-permute-start(bf16[32,2048]{1,0:T(8,128)(2,1)} %bitcast.17), channel_id=1, source_target_pairs={{0,2},{1,3},{2,4},{3,5},{4,6},{5,7},{6,8},{7,9},{8,10},{9,11},{10,... | collective-permute-start | bytes 393224 | tf_op jit(solution)/shard_map/ppermute | solution.py:317
  9.9 0.0 collective-permute-done.refs_1_
  9.9 2.0 %collective-permute-start.5 = (bf16[32,2048]{1,0:T(8,128)(2,1)S(1)}, bf16[32,2048]{1,0:T(8,128)(2,1)S(1)}, u32[]{:S(2)}, u32[]{:S(2)}) collective-permute-start(bf16[32,2048]{1,0:T(8,128)(2,1)S(1)} %collective-permute-done.refs_1_), channel_id=1, source_target_pairs={{0,14},{1,15},{2,0},{3,1},{4,2},{5,3},{6,4},{7,5},{8,6},{9,7},{10,... | collective-permute-start | bytes 393224 | tf_op jit(solution)/shard_map/ppermute | solution.py:317
  11.9 0.0 collective-permute-start.4
  11.9 0.0 copy-start.3
  11.9 1.7 %copy-done.3 = f32[16,144,144]{2,1,0:T(8,128)S(1)} copy-done((f32[16,144,144]{2,1,0:T(8,128)S(1)}, f32[16,144,144]{2,1,0:T(8,128)}, u32[]{:S(2)}) %copy-start.3) | copy-done | bytes 1327128
  13.6 2.3 %prepare.1.bias_ref = f32[16,144,144]{2,1,0:T(8,128)S(1)} custom-call(f32[16,144,144]{2,1,0:T(8,128)S(1)} %copy-done.3), custom_call_target="tpu_custom_call" | custom-call | flops 1048576 | bytes 65536 | tf_op jit(solution)/shard_map/prepare/pallas_call | solution.py:328
  15.9 0.0 copy-start.2
  15.9 0.5 collective-permute-done.3
  16.4 0.0 collective-permute-done.2
  16.4 1.3 %collective-permute-done.5 = bf16[32,2048]{1,0:T(8,128)(2,1)S(1)} collective-permute-done((bf16[32,2048]{1,0:T(8,128)(2,1)S(1)}, bf16[32,2048]{1,0:T(8,128)(2,1)S(1)}, u32[]{:S(2)}, u32[]{:S(2)}) %collective-permute-start.5) | collective-permute-done | bytes 131104 | tf_op jit(solution)/shard_map/ppermute | solution.py:317
  17.7 0.7 collective-permute-done.4
  18.4 0.0 collective-permute-done.1.right_ref
  18.4 3.1 %collective-permute-start.9 = (bf16[64,2048]{1,0:T(8,128)(2,1)S(1)}, bf16[64,2048]{1,0:T(8,128)(2,1)S(1)}, u32[]{:S(2)}, u32[]{:S(2)}) collective-permute-start(bf16[64,2048]{1,0:T(8,128)(2,1)S(1)} %constant_dynamic-update-slice_fusion.2.refs_5_), channel_id=1, source_target_pairs={{0,14},{1,15},{2,0},{3,1},{4,2},{5,3},{6,4},{7,5},{8,6},{9,7},{10,... | collective-permute-start | bytes 786440 | tf_op jit(solution)/shard_map/ppermute | solution.py:317
  21.5 0.1 collective-permute-start.8
  21.7 3.2 %collective-permute-start.6 = (bf16[2,72,512]{2,1,0:T(8,128)(2,1)S(1)}, bf16[2,72,512]{2,1,0:T(8,128)(2,1)S(1)}, u32[]{:S(2)}, u32[]{:S(2)}) collective-permute-start(bf16[2,72,512]{2,1,0:T(8,128)(2,1)S(1)} %pad_maximum_fusion), channel_id=1, source_target_pairs={{0,32},{32,64},{64,96},{96,128},{128,160},{160,192},{192,224},{1,3... | collective-permute-start | bytes 442376 | tf_op jit(solution)/shard_map/ppermute | solution.py:336
  24.9 4.4 %collective-permute-start.7 = (bf16[2,72,512]{2,1,0:T(8,128)(2,1)S(1)}, bf16[2,72,512]{2,1,0:T(8,128)(2,1)S(1)}, u32[]{:S(2)}, u32[]{:S(2)}) collective-permute-start(bf16[2,72,512]{2,1,0:T(8,128)(2,1)S(1)} %pad_maximum_fusion.1), channel_id=1, source_target_pairs={{32,0},{64,32},{96,64},{128,96},{160,128},{192,160},{224,192},{33,... | collective-permute-start | bytes 442376 | tf_op jit(solution)/shard_map/ppermute | solution.py:337
  29.3 0.0 copy-start
  29.3 0.0 copy-start.1
  29.3 0.0 copy-start.8
  29.3 3.1 %middle_attention.1.x_ref = bf16[288,512]{1,0:T(8,128)(2,1)S(1)} custom-call(bf16[288,512]{1,0:T(8,128)(2,1)S(1)} %get-tuple-element.25.left_ref, bf16[288,512]{1,0:T(8,128)(2,1)S(1)} %collective-permute-done.1.right_ref, f32[1,512]{1,0:T(1,128)S(1)} %bitcast.20, bf16[512,1536]{1,0:T(8,128)(2,1)S(1)} %copy-done.2, f32[16,144,144]{2,1,0:T(8,128)S(1)} %prepare.1.bias_ref, ...), custom_call_target="tpu_custom_call" | custom-call | flops 1048576 | bytes 65536 | tf_op jit(solution)/shard_map/middle_attention/pallas_call | solution.py:339
  32.4 2.0 %middle_mlp.1.blk1_ref = bf16[288,512]{1,0:T(8,128)(2,1)S(1)} custom-call(bf16[288,512]{1,0:T(8,128)(2,1)S(1)} %middle_attention.1.x_ref, f32[1,512]{1,0:T(1,128)S(1)} %bitcast.22, bf16[512,2048]{1,0:T(8,128)(2,1)S(1)} %copy-done, bf16[2048,512]{1,0:T(8,128)(2,1)S(1)} %copy-done.1), custom_call_target="tpu_custom_call" | custom-call | flops 1048576 | bytes 65536 | tf_op jit(solution)/shard_map/middle_mlp/pallas_call | solution.py:342
  34.4 0.0 collective-permute-done.6.top_ref
  34.5 0.0 collective-permute-done.7.bottom_ref
  34.5 0.0 collective-permute-done.9.refs_6_
  34.5 0.0 collective-permute-done.8.refs_3_
  34.5 0.1 collective-permute-start.12
  34.6 3.3 %collective-permute-start.13 = (bf16[64,2048]{1,0:T(8,128)(2,1)S(1)}, bf16[64,2048]{1,0:T(8,128)(2,1)S(1)}, u32[]{:S(2)}, u32[]{:S(2)}) collective-permute-start(bf16[64,2048]{1,0:T(8,128)(2,1)S(1)} %collective-permute-done.9.refs_6_), channel_id=1, source_target_pairs={{0,14},{1,15},{2,0},{3,1},{4,2},{5,3},{6,4},{7,5},{8,6},{9,7},{10,... | collective-permute-start | bytes 786440 | tf_op jit(solution)/shard_map/ppermute | solution.py:317
  37.9 1.5 %collective-permute-start.11 = (bf16[32,2048]{1,0:T(8,128)(2,1)S(1)}, bf16[32,2048]{1,0:T(8,128)(2,1)S(1)}, u32[]{:S(2)}, u32[]{:S(2)}) collective-permute-start(bf16[32,2048]{1,0:T(8,128)(2,1)S(1)} %slice.23), channel_id=1, source_target_pairs={{0,12},{1,13},{2,14},{3,15},{4,0},{5,1},{6,2},{7,3},{8,4},{9,5},{1... | collective-permute-start | bytes 393224 | tf_op jit(solution)/shard_map/ppermute | solution.py:317
  39.4 1.5 %collective-permute-start.10 = (bf16[32,2048]{1,0:T(8,128)(2,1)S(1)}, bf16[32,2048]{1,0:T(8,128)(2,1)S(1)}, u32[]{:S(2)}, u32[]{:S(2)}) collective-permute-start(bf16[32,2048]{1,0:T(8,128)(2,1)S(1)} %slice.22), channel_id=1, source_target_pairs={{0,4},{1,5},{2,6},{3,7},{4,8},{5,9},{6,10},{7,11},{8,12},{9,13},{1... | collective-permute-start | bytes 393224 | tf_op jit(solution)/shard_map/ppermute | solution.py:317
  40.9 3.6 %edge_attention.1.x_ref = bf16[288,512]{1,0:T(8,128)(2,1)S(1)} custom-call(bf16[72,512]{1,0:T(8,128)(2,1)S(1)} %get-tuple-element.48.lt_ref, bf16[72,512]{1,0:T(8,128)(2,1)S(1)} %get-tuple-element.52.rt_ref, bf16[72,512]{1,0:T(8,128)(2,1)S(1)} %get-tuple-element.47.lb_ref, bf16[72,512]{1,0:T(8,128)(2,1)S(1)} %get-tuple-element.51.rb_ref, ...), custom_call_target="tpu_custom_call" | custom-call | flops 1048576 | bytes 65536 | tf_op jit(solution)/shard_map/edge_attention/pallas_call | solution.py:348
  44.5 0.0 copy-start.6
  44.6 3.2 %edge_mlp.1.joined_ref = bf16[4,160,512]{2,1,0:T(8,128)(2,1)S(1)} custom-call(bf16[288,512]{1,0:T(8,128)(2,1)S(1)} %edge_attention.1.x_ref, bf16[288,512]{1,0:T(8,128)(2,1)S(1)} %middle_mlp.1.blk1_ref, f32[1,512]{1,0:T(1,128)S(1)} %bitcast.23, bf16[512,2048]{1,0:T(8,128)(2,1)S(1)} %copy-done, bf16[2048,512]{1,0:T(8,128)(2,1)S(1)} %copy-done.1, ...), custom_call_target="tpu_custom_call" | custom-call | flops 1048576 | bytes 65536 | tf_op jit(solution)/shard_map/edge_mlp/pallas_call | solution.py:351
  47.7 0.0 collective-permute-done.11.refs_9_
  47.7 0.5 collective-permute-done.10.refs_8_
  48.2 0.0 collective-permute-done.12.refs_4_
  48.2 0.0 collective-permute-done.13.refs_7_
  48.2 0.0 collective-permute-start.14
  48.3 0.8 %merge_own.1.own_ref = f32[160,512]{1,0:T(8,128)S(1)} custom-call(bf16[4,160,512]{2,1,0:T(8,128)(2,1)S(1)} %edge_mlp.1.joined_ref, bf16[32,2048]{1,0:T(8,128)(2,1)S(1)} %bitcast.18, bf16[32,2048]{1,0:T(8,128)(2,1)S(1)} %collective-permute-done.refs_1_, bf16[64,2048]{1,0:T(8,128)(2,1)S(1)} %constant_dynamic-update-slice_fusion.refs_2_, ...), custom_call_target="tpu_custom_call" | custom-call | flops 1048576 | bytes 65536 | tf_op jit(solution)/shard_map/merge_own/pallas_call | solution.py:357
  49.1 1.2 %collective-permute-done.14.joined_ref = bf16[4,160,512]{2,1,0:T(8,128)(2,1)S(1)} collective-permute-done((bf16[4,160,512]{2,1,0:T(8,128)(2,1)S(1)}, bf16[4,160,512]{2,1,0:T(8,128)(2,1)S(1)}, u32[]{:S(2)}, u32[]{:S(2)}) %collective-permute-start.14) | collective-permute-done | bytes 655392 | tf_op jit(solution)/shard_map/ppermute | solution.py:355
  50.3 1.4 %merge.1 = bf16[16,72,128]{2,1,0:T(8,128)(2,1)S(1)} custom-call(bf16[4,160,512]{2,1,0:T(8,128)(2,1)S(1)} %collective-permute-done.14.joined_ref, f32[160,512]{1,0:T(8,128)S(1)} %merge_own.1.own_ref, bf16[32,2048]{1,0:T(8,128)(2,1)S(1)} %bitcast.19, bf16[32,2048]{1,0:T(8,128)(2,1)S(1)} %collective-permute-done.refs_1_, ...), custom_call_target="tpu_custom_call" | custom-call | flops 1048576 | bytes 65536 | tf_op jit(solution)/shard_map/merge/pallas_call | solution.py:358
  51.8 16.0 %all_to_all.5.in_ref = bf16[16,72,128]{2,1,0:T(8,128)(2,1)S(1)} all-to-all(bf16[16,72,128]{2,1,0:T(8,128)(2,1)S(1)} %merge.1), channel_id=1, replica_groups={{0,2,4,6,8,10,12,14,16,18,20,22,24,26,28,30},{1,3,5,7,9,11,13,15,17,19,..., dimensions={0} | all-to-all | bytes 589824 | tf_op jit(solution)/shard_map/all_to_all | solution.py:366
  67.7 1.0 %unpack.1 = bf16[6,128,192]{2,1,0:T(8,128)(2,1)} custom-call(bf16[16,72,128]{2,1,0:T(8,128)(2,1)S(1)} %all_to_all.5.in_ref), custom_call_target="tpu_custom_call" | custom-call | flops 1048576 | bytes 65536 | tf_op jit(solution)/shard_map/unpack/pallas_call | solution.py:367
  (22 shorter events, 0.2 us)
Async XLA Ops:
  0.0 9.9 %collective-permute-start = (bf16[32,2048]{1,0:T(8,128)(2,1)}, bf16[32,2048]{1,0:T(8,128)(2,1)S(1)}, u32[]{:S(2)}, u32[]{:S(2)}) collective-permute-start(bf16[32,2048]{1,0:T(8,128)(2,1)} %bitcast.15), channel_id=1, source_target_pairs={{0,16},{1,17},{2,18},{3,19},{4,20},{5,21},{6,22},{7,23},{8,24},{9,... | collective-permute-start | bytes 393224 | tf_op jit(solution)/shard_map/ppermute | solution.py:320
  1.3 1.1 %copy-start.5 = (bf16[12,12,4,512]{3,2,1,0:T(4,128)(2,1)S(1)}, bf16[12,12,4,512]{3,2,1,0:T(4,128)(2,1)}, u32[]{:S(2)}) copy-start(bf16[12,12,4,512]{3,2,1,0:T(4,128)(2,1)} %tokens_hbm.1) | copy-start | bytes 1769476
  2.6 15.8 %collective-permute-start.1 = (bf16[288,512]{1,0:T(8,128)(2,1)S(1)}, bf16[288,512]{1,0:T(8,128)(2,1)S(1)}, u32[]{:S(2)}, u32[]{:S(2)}) collective-permute-start(bf16[288,512]{1,0:T(8,128)(2,1)S(1)} %get-tuple-element.27), channel_id=1, source_target_pairs={{1,0},{2,1},{3,2},{4,3},{5,4},{6,5},{7,6},{8,7},{9,8},{10,9},{11,1... | collective-permute-start | bytes 884744 | tf_op jit(solution)/shard_map/ppermute | solution.py:324
  7.8 8.6 %collective-permute-start.3 = (bf16[32,2048]{1,0:T(8,128)(2,1)}, bf16[32,2048]{1,0:T(8,128)(2,1)S(1)}, u32[]{:S(2)}, u32[]{:S(2)}) collective-permute-start(bf16[32,2048]{1,0:T(8,128)(2,1)} %bitcast.16), channel_id=1, source_target_pairs={{0,14},{1,15},{2,0},{3,1},{4,2},{5,3},{6,4},{7,5},{8,6},{9,7},{10,... | collective-permute-start | bytes 393224 | tf_op jit(solution)/shard_map/ppermute | solution.py:317
  8.7 7.7 %collective-permute-start.2 = (bf16[32,2048]{1,0:T(8,128)(2,1)}, bf16[32,2048]{1,0:T(8,128)(2,1)S(1)}, u32[]{:S(2)}, u32[]{:S(2)}) collective-permute-start(bf16[32,2048]{1,0:T(8,128)(2,1)} %bitcast.17), channel_id=1, source_target_pairs={{0,2},{1,3},{2,4},{3,5},{4,6},{5,7},{6,8},{7,9},{8,10},{9,11},{10,... | collective-permute-start | bytes 393224 | tf_op jit(solution)/shard_map/ppermute | solution.py:317
  9.9 7.8 %collective-permute-start.5 = (bf16[32,2048]{1,0:T(8,128)(2,1)S(1)}, bf16[32,2048]{1,0:T(8,128)(2,1)S(1)}, u32[]{:S(2)}, u32[]{:S(2)}) collective-permute-start(bf16[32,2048]{1,0:T(8,128)(2,1)S(1)} %collective-permute-done.refs_1_), channel_id=1, source_target_pairs={{0,14},{1,15},{2,0},{3,1},{4,2},{5,3},{6,4},{7,5},{8,6},{9,7},{10,... | collective-permute-start | bytes 393224 | tf_op jit(solution)/shard_map/ppermute | solution.py:317
  11.9 6.5 %collective-permute-start.4 = (bf16[32,2048]{1,0:T(8,128)(2,1)S(1)}, bf16[32,2048]{1,0:T(8,128)(2,1)S(1)}, u32[]{:S(2)}, u32[]{:S(2)}) collective-permute-start(bf16[32,2048]{1,0:T(8,128)(2,1)S(1)} %collective-permute-done.refs_1_), channel_id=1, source_target_pairs={{0,2},{1,3},{2,4},{3,5},{4,6},{5,7},{6,8},{7,9},{8,10},{9,11},{10,... | collective-permute-start | bytes 393224 | tf_op jit(solution)/shard_map/ppermute | solution.py:317
  11.9 1.7 %copy-start.3 = (f32[16,144,144]{2,1,0:T(8,128)S(1)}, f32[16,144,144]{2,1,0:T(8,128)}, u32[]{:S(2)}) copy-start(f32[16,144,144]{2,1,0:T(8,128)} %bias_ref) | copy-start | bytes 3981316
  13.6 15.6 %copy-start.4 = (bf16[512,512]{1,0:T(8,128)(2,1)S(1)}, bf16[512,512]{1,0:T(8,128)(2,1)}, u32[]{:S(2)}) copy-start(bf16[512,512]{1,0:T(8,128)(2,1)} %wout_ref.3) | copy-start | bytes 1572868
  13.6 15.7 %copy-start.7 = (f32[512]{0:T(512)S(1)}, f32[512]{0:T(512)}, u32[]{:S(2)}) copy-start(f32[512]{0:T(512)} %param.11) | copy-start | bytes 6148
  15.9 13.4 %copy-start.2 = (bf16[512,1536]{1,0:T(8,128)(2,1)S(1)}, bf16[512,1536]{1,0:T(8,128)(2,1)}, u32[]{:S(2)}) copy-start(bf16[512,1536]{1,0:T(8,128)(2,1)} %wqkv_ref.3) | copy-start | bytes 4718596
  18.4 16.1 %collective-permute-start.9 = (bf16[64,2048]{1,0:T(8,128)(2,1)S(1)}, bf16[64,2048]{1,0:T(8,128)(2,1)S(1)}, u32[]{:S(2)}, u32[]{:S(2)}) collective-permute-start(bf16[64,2048]{1,0:T(8,128)(2,1)S(1)} %constant_dynamic-update-slice_fusion.2.refs_5_), channel_id=1, source_target_pairs={{0,14},{1,15},{2,0},{3,1},{4,2},{5,3},{6,4},{7,5},{8,6},{9,7},{10,... | collective-permute-start | bytes 786440 | tf_op jit(solution)/shard_map/ppermute | solution.py:317
  21.5 12.9 %collective-permute-start.8 = (bf16[64,2048]{1,0:T(8,128)(2,1)S(1)}, bf16[64,2048]{1,0:T(8,128)(2,1)S(1)}, u32[]{:S(2)}, u32[]{:S(2)}) collective-permute-start(bf16[64,2048]{1,0:T(8,128)(2,1)S(1)} %constant_dynamic-update-slice_fusion.refs_2_), channel_id=1, source_target_pairs={{0,2},{1,3},{2,4},{3,5},{4,6},{5,7},{6,8},{7,9},{8,10},{9,11},{10,... | collective-permute-start | bytes 786440 | tf_op jit(solution)/shard_map/ppermute | solution.py:317
  21.7 12.8 %collective-permute-start.6 = (bf16[2,72,512]{2,1,0:T(8,128)(2,1)S(1)}, bf16[2,72,512]{2,1,0:T(8,128)(2,1)S(1)}, u32[]{:S(2)}, u32[]{:S(2)}) collective-permute-start(bf16[2,72,512]{2,1,0:T(8,128)(2,1)S(1)} %pad_maximum_fusion), channel_id=1, source_target_pairs={{0,32},{32,64},{64,96},{96,128},{128,160},{160,192},{192,224},{1,3... | collective-permute-start | bytes 442376 | tf_op jit(solution)/shard_map/ppermute | solution.py:336
  24.9 9.6 %collective-permute-start.7 = (bf16[2,72,512]{2,1,0:T(8,128)(2,1)S(1)}, bf16[2,72,512]{2,1,0:T(8,128)(2,1)S(1)}, u32[]{:S(2)}, u32[]{:S(2)}) collective-permute-start(bf16[2,72,512]{2,1,0:T(8,128)(2,1)S(1)} %pad_maximum_fusion.1), channel_id=1, source_target_pairs={{32,0},{64,32},{96,64},{128,96},{160,128},{192,160},{224,192},{33,... | collective-permute-start | bytes 442376 | tf_op jit(solution)/shard_map/ppermute | solution.py:337
  29.3 3.1 %copy-start = (bf16[512,2048]{1,0:T(8,128)(2,1)S(1)}, bf16[512,2048]{1,0:T(8,128)(2,1)}, u32[]{:S(2)}) copy-start(bf16[512,2048]{1,0:T(8,128)(2,1)} %up_ref.3) | copy-start | bytes 6291460
  29.3 3.1 %copy-start.1 = (bf16[2048,512]{1,0:T(8,128)(2,1)S(1)}, bf16[2048,512]{1,0:T(8,128)(2,1)}, u32[]{:S(2)}) copy-start(bf16[2048,512]{1,0:T(8,128)(2,1)} %down_ref.3) | copy-start | bytes 6291460
  29.3 3.1 %copy-start.8 = (f32[512]{0:T(512)S(1)}, f32[512]{0:T(512)}, u32[]{:S(2)}) copy-start(f32[512]{0:T(512)} %param.15) | copy-start | bytes 6148
  34.5 13.7 %collective-permute-start.12 = (bf16[64,2048]{1,0:T(8,128)(2,1)S(1)}, bf16[64,2048]{1,0:T(8,128)(2,1)S(1)}, u32[]{:S(2)}, u32[]{:S(2)}) collective-permute-start(bf16[64,2048]{1,0:T(8,128)(2,1)S(1)} %collective-permute-done.8.refs_3_), channel_id=1, source_target_pairs={{0,2},{1,3},{2,4},{3,5},{4,6},{5,7},{6,8},{7,9},{8,10},{9,11},{10,... | collective-permute-start | bytes 786440 | tf_op jit(solution)/shard_map/ppermute | solution.py:317
  34.6 13.7 %collective-permute-start.13 = (bf16[64,2048]{1,0:T(8,128)(2,1)S(1)}, bf16[64,2048]{1,0:T(8,128)(2,1)S(1)}, u32[]{:S(2)}, u32[]{:S(2)}) collective-permute-start(bf16[64,2048]{1,0:T(8,128)(2,1)S(1)} %collective-permute-done.9.refs_6_), channel_id=1, source_target_pairs={{0,14},{1,15},{2,0},{3,1},{4,2},{5,3},{6,4},{7,5},{8,6},{9,7},{10,... | collective-permute-start | bytes 786440 | tf_op jit(solution)/shard_map/ppermute | solution.py:317
  37.9 9.8 %collective-permute-start.11 = (bf16[32,2048]{1,0:T(8,128)(2,1)S(1)}, bf16[32,2048]{1,0:T(8,128)(2,1)S(1)}, u32[]{:S(2)}, u32[]{:S(2)}) collective-permute-start(bf16[32,2048]{1,0:T(8,128)(2,1)S(1)} %slice.23), channel_id=1, source_target_pairs={{0,12},{1,13},{2,14},{3,15},{4,0},{5,1},{6,2},{7,3},{8,4},{9,5},{1... | collective-permute-start | bytes 393224 | tf_op jit(solution)/shard_map/ppermute | solution.py:317
  39.4 8.9 %collective-permute-start.10 = (bf16[32,2048]{1,0:T(8,128)(2,1)S(1)}, bf16[32,2048]{1,0:T(8,128)(2,1)S(1)}, u32[]{:S(2)}, u32[]{:S(2)}) collective-permute-start(bf16[32,2048]{1,0:T(8,128)(2,1)S(1)} %slice.22), channel_id=1, source_target_pairs={{0,4},{1,5},{2,6},{3,7},{4,8},{5,9},{6,10},{7,11},{8,12},{9,13},{1... | collective-permute-start | bytes 393224 | tf_op jit(solution)/shard_map/ppermute | solution.py:317
  40.9 3.6 %copy-start.9 = (f32[2048]{0:T(1024)S(1)}, f32[2048]{0:T(1024)}, u32[]{:S(2)}) copy-start(f32[2048]{0:T(1024)} %param.18) | copy-start | bytes 24580
  44.5 3.7 %copy-start.6 = (bf16[2048,32]{0,1:T(8,128)(2,1)S(1)}, bf16[2048,32]{0,1:T(8,128)(2,1)}, u32[]{:S(2)}) copy-start(bf16[2048,32]{0,1:T(8,128)(2,1)} %param.19) | copy-start | bytes 393220
  48.2 2.1 %collective-permute-start.14 = (bf16[4,160,512]{2,1,0:T(8,128)(2,1)S(1)}, bf16[4,160,512]{2,1,0:T(8,128)(2,1)S(1)}, u32[]{:S(2)}, u32[]{:S(2)}) collective-permute-start(bf16[4,160,512]{2,1,0:T(8,128)(2,1)S(1)} %edge_mlp.1.joined_ref), channel_id=1, source_target_pairs={{0,1},{1,0},{2,3},{3,2},{4,5},{5,4},{6,7},{7,6},{8,9},{9,8},{10,11... | collective-permute-start | bytes 1966088 | tf_op jit(solution)/shard_map/ppermute | solution.py:355

commit v4 on v3

--- a/solution.py
+++ b/solution.py
@@ -232,47 +232,46 @@
 
 
 def merge_columns(joined_ref, w_refs):
-    total = 0.0
-    for p in range(4):
-        lanes = slice(p * WIDTH, (p + 1) * WIDTH)
-        w = jnp.concatenate([r[:, lanes] for r in w_refs], axis=0)
-        total = total + dot(joined_ref[p], w, NT)
-    return total
-
-
-def merge_own_kernel(joined_ref, *refs):
-    w_refs, out_ref = refs[:-1], refs[-1]
-    out_ref[:, :256] = merge_columns(joined_ref, w_refs[:5])
-    out_ref[:, 256:] = merge_columns(joined_ref, w_refs[5:])
-
-
-def merge_kernel(joined_ref, own_ref, *refs):
-    w_refs, (out_ref, merged_ref, message_ref) = refs[:-3], refs[-3:]
-    lon = lax.axis_index("lon")
-    chips = lax.axis_size("lon") // 2
-    core = lax.rem(lon, 2)
-    z = lax.rem(lon // 2, 8)
-    y = lon // chips
-    merged_ref[core] = own_ref[...]
-    merged_ref[1 - core, :, :256] = merge_columns(joined_ref, w_refs[:5])
-    merged_ref[1 - core, :, 256:] = merge_columns(joined_ref, w_refs[5:])
     chunk = lax.broadcasted_iota(jnp.int32, (MERGE_PAD, 128), 1) // 32
-    for tile in range(4):
-        for c in range(2):
-            parts = [
-                merged_ref[c, lev * MERGE_PAD : (lev + 1) * MERGE_PAD, tile * 128 : (tile + 1) * 128] for lev in range(4)
+    messages = []
+    for part in (w_refs[:5], w_refs[5:]):
+        total = 0.0
+        for p in range(4):
+            lanes = slice(p * WIDTH, (p + 1) * WIDTH)
+            total = total + dot(joined_ref[p], jnp.concatenate([r[:, lanes] for r in part], axis=0), NT)
+        for tile in range(2):
+            levels = [
+                total[lev * MERGE_PAD : (lev + 1) * MERGE_PAD, tile * 128 : (tile + 1) * 128] for lev in range(4)
             ]
             for d in range(4):
                 value = jnp.zeros((MERGE_PAD, 128), F32)
                 for lev in range(4):
                     shift = (lev - d) % 4 * 32
-                    moved = pltpu.roll(parts[lev], shift, 1) if shift else parts[lev]
+                    moved = pltpu.roll(levels[lev], shift, 1) if shift else levels[lev]
                     value = jnp.where(chunk == lev, moved, value)
-                message_ref[tile * 4 + d, c * 36 : c * 36 + 36, :] = value[:36]
-    for block in range(16):
+                messages.append(value)
+    return messages
+
+
+def merge_own_kernel(joined_ref, *refs):
+    for block, value in enumerate(merge_columns(joined_ref, refs[:-1])):
+        refs[-1][block] = value
+
+
+def merge_kernel(joined_ref, own_ref, *refs):
+    w_refs, (out_ref, message_ref) = refs[:-2], refs[-2:]
+    lon = lax.axis_index("lon")
+    chips = lax.axis_size("lon") // 2
+    first = lax.rem(lon, 2) == 0
+    z = lax.rem(lon // 2, 8)
+    y = lon // chips
+    for block, other in enumerate(merge_columns(joined_ref, w_refs)):
+        own = own_ref[block]
+        message_ref[block, :MERGE_PAD] = jnp.where(first, own, other)
+        message_ref[block, 36 : 36 + MERGE_PAD] = jnp.where(first, other, own)
         zd = lax.rem(z + Z_STEPS[block // 2] + 8, 8)
         yd = 1 - y if block % 2 else y
-        out_ref[yd * 8 + zd] = message_ref[block].astype(BF)
+        out_ref[yd * 8 + zd] = message_ref[block, :72].astype(BF)
 
 
 def unpack_kernel(in_ref, out_ref, rows_ref):
@@ -354,17 +353,17 @@
     joined, far_up, far_down, up[-1], down[-1] = barrier((joined, far_up, far_down, up[-1], down[-1]))
     neighbour = lax.ppermute(joined, "lon", [(i, i ^ 1) for i in range(lon_count)])
     w_cols = [w_own, w_pair] + up + down + [far_up, far_down]
-    own = call(merge_own_kernel, shape((4 * MERGE_PAD, WIDTH), F32), [VMEM] * 11, [], "merge_own")(joined, *w_cols)
+    own = call(merge_own_kernel, shape((16, MERGE_PAD, 128), F32), [VMEM] * 11, [], "merge_own")(joined, *w_cols)
     messages = call(
         merge_kernel,
         shape((16, 72, 128)),
         [VMEM] * 12,
-        [pltpu.VMEM((2, 4 * MERGE_PAD, WIDTH), F32), pltpu.VMEM((16, 72, 128), F32)],
+        [pltpu.VMEM((16, 80, 128), F32)],
         "merge",
     )(neighbour, own, *w_cols)
     cores = [[2 * i + c for i in range(chips)] for c in range(2)]
     received = lax.all_to_all(messages, "lon", 0, 0, tiled=True, axis_index_groups=cores)
-    out = call(unpack_kernel, shape((6, 128, 192)), [VMEM], [pltpu.VMEM((1152, 128), F32)],  "unpack")(received)
+    out = call(unpack_kernel, shape((6, 128, 192)), [VMEM], [pltpu.VMEM((1160, 128), F32)],  "unpack")(received)
     return out.reshape(6, 4, 32, 192).transpose(0, 3, 1, 2)
 
 

time: 69.5 us -> 69.2 us (level)
  transfers between devices with their start and end apart: 15 -> 15, of which waited for: 5 -> 5; matrix products, arithmetic and copies ran while one was open for 0% -> 0% of each run, Pallas kernels for 22% -> 23%
where the time goes in v4:
time: 69.2 us; the launch traced here: 68.4 us
  starting transfers between devices  27.7 us (40%)
  Pallas kernels  17.6 us (25%)
  blocking collectives  16 us (23%)
  waiting for transfers between devices  3.95 us (6%)
  local copies, waits for them, and re-layouts  2.87 us (4%)
    all_to_all x1, blocking collectives, on_device(): lax.all_to_all(messages, 'lon', 0, 0, tiled=True, axis_index_groups=cores)  16 us
    ppermute x10, starting transfers between devices, around(): return lax.ppermute(block, 'lon', route)  13.6 us
    ppermute x1, starting transfers between devices, on_device(): lax.ppermute(right_own, 'lon', [((i + 1) % lon_count, i) for i in range(l...  5.27 us
    ppermute x1, starting transfers between devices, on_device(): lax.ppermute(top_rows, 'lat', [(i + 1, i) for i in range(lat_count - 1)])  4.35 us
    pallas_call x1, Pallas kernels, on_device(): call(edge_attention_kernel, shape((BAND, WIDTH)), [VMEM] * 10, [], 'edge_...  3.62 us
    ppermute x1, starting transfers between devices, on_device(): lax.ppermute(bottom_rows, 'lat', [(i, i + 1) for i in range(lat_count - 1)])  3.17 us
    pallas_call x1, Pallas kernels, on_device(): call(edge_mlp_kernel, shape((4, 4 * MERGE_PAD, WIDTH)), [VMEM] * 6, [], '...  3.15 us
    pallas_call x1, Pallas kernels, on_device(): call(middle_attention_kernel, shape((BAND, WIDTH)), [VMEM] * 6, [], 'midd...  3.06 us
  transfers between devices with their start and end apart: 15, of which 5 were waited for; matrix products, arithmetic and copies ran while one was open for 0% of the time, Pallas kernels for 23%

profile of v4, /device:TPU:18, one launch (start us, length us, event | category | flops | bytes accessed | tf_op | source)
XLA Modules:
  0.0 68.4 jit_solution(1013315429496848185)
XLA Ops:
  0.0 1.3 %collective-permute-start = (bf16[32,2048]{1,0:T(8,128)(2,1)}, bf16[32,2048]{1,0:T(8,128)(2,1)S(1)}, u32[]{:S(2)}, u32[]{:S(2)}) collective-permute-start(bf16[32,2048]{1,0:T(8,128)(2,1)} %bitcast.15), channel_id=1, source_target_pairs={{0,16},{1,17},{2,18},{3,19},{4,20},{5,21},{6,22},{7,23},{8,24},{9,... | collective-permute-start | bytes 393224 | tf_op jit(solution)/shard_map/ppermute | solution.py:319
  1.3 1.1 %copy-done.5 = bf16[12,12,4,512]{3,2,1,0:T(4,128)(2,1)S(1)} copy-done((bf16[12,12,4,512]{3,2,1,0:T(4,128)(2,1)S(1)}, bf16[12,12,4,512]{3,2,1,0:T(4,128)(2,1)}, u32[]{:S(2)}) %copy-start.5) | copy-done | bytes 589848
  2.3 0.2 split.1
  2.6 5.3 %collective-permute-start.1 = (bf16[288,512]{1,0:T(8,128)(2,1)S(1)}, bf16[288,512]{1,0:T(8,128)(2,1)S(1)}, u32[]{:S(2)}, u32[]{:S(2)}) collective-permute-start(bf16[288,512]{1,0:T(8,128)(2,1)S(1)} %get-tuple-element.27), channel_id=1, source_target_pairs={{1,0},{2,1},{3,2},{4,3},{5,4},{6,5},{7,6},{8,7},{9,8},{10,9},{11,1... | collective-permute-start | bytes 884744 | tf_op jit(solution)/shard_map/ppermute | solution.py:323
  7.8 0.8 %collective-permute-start.3 = (bf16[32,2048]{1,0:T(8,128)(2,1)}, bf16[32,2048]{1,0:T(8,128)(2,1)S(1)}, u32[]{:S(2)}, u32[]{:S(2)}) collective-permute-start(bf16[32,2048]{1,0:T(8,128)(2,1)} %bitcast.16), channel_id=1, source_target_pairs={{0,14},{1,15},{2,0},{3,1},{4,2},{5,3},{6,4},{7,5},{8,6},{9,7},{10,... | collective-permute-start | bytes 393224 | tf_op jit(solution)/shard_map/ppermute | solution.py:316
  8.7 1.2 %collective-permute-start.2 = (bf16[32,2048]{1,0:T(8,128)(2,1)}, bf16[32,2048]{1,0:T(8,128)(2,1)S(1)}, u32[]{:S(2)}, u32[]{:S(2)}) collective-permute-start(bf16[32,2048]{1,0:T(8,128)(2,1)} %bitcast.17), channel_id=1, source_target_pairs={{0,2},{1,3},{2,4},{3,5},{4,6},{5,7},{6,8},{7,9},{8,10},{9,11},{10,... | collective-permute-start | bytes 393224 | tf_op jit(solution)/shard_map/ppermute | solution.py:316
  9.9 0.0 collective-permute-done.refs_1_
  9.9 2.0 %collective-permute-start.5 = (bf16[32,2048]{1,0:T(8,128)(2,1)S(1)}, bf16[32,2048]{1,0:T(8,128)(2,1)S(1)}, u32[]{:S(2)}, u32[]{:S(2)}) collective-permute-start(bf16[32,2048]{1,0:T(8,128)(2,1)S(1)} %collective-permute-done.refs_1_), channel_id=1, source_target_pairs={{0,14},{1,15},{2,0},{3,1},{4,2},{5,3},{6,4},{7,5},{8,6},{9,7},{10,... | collective-permute-start | bytes 393224 | tf_op jit(solution)/shard_map/ppermute | solution.py:316
  11.9 0.0 collective-permute-start.4
  11.9 0.0 copy-start.3
  11.9 1.7 %copy-done.3 = f32[16,144,144]{2,1,0:T(8,128)S(1)} copy-done((f32[16,144,144]{2,1,0:T(8,128)S(1)}, f32[16,144,144]{2,1,0:T(8,128)}, u32[]{:S(2)}) %copy-start.3) | copy-done | bytes 1327128
  13.6 2.3 %prepare.1.bias_ref = f32[16,144,144]{2,1,0:T(8,128)S(1)} custom-call(f32[16,144,144]{2,1,0:T(8,128)S(1)} %copy-done.3), custom_call_target="tpu_custom_call" | custom-call | flops 1048576 | bytes 65536 | tf_op jit(solution)/shard_map/prepare/pallas_call | solution.py:327
  15.9 0.0 copy-start.2
  15.9 0.5 collective-permute-done.3
  16.4 0.0 collective-permute-done.2
  16.4 1.3 %collective-permute-done.5 = bf16[32,2048]{1,0:T(8,128)(2,1)S(1)} collective-permute-done((bf16[32,2048]{1,0:T(8,128)(2,1)S(1)}, bf16[32,2048]{1,0:T(8,128)(2,1)S(1)}, u32[]{:S(2)}, u32[]{:S(2)}) %collective-permute-start.5) | collective-permute-done | bytes 131104 | tf_op jit(solution)/shard_map/ppermute | solution.py:316
  17.7 0.7 collective-permute-done.4
  18.4 0.0 collective-permute-done.1.right_ref
  18.4 3.1 %collective-permute-start.9 = (bf16[64,2048]{1,0:T(8,128)(2,1)S(1)}, bf16[64,2048]{1,0:T(8,128)(2,1)S(1)}, u32[]{:S(2)}, u32[]{:S(2)}) collective-permute-start(bf16[64,2048]{1,0:T(8,128)(2,1)S(1)} %constant_dynamic-update-slice_fusion.2.refs_5_), channel_id=1, source_target_pairs={{0,14},{1,15},{2,0},{3,1},{4,2},{5,3},{6,4},{7,5},{8,6},{9,7},{10,... | collective-permute-start | bytes 786440 | tf_op jit(solution)/shard_map/ppermute | solution.py:316
  21.5 0.1 collective-permute-start.8
  21.7 3.2 %collective-permute-start.6 = (bf16[2,72,512]{2,1,0:T(8,128)(2,1)S(1)}, bf16[2,72,512]{2,1,0:T(8,128)(2,1)S(1)}, u32[]{:S(2)}, u32[]{:S(2)}) collective-permute-start(bf16[2,72,512]{2,1,0:T(8,128)(2,1)S(1)} %pad_maximum_fusion), channel_id=1, source_target_pairs={{0,32},{32,64},{64,96},{96,128},{128,160},{160,192},{192,224},{1,3... | collective-permute-start | bytes 442376 | tf_op jit(solution)/shard_map/ppermute | solution.py:335
  24.9 4.4 %collective-permute-start.7 = (bf16[2,72,512]{2,1,0:T(8,128)(2,1)S(1)}, bf16[2,72,512]{2,1,0:T(8,128)(2,1)S(1)}, u32[]{:S(2)}, u32[]{:S(2)}) collective-permute-start(bf16[2,72,512]{2,1,0:T(8,128)(2,1)S(1)} %pad_maximum_fusion.1), channel_id=1, source_target_pairs={{32,0},{64,32},{96,64},{128,96},{160,128},{192,160},{224,192},{33,... | collective-permute-start | bytes 442376 | tf_op jit(solution)/shard_map/ppermute | solution.py:336
  29.3 0.0 copy-start
  29.3 0.0 copy-start.1
  29.3 0.0 copy-start.8
  29.3 3.1 %middle_attention.1.x_ref = bf16[288,512]{1,0:T(8,128)(2,1)S(1)} custom-call(bf16[288,512]{1,0:T(8,128)(2,1)S(1)} %get-tuple-element.25.left_ref, bf16[288,512]{1,0:T(8,128)(2,1)S(1)} %collective-permute-done.1.right_ref, f32[1,512]{1,0:T(1,128)S(1)} %bitcast.20, bf16[512,1536]{1,0:T(8,128)(2,1)S(1)} %copy-done.2, f32[16,144,144]{2,1,0:T(8,128)S(1)} %prepare.1.bias_ref, ...), custom_call_target="tpu_custom_call" | custom-call | flops 1048576 | bytes 65536 | tf_op jit(solution)/shard_map/middle_attention/pallas_call | solution.py:338
  32.4 2.0 %middle_mlp.1.blk1_ref = bf16[288,512]{1,0:T(8,128)(2,1)S(1)} custom-call(bf16[288,512]{1,0:T(8,128)(2,1)S(1)} %middle_attention.1.x_ref, f32[1,512]{1,0:T(1,128)S(1)} %bitcast.22, bf16[512,2048]{1,0:T(8,128)(2,1)S(1)} %copy-done, bf16[2048,512]{1,0:T(8,128)(2,1)S(1)} %copy-done.1), custom_call_target="tpu_custom_call" | custom-call | flops 1048576 | bytes 65536 | tf_op jit(solution)/shard_map/middle_mlp/pallas_call | solution.py:341
  34.4 0.0 collective-permute-done.6.top_ref
  34.5 0.0 collective-permute-done.7.bottom_ref
  34.5 0.0 collective-permute-done.9.refs_6_
  34.5 0.0 collective-permute-done.8.refs_3_
  34.5 0.1 collective-permute-start.12
  34.6 3.3 %collective-permute-start.13 = (bf16[64,2048]{1,0:T(8,128)(2,1)S(1)}, bf16[64,2048]{1,0:T(8,128)(2,1)S(1)}, u32[]{:S(2)}, u32[]{:S(2)}) collective-permute-start(bf16[64,2048]{1,0:T(8,128)(2,1)S(1)} %collective-permute-done.9.refs_6_), channel_id=1, source_target_pairs={{0,14},{1,15},{2,0},{3,1},{4,2},{5,3},{6,4},{7,5},{8,6},{9,7},{10,... | collective-permute-start | bytes 786440 | tf_op jit(solution)/shard_map/ppermute | solution.py:316
  37.9 1.5 %collective-permute-start.11 = (bf16[32,2048]{1,0:T(8,128)(2,1)S(1)}, bf16[32,2048]{1,0:T(8,128)(2,1)S(1)}, u32[]{:S(2)}, u32[]{:S(2)}) collective-permute-start(bf16[32,2048]{1,0:T(8,128)(2,1)S(1)} %slice.23), channel_id=1, source_target_pairs={{0,12},{1,13},{2,14},{3,15},{4,0},{5,1},{6,2},{7,3},{8,4},{9,5},{1... | collective-permute-start | bytes 393224 | tf_op jit(solution)/shard_map/ppermute | solution.py:316
  39.4 1.5 %collective-permute-start.10 = (bf16[32,2048]{1,0:T(8,128)(2,1)S(1)}, bf16[32,2048]{1,0:T(8,128)(2,1)S(1)}, u32[]{:S(2)}, u32[]{:S(2)}) collective-permute-start(bf16[32,2048]{1,0:T(8,128)(2,1)S(1)} %slice.22), channel_id=1, source_target_pairs={{0,4},{1,5},{2,6},{3,7},{4,8},{5,9},{6,10},{7,11},{8,12},{9,13},{1... | collective-permute-start | bytes 393224 | tf_op jit(solution)/shard_map/ppermute | solution.py:316
  40.9 3.6 %edge_attention.1.x_ref = bf16[288,512]{1,0:T(8,128)(2,1)S(1)} custom-call(bf16[72,512]{1,0:T(8,128)(2,1)S(1)} %get-tuple-element.48.lt_ref, bf16[72,512]{1,0:T(8,128)(2,1)S(1)} %get-tuple-element.52.rt_ref, bf16[72,512]{1,0:T(8,128)(2,1)S(1)} %get-tuple-element.47.lb_ref, bf16[72,512]{1,0:T(8,128)(2,1)S(1)} %get-tuple-element.51.rb_ref, ...), custom_call_target="tpu_custom_call" | custom-call | flops 1048576 | bytes 65536 | tf_op jit(solution)/shard_map/edge_attention/pallas_call | solution.py:347
  44.5 0.0 copy-start.6
  44.6 3.2 %edge_mlp.1.joined_ref = bf16[4,160,512]{2,1,0:T(8,128)(2,1)S(1)} custom-call(bf16[288,512]{1,0:T(8,128)(2,1)S(1)} %edge_attention.1.x_ref, bf16[288,512]{1,0:T(8,128)(2,1)S(1)} %middle_mlp.1.blk1_ref, f32[1,512]{1,0:T(1,128)S(1)} %bitcast.23, bf16[512,2048]{1,0:T(8,128)(2,1)S(1)} %copy-done, bf16[2048,512]{1,0:T(8,128)(2,1)S(1)} %copy-done.1, ...), custom_call_target="tpu_custom_call" | custom-call | flops 1048576 | bytes 65536 | tf_op jit(solution)/shard_map/edge_mlp/pallas_call | solution.py:350
  47.7 0.0 collective-permute-done.11.refs_9_
  47.7 0.5 collective-permute-done.10.refs_8_
  48.2 0.0 collective-permute-done.12.refs_4_
  48.2 0.0 collective-permute-done.13.refs_7_
  48.2 0.0 collective-permute-start.14
  48.3 1.1 %merge_own.1.own_ref = f32[16,40,128]{2,1,0:T(8,128)S(1)} custom-call(bf16[4,160,512]{2,1,0:T(8,128)(2,1)S(1)} %edge_mlp.1.joined_ref, bf16[32,2048]{1,0:T(8,128)(2,1)S(1)} %bitcast.18, bf16[32,2048]{1,0:T(8,128)(2,1)S(1)} %collective-permute-done.refs_1_, bf16[64,2048]{1,0:T(8,128)(2,1)S(1)} %constant_dynamic-update-slice_fusion.refs_2_, ...), custom_call_target="tpu_custom_call" | custom-call | flops 1048576 | bytes 65536 | tf_op jit(solution)/shard_map/merge_own/pallas_call | solution.py:356
  49.4 1.0 %collective-permute-done.14.joined_ref = bf16[4,160,512]{2,1,0:T(8,128)(2,1)S(1)} collective-permute-done((bf16[4,160,512]{2,1,0:T(8,128)(2,1)S(1)}, bf16[4,160,512]{2,1,0:T(8,128)(2,1)S(1)}, u32[]{:S(2)}, u32[]{:S(2)}) %collective-permute-start.14) | collective-permute-done | bytes 655392 | tf_op jit(solution)/shard_map/ppermute | solution.py:354
  50.3 1.1 %merge.1 = bf16[16,72,128]{2,1,0:T(8,128)(2,1)S(1)} custom-call(bf16[4,160,512]{2,1,0:T(8,128)(2,1)S(1)} %collective-permute-done.14.joined_ref, f32[16,40,128]{2,1,0:T(8,128)S(1)} %merge_own.1.own_ref, bf16[32,2048]{1,0:T(8,128)(2,1)S(1)} %bitcast.19, bf16[32,2048]{1,0:T(8,128)(2,1)S(1)} %collective-permute-done.refs_1_, ...), custom_call_target="tpu_custom_call" | custom-call | flops 1048576 | bytes 65536 | tf_op jit(solution)/shard_map/merge/pallas_call | solution.py:357
  51.5 16.0 %all_to_all.5.in_ref = bf16[16,72,128]{2,1,0:T(8,128)(2,1)S(1)} all-to-all(bf16[16,72,128]{2,1,0:T(8,128)(2,1)S(1)} %merge.1), channel_id=1, replica_groups={{0,2,4,6,8,10,12,14,16,18,20,22,24,26,28,30},{1,3,5,7,9,11,13,15,17,19,..., dimensions={0} | all-to-all | bytes 589824 | tf_op jit(solution)/shard_map/all_to_all | solution.py:365
  67.5 1.0 %unpack.1 = bf16[6,128,192]{2,1,0:T(8,128)(2,1)} custom-call(bf16[16,72,128]{2,1,0:T(8,128)(2,1)S(1)} %all_to_all.5.in_ref), custom_call_target="tpu_custom_call" | custom-call | flops 1048576 | bytes 65536 | tf_op jit(solution)/shard_map/unpack/pallas_call | solution.py:366
  (22 shorter events, 0.2 us)
Async XLA Ops:
  0.0 9.9 %collective-permute-start = (bf16[32,2048]{1,0:T(8,128)(2,1)}, bf16[32,2048]{1,0:T(8,128)(2,1)S(1)}, u32[]{:S(2)}, u32[]{:S(2)}) collective-permute-start(bf16[32,2048]{1,0:T(8,128)(2,1)} %bitcast.15), channel_id=1, source_target_pairs={{0,16},{1,17},{2,18},{3,19},{4,20},{5,21},{6,22},{7,23},{8,24},{9,... | collective-permute-start | bytes 393224 | tf_op jit(solution)/shard_map/ppermute | solution.py:319
  1.3 1.1 %copy-start.5 = (bf16[12,12,4,512]{3,2,1,0:T(4,128)(2,1)S(1)}, bf16[12,12,4,512]{3,2,1,0:T(4,128)(2,1)}, u32[]{:S(2)}) copy-start(bf16[12,12,4,512]{3,2,1,0:T(4,128)(2,1)} %tokens_hbm.1) | copy-start | bytes 1769476
  2.6 15.8 %collective-permute-start.1 = (bf16[288,512]{1,0:T(8,128)(2,1)S(1)}, bf16[288,512]{1,0:T(8,128)(2,1)S(1)}, u32[]{:S(2)}, u32[]{:S(2)}) collective-permute-start(bf16[288,512]{1,0:T(8,128)(2,1)S(1)} %get-tuple-element.27), channel_id=1, source_target_pairs={{1,0},{2,1},{3,2},{4,3},{5,4},{6,5},{7,6},{8,7},{9,8},{10,9},{11,1... | collective-permute-start | bytes 884744 | tf_op jit(solution)/shard_map/ppermute | solution.py:323
  7.8 8.6 %collective-permute-start.3 = (bf16[32,2048]{1,0:T(8,128)(2,1)}, bf16[32,2048]{1,0:T(8,128)(2,1)S(1)}, u32[]{:S(2)}, u32[]{:S(2)}) collective-permute-start(bf16[32,2048]{1,0:T(8,128)(2,1)} %bitcast.16), channel_id=1, source_target_pairs={{0,14},{1,15},{2,0},{3,1},{4,2},{5,3},{6,4},{7,5},{8,6},{9,7},{10,... | collective-permute-start | bytes 393224 | tf_op jit(solution)/shard_map/ppermute | solution.py:316
  8.7 7.7 %collective-permute-start.2 = (bf16[32,2048]{1,0:T(8,128)(2,1)}, bf16[32,2048]{1,0:T(8,128)(2,1)S(1)}, u32[]{:S(2)}, u32[]{:S(2)}) collective-permute-start(bf16[32,2048]{1,0:T(8,128)(2,1)} %bitcast.17), channel_id=1, source_target_pairs={{0,2},{1,3},{2,4},{3,5},{4,6},{5,7},{6,8},{7,9},{8,10},{9,11},{10,... | collective-permute-start | bytes 393224 | tf_op jit(solution)/shard_map/ppermute | solution.py:316
  9.9 7.8 %collective-permute-start.5 = (bf16[32,2048]{1,0:T(8,128)(2,1)S(1)}, bf16[32,2048]{1,0:T(8,128)(2,1)S(1)}, u32[]{:S(2)}, u32[]{:S(2)}) collective-permute-start(bf16[32,2048]{1,0:T(8,128)(2,1)S(1)} %collective-permute-done.refs_1_), channel_id=1, source_target_pairs={{0,14},{1,15},{2,0},{3,1},{4,2},{5,3},{6,4},{7,5},{8,6},{9,7},{10,... | collective-permute-start | bytes 393224 | tf_op jit(solution)/shard_map/ppermute | solution.py:316
  11.9 6.5 %collective-permute-start.4 = (bf16[32,2048]{1,0:T(8,128)(2,1)S(1)}, bf16[32,2048]{1,0:T(8,128)(2,1)S(1)}, u32[]{:S(2)}, u32[]{:S(2)}) collective-permute-start(bf16[32,2048]{1,0:T(8,128)(2,1)S(1)} %collective-permute-done.refs_1_), channel_id=1, source_target_pairs={{0,2},{1,3},{2,4},{3,5},{4,6},{5,7},{6,8},{7,9},{8,10},{9,11},{10,... | collective-permute-start | bytes 393224 | tf_op jit(solution)/shard_map/ppermute | solution.py:316
  11.9 1.7 %copy-start.3 = (f32[16,144,144]{2,1,0:T(8,128)S(1)}, f32[16,144,144]{2,1,0:T(8,128)}, u32[]{:S(2)}) copy-start(f32[16,144,144]{2,1,0:T(8,128)} %bias_ref) | copy-start | bytes 3981316
  13.6 15.6 %copy-start.4 = (bf16[512,512]{1,0:T(8,128)(2,1)S(1)}, bf16[512,512]{1,0:T(8,128)(2,1)}, u32[]{:S(2)}) copy-start(bf16[512,512]{1,0:T(8,128)(2,1)} %wout_ref.3) | copy-start | bytes 1572868
  13.6 15.7 %copy-start.7 = (f32[512]{0:T(512)S(1)}, f32[512]{0:T(512)}, u32[]{:S(2)}) copy-start(f32[512]{0:T(512)} %param.11) | copy-start | bytes 6148
  15.9 13.4 %copy-start.2 = (bf16[512,1536]{1,0:T(8,128)(2,1)S(1)}, bf16[512,1536]{1,0:T(8,128)(2,1)}, u32[]{:S(2)}) copy-start(bf16[512,1536]{1,0:T(8,128)(2,1)} %wqkv_ref.3) | copy-start | bytes 4718596
  18.4 16.1 %collective-permute-start.9 = (bf16[64,2048]{1,0:T(8,128)(2,1)S(1)}, bf16[64,2048]{1,0:T(8,128)(2,1)S(1)}, u32[]{:S(2)}, u32[]{:S(2)}) collective-permute-start(bf16[64,2048]{1,0:T(8,128)(2,1)S(1)} %constant_dynamic-update-slice_fusion.2.refs_5_), channel_id=1, source_target_pairs={{0,14},{1,15},{2,0},{3,1},{4,2},{5,3},{6,4},{7,5},{8,6},{9,7},{10,... | collective-permute-start | bytes 786440 | tf_op jit(solution)/shard_map/ppermute | solution.py:316
  21.5 12.9 %collective-permute-start.8 = (bf16[64,2048]{1,0:T(8,128)(2,1)S(1)}, bf16[64,2048]{1,0:T(8,128)(2,1)S(1)}, u32[]{:S(2)}, u32[]{:S(2)}) collective-permute-start(bf16[64,2048]{1,0:T(8,128)(2,1)S(1)} %constant_dynamic-update-slice_fusion.refs_2_), channel_id=1, source_target_pairs={{0,2},{1,3},{2,4},{3,5},{4,6},{5,7},{6,8},{7,9},{8,10},{9,11},{10,... | collective-permute-start | bytes 786440 | tf_op jit(solution)/shard_map/ppermute | solution.py:316
  21.7 12.8 %collective-permute-start.6 = (bf16[2,72,512]{2,1,0:T(8,128)(2,1)S(1)}, bf16[2,72,512]{2,1,0:T(8,128)(2,1)S(1)}, u32[]{:S(2)}, u32[]{:S(2)}) collective-permute-start(bf16[2,72,512]{2,1,0:T(8,128)(2,1)S(1)} %pad_maximum_fusion), channel_id=1, source_target_pairs={{0,32},{32,64},{64,96},{96,128},{128,160},{160,192},{192,224},{1,3... | collective-permute-start | bytes 442376 | tf_op jit(solution)/shard_map/ppermute | solution.py:335
  24.9 9.6 %collective-permute-start.7 = (bf16[2,72,512]{2,1,0:T(8,128)(2,1)S(1)}, bf16[2,72,512]{2,1,0:T(8,128)(2,1)S(1)}, u32[]{:S(2)}, u32[]{:S(2)}) collective-permute-start(bf16[2,72,512]{2,1,0:T(8,128)(2,1)S(1)} %pad_maximum_fusion.1), channel_id=1, source_target_pairs={{32,0},{64,32},{96,64},{128,96},{160,128},{192,160},{224,192},{33,... | collective-permute-start | bytes 442376 | tf_op jit(solution)/shard_map/ppermute | solution.py:336
  29.3 3.1 %copy-start = (bf16[512,2048]{1,0:T(8,128)(2,1)S(1)}, bf16[512,2048]{1,0:T(8,128)(2,1)}, u32[]{:S(2)}) copy-start(bf16[512,2048]{1,0:T(8,128)(2,1)} %up_ref.3) | copy-start | bytes 6291460
  29.3 3.1 %copy-start.1 = (bf16[2048,512]{1,0:T(8,128)(2,1)S(1)}, bf16[2048,512]{1,0:T(8,128)(2,1)}, u32[]{:S(2)}) copy-start(bf16[2048,512]{1,0:T(8,128)(2,1)} %down_ref.3) | copy-start | bytes 6291460
  29.3 3.1 %copy-start.8 = (f32[512]{0:T(512)S(1)}, f32[512]{0:T(512)}, u32[]{:S(2)}) copy-start(f32[512]{0:T(512)} %param.15) | copy-start | bytes 6148
  34.5 13.7 %collective-permute-start.12 = (bf16[64,2048]{1,0:T(8,128)(2,1)S(1)}, bf16[64,2048]{1,0:T(8,128)(2,1)S(1)}, u32[]{:S(2)}, u32[]{:S(2)}) collective-permute-start(bf16[64,2048]{1,0:T(8,128)(2,1)S(1)} %collective-permute-done.8.refs_3_), channel_id=1, source_target_pairs={{0,2},{1,3},{2,4},{3,5},{4,6},{5,7},{6,8},{7,9},{8,10},{9,11},{10,... | collective-permute-start | bytes 786440 | tf_op jit(solution)/shard_map/ppermute | solution.py:316
  34.6 13.7 %collective-permute-start.13 = (bf16[64,2048]{1,0:T(8,128)(2,1)S(1)}, bf16[64,2048]{1,0:T(8,128)(2,1)S(1)}, u32[]{:S(2)}, u32[]{:S(2)}) collective-permute-start(bf16[64,2048]{1,0:T(8,128)(2,1)S(1)} %collective-permute-done.9.refs_6_), channel_id=1, source_target_pairs={{0,14},{1,15},{2,0},{3,1},{4,2},{5,3},{6,4},{7,5},{8,6},{9,7},{10,... | collective-permute-start | bytes 786440 | tf_op jit(solution)/shard_map/ppermute | solution.py:316
  37.9 9.8 %collective-permute-start.11 = (bf16[32,2048]{1,0:T(8,128)(2,1)S(1)}, bf16[32,2048]{1,0:T(8,128)(2,1)S(1)}, u32[]{:S(2)}, u32[]{:S(2)}) collective-permute-start(bf16[32,2048]{1,0:T(8,128)(2,1)S(1)} %slice.23), channel_id=1, source_target_pairs={{0,12},{1,13},{2,14},{3,15},{4,0},{5,1},{6,2},{7,3},{8,4},{9,5},{1... | collective-permute-start | bytes 393224 | tf_op jit(solution)/shard_map/ppermute | solution.py:316
  39.4 8.9 %collective-permute-start.10 = (bf16[32,2048]{1,0:T(8,128)(2,1)S(1)}, bf16[32,2048]{1,0:T(8,128)(2,1)S(1)}, u32[]{:S(2)}, u32[]{:S(2)}) collective-permute-start(bf16[32,2048]{1,0:T(8,128)(2,1)S(1)} %slice.22), channel_id=1, source_target_pairs={{0,4},{1,5},{2,6},{3,7},{4,8},{5,9},{6,10},{7,11},{8,12},{9,13},{1... | collective-permute-start | bytes 393224 | tf_op jit(solution)/shard_map/ppermute | solution.py:316
  40.9 3.6 %copy-start.9 = (f32[2048]{0:T(1024)S(1)}, f32[2048]{0:T(1024)}, u32[]{:S(2)}) copy-start(f32[2048]{0:T(1024)} %param.18) | copy-start | bytes 24580
  44.5 3.7 %copy-start.6 = (bf16[2048,32]{0,1:T(8,128)(2,1)S(1)}, bf16[2048,32]{0,1:T(8,128)(2,1)}, u32[]{:S(2)}) copy-start(bf16[2048,32]{0,1:T(8,128)(2,1)} %param.19) | copy-start | bytes 393220
  48.2 2.1 %collective-permute-start.14 = (bf16[4,160,512]{2,1,0:T(8,128)(2,1)S(1)}, bf16[4,160,512]{2,1,0:T(8,128)(2,1)S(1)}, u32[]{:S(2)}, u32[]{:S(2)}) collective-permute-start(bf16[4,160,512]{2,1,0:T(8,128)(2,1)S(1)} %edge_mlp.1.joined_ref), channel_id=1, source_target_pairs={{0,1},{1,0},{2,3},{3,2},{4,5},{5,4},{6,7},{7,6},{8,9},{9,8},{10,11... | collective-permute-start | bytes 1966088 | tf_op jit(solution)/shard_map/ppermute | solution.py:354

commit v5 on v4

--- a/solution.py
+++ b/solution.py
@@ -109,11 +109,19 @@
         out[...] = held[...].astype(F32).reshape(BAND, WIDTH).astype(BF)
 
 
-def prepare_kernel(bias_ref, out_ref):
+def prepare_kernel(bias_ref, bias_out, middle_out, edges_out, patches_out):
     perm = bias_permutation()
     for h in range(HEADS):
         parts = split3(bias_ref[h] * LOG2E)
-        out_ref[h] = sum(dot(dot(perm, part).astype(BF), perm, NT) for part in parts)
+        bias_out[h] = sum(dot(dot(perm, part).astype(BF), perm, NT) for part in parts)
+    half, ihalf, place = band_places()
+    for n in range(2):
+        middle_out[n] = one_hot(jnp.where(half == n, 72 + 72 * ihalf + place, -1), BAND)
+    for n in range(4):
+        edges_out[n] = one_hot(jnp.where(2 * half + ihalf == n, place, -1), HALF_WIN)
+    for p in range(4):
+        middle, edge = merge_places(p // 2, p % 2)
+        patches_out[p] = one_hot(jnp.where(middle >= 0, middle, jnp.where(edge >= 0, BAND + edge, -1)), 2 * BAND)
 
 
 def attend_window(q, k, v, bias, kaug, qaug):
@@ -151,11 +159,8 @@
     return (row % HALF_WIN) // 36, row // HALF_WIN, lane
 
 
-def middle_attention_kernel(left_ref, right_ref, ga_ref, wqkv_ref, bias_ref, wout_ref, out_ref):
-    half, ihalf, place = band_places()
-    place = 72 + 72 * ihalf + place
-    x = dot(one_hot(jnp.where(half == 0, place, -1), BAND), left_ref[...])
-    x = x + dot(one_hot(jnp.where(half == 1, place, -1), BAND), right_ref[...])
+def middle_attention_kernel(left_ref, right_ref, perm_ref, ga_ref, wqkv_ref, bias_ref, wout_ref, out_ref):
+    x = dot(perm_ref[0], left_ref[...]) + dot(perm_ref[1], right_ref[...])
     qkv = dot(normalise(x, ga_ref[...]).astype(BF), wqkv_ref[...])
     q = qkv[:, :WIDTH] * (LOG2E * HEAD_DIM**-0.5)
     group, _, lane = group_lanes(WIN)
@@ -179,15 +184,13 @@
 
 
 def edge_attention_kernel(
-    lt_ref, rt_ref, lb_ref, rb_ref, top_ref, bottom_ref, ga_ref, wqkv_ref, bias_ref, wout_ref, out_ref
+    lt_ref, rt_ref, lb_ref, rb_ref, top_ref, bottom_ref, perm_ref, ga_ref, wqkv_ref, bias_ref, wout_ref, out_ref
 ):
     bands = (
         (top_ref[0], lt_ref[...], top_ref[1], rt_ref[...]),
         (lb_ref[...], bottom_ref[0], rb_ref[...], bottom_ref[1]),
     )
-    half, ihalf, place = band_places()
-    perm = [one_hot(jnp.where(2 * half + ihalf == n, place, -1), HALF_WIN) for n in range(4)]
-    x = jnp.concatenate([sum(dot(perm[n], piece) for n, piece in enumerate(band)) for band in bands], axis=0)
+    x = jnp.concatenate([sum(dot(perm_ref[n], piece) for n, piece in enumerate(band)) for band in bands], axis=0)
     normed = normalise(x, ga_ref[...])
     kv = dot(normed.astype(BF), wqkv_ref[:, WIDTH:])
     group, half, lane = group_lanes(WIN)
@@ -216,13 +219,10 @@
     out_ref[...] = (kept + update).astype(BF)
 
 
-def edge_mlp_kernel(x_ref, blk1_ref, gm_ref, up_ref, down_ref, gg_ref, out_ref):
+def edge_mlp_kernel(x_ref, blk1_ref, gm_ref, up_ref, down_ref, gg_ref, patches_ref, out_ref):
     block = feed_forward(x_ref[...].astype(F32), gm_ref[...], up_ref, down_ref).astype(BF)
-    first = blk1_ref[...]
-    patches = []
-    for p in range(4):
-        middle, edge = merge_places(p // 2, p % 2)
-        patches.append(dot(one_hot(middle, BAND), first) + dot(one_hot(edge, BAND), block))
+    blocks = jnp.concatenate([blk1_ref[...], block], axis=0)
+    patches = [dot(patches_ref[p], blocks) for p in range(4)]
     mean = sum(jnp.sum(v, axis=-1, keepdims=True) for v in patches) * (1.0 / (4 * WIDTH))
     centred = [v - mean for v in patches]
     spread = sum(jnp.sum(v * v, axis=-1, keepdims=True) for v in centred) * (1.0 / (4 * WIDTH))
@@ -324,7 +324,13 @@
     own_up, own_down = around(w_own, 1), around(w_own, -1)
     w_pair, pos_bias = barrier((w_pair, pos_bias))
     pair_up, pair_down = around(w_pair, 1), around(w_pair, -1)
-    bias = call(prepare_kernel, shape((HEADS, WIN, WIN), F32), [VMEM], [], "prepare")(pos_bias)
+    made = (
+        shape((HEADS, WIN, WIN), F32),
+        shape((2, BAND, BAND)),
+        shape((4, BAND, HALF_WIN)),
+        shape((4, 4 * MERGE_PAD, 2 * BAND)),
+    )
+    bias, middle_perm, edge_perm, patch_perm = call(prepare_kernel, made, [VMEM], [], "prepare")(pos_bias)
 
     bias, right, own_up, own_down, pair_up, pair_down = barrier((bias, right, own_up, own_down, pair_up, pair_down))
     up, down = [jnp.concatenate([own_up, pair_up], axis=0)], [jnp.concatenate([own_down, pair_down], axis=0)]
@@ -335,8 +341,8 @@
     from_above = lax.ppermute(bottom_rows, "lat", [(i, i + 1) for i in range(lat_count - 1)])
     from_below = lax.ppermute(top_rows, "lat", [(i + 1, i) for i in range(lat_count - 1)])
     ga, gm = norm_attn.reshape(1, WIDTH), norm_mlp.reshape(1, WIDTH)
-    attended1 = call(middle_attention_kernel, shape((BAND, WIDTH)), [VMEM] * 6, [], "middle_attention")(
-        left, right, ga, w_qkv, bias, w_out
+    attended1 = call(middle_attention_kernel, shape((BAND, WIDTH)), [VMEM] * 7, [], "middle_attention")(
+        left, right, middle_perm, ga, w_qkv, bias, w_out
     )
     block1 = call(middle_mlp_kernel, shape((BAND, WIDTH)), [VMEM] * 4, [], "middle_mlp")(attended1, gm, w_up, w_down)
 
@@ -344,11 +350,11 @@
     up.append(around(u, 1))
     down.append(around(d, -1))
     far_up, far_down = around(u[:32], 2), around(d[32:], -2)
-    attended2 = call(edge_attention_kernel, shape((BAND, WIDTH)), [VMEM] * 10, [], "edge_attention")(
-        top_rows[0], top_rows[1], bottom_rows[0], bottom_rows[1], from_above, from_below, ga, w_qkv, bias, w_out
-    )
-    joined = call(edge_mlp_kernel, shape((4, 4 * MERGE_PAD, WIDTH)), [VMEM] * 6, [], "edge_mlp")(
-        attended2, block1, gm, w_up, w_down, norm_merge.reshape(4, 1, WIDTH)
+    attended2 = call(edge_attention_kernel, shape((BAND, WIDTH)), [VMEM] * 11, [], "edge_attention")(
+        top_rows[0], top_rows[1], bottom_rows[0], bottom_rows[1], from_above, from_below, edge_perm, ga, w_qkv, bias, w_out
+    )
+    joined = call(edge_mlp_kernel, shape((4, 4 * MERGE_PAD, WIDTH)), [VMEM] * 7, [], "edge_mlp")(
+        attended2, block1, gm, w_up, w_down, norm_merge.reshape(4, 1, WIDTH), patch_perm
     )
     joined, far_up, far_down, up[-1], down[-1] = barrier((joined, far_up, far_down, up[-1], down[-1]))
     neighbour = lax.ppermute(joined, "lon", [(i, i ^ 1) for i in range(lon_count)])

time: 69.2 us -> 68.7 us (level)
  transfers between devices with their start and end apart: 15 -> 15, of which waited for: 5 -> 4; matrix products, arithmetic and copies ran while one was open for 0% -> 0% of each run, Pallas kernels for 23% -> 23%
where the time goes in v5:
time: 68.7 us; the launch traced here: 68 us
  starting transfers between devices  27.7 us (40%)
  Pallas kernels  17.6 us (26%)
  blocking collectives  16 us (23%)
  waiting for transfers between devices  3.48 us (5%)
  local copies, waits for them, and re-layouts  2.87 us (4%)
    all_to_all x1, blocking collectives, on_device(): lax.all_to_all(messages, 'lon', 0, 0, tiled=True, axis_index_groups=cores)  16 us
    ppermute x10, starting transfers between devices, around(): return lax.ppermute(block, 'lon', route)  13.6 us
    ppermute x1, starting transfers between devices, on_device(): lax.ppermute(right_own, 'lon', [((i + 1) % lon_count, i) for i in range(l...  5.27 us
    ppermute x1, starting transfers between devices, on_device(): lax.ppermute(top_rows, 'lat', [(i + 1, i) for i in range(lat_count - 1)])  4.35 us
    pallas_call x1, Pallas kernels, on_device(): call(edge_attention_kernel, shape((BAND, WIDTH)), [VMEM] * 11, [], 'edge_...  3.47 us
    ppermute x1, starting transfers between devices, on_device(): lax.ppermute(bottom_rows, 'lat', [(i, i + 1) for i in range(lat_count - 1)])  3.17 us
    pallas_call x1, Pallas kernels, on_device(): call(middle_attention_kernel, shape((BAND, WIDTH)), [VMEM] * 7, [], 'midd...  2.99 us
    pallas_call x1, Pallas kernels, on_device(): call(edge_mlp_kernel, shape((4, 4 * MERGE_PAD, WIDTH)), [VMEM] * 7, [], '...  2.89 us
  transfers between devices with their start and end apart: 15, of which 4 were waited for; matrix products, arithmetic and copies ran while one was open for 0% of the time, Pallas kernels for 23%

profile of v5, /device:TPU:18, one launch (start us, length us, event | category | flops | bytes accessed | tf_op | source)
XLA Modules:
  0.0 68.0 jit_solution(2120034430913864275)
XLA Ops:
  0.0 1.3 %collective-permute-start = (bf16[32,2048]{1,0:T(8,128)(2,1)}, bf16[32,2048]{1,0:T(8,128)(2,1)S(1)}, u32[]{:S(2)}, u32[]{:S(2)}) collective-permute-start(bf16[32,2048]{1,0:T(8,128)(2,1)} %bitcast.15), channel_id=1, source_target_pairs={{0,16},{1,17},{2,18},{3,19},{4,20},{5,21},{6,22},{7,23},{8,24},{9,... | collective-permute-start | bytes 393224 | tf_op jit(solution)/shard_map/ppermute | solution.py:319
  1.3 1.1 %copy-done.5 = bf16[12,12,4,512]{3,2,1,0:T(4,128)(2,1)S(1)} copy-done((bf16[12,12,4,512]{3,2,1,0:T(4,128)(2,1)S(1)}, bf16[12,12,4,512]{3,2,1,0:T(4,128)(2,1)}, u32[]{:S(2)}) %copy-start.5) | copy-done | bytes 589848
  2.3 0.2 split.1
  2.6 5.3 %collective-permute-start.1 = (bf16[288,512]{1,0:T(8,128)(2,1)S(1)}, bf16[288,512]{1,0:T(8,128)(2,1)S(1)}, u32[]{:S(2)}, u32[]{:S(2)}) collective-permute-start(bf16[288,512]{1,0:T(8,128)(2,1)S(1)} %get-tuple-element.32), channel_id=1, source_target_pairs={{1,0},{2,1},{3,2},{4,3},{5,4},{6,5},{7,6},{8,7},{9,8},{10,9},{11,1... | collective-permute-start | bytes 884744 | tf_op jit(solution)/shard_map/ppermute | solution.py:323
  7.8 0.8 %collective-permute-start.3 = (bf16[32,2048]{1,0:T(8,128)(2,1)}, bf16[32,2048]{1,0:T(8,128)(2,1)S(1)}, u32[]{:S(2)}, u32[]{:S(2)}) collective-permute-start(bf16[32,2048]{1,0:T(8,128)(2,1)} %bitcast.16), channel_id=1, source_target_pairs={{0,14},{1,15},{2,0},{3,1},{4,2},{5,3},{6,4},{7,5},{8,6},{9,7},{10,... | collective-permute-start | bytes 393224 | tf_op jit(solution)/shard_map/ppermute | solution.py:316
  8.7 1.2 %collective-permute-start.2 = (bf16[32,2048]{1,0:T(8,128)(2,1)}, bf16[32,2048]{1,0:T(8,128)(2,1)S(1)}, u32[]{:S(2)}, u32[]{:S(2)}) collective-permute-start(bf16[32,2048]{1,0:T(8,128)(2,1)} %bitcast.17), channel_id=1, source_target_pairs={{0,2},{1,3},{2,4},{3,5},{4,6},{5,7},{6,8},{7,9},{8,10},{9,11},{10,... | collective-permute-start | bytes 393224 | tf_op jit(solution)/shard_map/ppermute | solution.py:316
  9.9 0.0 collective-permute-done.refs_1_
  9.9 2.0 %collective-permute-start.5 = (bf16[32,2048]{1,0:T(8,128)(2,1)S(1)}, bf16[32,2048]{1,0:T(8,128)(2,1)S(1)}, u32[]{:S(2)}, u32[]{:S(2)}) collective-permute-start(bf16[32,2048]{1,0:T(8,128)(2,1)S(1)} %collective-permute-done.refs_1_), channel_id=1, source_target_pairs={{0,14},{1,15},{2,0},{3,1},{4,2},{5,3},{6,4},{7,5},{8,6},{9,7},{10,... | collective-permute-start | bytes 393224 | tf_op jit(solution)/shard_map/ppermute | solution.py:316
  11.9 0.0 collective-permute-start.4
  11.9 0.0 copy-start.3
  11.9 1.7 %copy-done.3 = f32[16,144,144]{2,1,0:T(8,128)S(1)} copy-done((f32[16,144,144]{2,1,0:T(8,128)S(1)}, f32[16,144,144]{2,1,0:T(8,128)}, u32[]{:S(2)}) %copy-start.3) | copy-done | bytes 1327128
  13.6 2.8 %prepare.1 = (f32[16,144,144]{2,1,0:T(8,128)S(1)}, bf16[2,288,288]{2,1,0:T(8,128)(2,1)S(1)}, bf16[4,288,72]{2,1,0:T(8,128)(2,1)S(1)}, bf16[4,160,576]{2,1,0:T(8,128)(2,1)S(1)}) custom-call(f32[16,144,144]{2,1,0:T(8,128)S(1)} %copy-done.3), custom_call_target="tpu_custom_call" | custom-call | flops 1048576 | bytes 65536 | tf_op jit(solution)/shard_map/prepare/pallas_call | solution.py:333
  16.5 0.0 collective-permute-done.3
  16.5 0.0 collective-permute-done.2
  16.5 1.2 %collective-permute-done.5 = bf16[32,2048]{1,0:T(8,128)(2,1)S(1)} collective-permute-done((bf16[32,2048]{1,0:T(8,128)(2,1)S(1)}, bf16[32,2048]{1,0:T(8,128)(2,1)S(1)}, u32[]{:S(2)}, u32[]{:S(2)}) %collective-permute-start.5) | collective-permute-done | bytes 131104 | tf_op jit(solution)/shard_map/ppermute | solution.py:316
  17.7 0.7 collective-permute-done.4
  18.4 0.0 collective-permute-done.1.right_ref
  18.4 3.1 %collective-permute-start.9 = (bf16[64,2048]{1,0:T(8,128)(2,1)S(1)}, bf16[64,2048]{1,0:T(8,128)(2,1)S(1)}, u32[]{:S(2)}, u32[]{:S(2)}) collective-permute-start(bf16[64,2048]{1,0:T(8,128)(2,1)S(1)} %constant_dynamic-update-slice_fusion.2.refs_5_), channel_id=1, source_target_pairs={{0,14},{1,15},{2,0},{3,1},{4,2},{5,3},{6,4},{7,5},{8,6},{9,7},{10,... | collective-permute-start | bytes 786440 | tf_op jit(solution)/shard_map/ppermute | solution.py:316
  21.5 0.1 collective-permute-start.8
  21.7 3.2 %collective-permute-start.6 = (bf16[2,72,512]{2,1,0:T(8,128)(2,1)S(1)}, bf16[2,72,512]{2,1,0:T(8,128)(2,1)S(1)}, u32[]{:S(2)}, u32[]{:S(2)}) collective-permute-start(bf16[2,72,512]{2,1,0:T(8,128)(2,1)S(1)} %pad_maximum_fusion), channel_id=1, source_target_pairs={{0,32},{32,64},{64,96},{96,128},{128,160},{160,192},{192,224},{1,3... | collective-permute-start | bytes 442376 | tf_op jit(solution)/shard_map/ppermute | solution.py:341
  24.9 4.4 %collective-permute-start.7 = (bf16[2,72,512]{2,1,0:T(8,128)(2,1)S(1)}, bf16[2,72,512]{2,1,0:T(8,128)(2,1)S(1)}, u32[]{:S(2)}, u32[]{:S(2)}) collective-permute-start(bf16[2,72,512]{2,1,0:T(8,128)(2,1)S(1)} %pad_maximum_fusion.1), channel_id=1, source_target_pairs={{32,0},{64,32},{96,64},{128,96},{160,128},{192,160},{224,192},{33,... | collective-permute-start | bytes 442376 | tf_op jit(solution)/shard_map/ppermute | solution.py:342
  29.2 0.0 copy-done.2
  29.3 0.0 copy-start
  29.3 0.0 copy-start.1
  29.3 0.0 copy-start.9
  29.3 3.0 %middle_attention.1.x_ref = bf16[288,512]{1,0:T(8,128)(2,1)S(1)} custom-call(bf16[288,512]{1,0:T(8,128)(2,1)S(1)} %get-tuple-element.29.left_ref, bf16[288,512]{1,0:T(8,128)(2,1)S(1)} %collective-permute-done.1.right_ref, bf16[2,288,288]{2,1,0:T(8,128)(2,1)S(1)} %get-tuple-element.35.perm_ref, f32[1,512]{1,0:T(1,128)S(1)} %bitcast.20, ...), custom_call_target="tpu_custom_call" | custom-call | flops 1048576 | bytes 65536 | tf_op jit(solution)/shard_map/middle_attention/pallas_call | solution.py:344
  32.3 2.0 %middle_mlp.1.blk1_ref = bf16[288,512]{1,0:T(8,128)(2,1)S(1)} custom-call(bf16[288,512]{1,0:T(8,128)(2,1)S(1)} %middle_attention.1.x_ref, f32[1,512]{1,0:T(1,128)S(1)} %bitcast.23, bf16[512,2048]{1,0:T(8,128)(2,1)S(1)} %copy-done, bf16[2048,512]{1,0:T(8,128)(2,1)S(1)} %copy-done.1), custom_call_target="tpu_custom_call" | custom-call | flops 1048576 | bytes 65536 | tf_op jit(solution)/shard_map/middle_mlp/pallas_call | solution.py:347
  34.3 0.0 collective-permute-done.6.top_ref
  34.4 0.0 collective-permute-done.7.bottom_ref
  34.4 0.0 collective-permute-done.9.refs_6_
  34.4 0.0 collective-permute-done.8.refs_3_
  34.4 0.1 collective-permute-start.12
  34.5 3.3 %collective-permute-start.13 = (bf16[64,2048]{1,0:T(8,128)(2,1)S(1)}, bf16[64,2048]{1,0:T(8,128)(2,1)S(1)}, u32[]{:S(2)}, u32[]{:S(2)}) collective-permute-start(bf16[64,2048]{1,0:T(8,128)(2,1)S(1)} %collective-permute-done.9.refs_6_), channel_id=1, source_target_pairs={{0,14},{1,15},{2,0},{3,1},{4,2},{5,3},{6,4},{7,5},{8,6},{9,7},{10,... | collective-permute-start | bytes 786440 | tf_op jit(solution)/shard_map/ppermute | solution.py:316
  37.8 1.5 %collective-permute-start.11 = (bf16[32,2048]{1,0:T(8,128)(2,1)S(1)}, bf16[32,2048]{1,0:T(8,128)(2,1)S(1)}, u32[]{:S(2)}, u32[]{:S(2)}) collective-permute-start(bf16[32,2048]{1,0:T(8,128)(2,1)S(1)} %slice.23), channel_id=1, source_target_pairs={{0,12},{1,13},{2,14},{3,15},{4,0},{5,1},{6,2},{7,3},{8,4},{9,5},{1... | collective-permute-start | bytes 393224 | tf_op jit(solution)/shard_map/ppermute | solution.py:316
  39.2 1.5 %collective-permute-start.10 = (bf16[32,2048]{1,0:T(8,128)(2,1)S(1)}, bf16[32,2048]{1,0:T(8,128)(2,1)S(1)}, u32[]{:S(2)}, u32[]{:S(2)}) collective-permute-start(bf16[32,2048]{1,0:T(8,128)(2,1)S(1)} %slice.22), channel_id=1, source_target_pairs={{0,4},{1,5},{2,6},{3,7},{4,8},{5,9},{6,10},{7,11},{8,12},{9,13},{1... | collective-permute-start | bytes 393224 | tf_op jit(solution)/shard_map/ppermute | solution.py:316
  40.8 3.5 %edge_attention.1.x_ref = bf16[288,512]{1,0:T(8,128)(2,1)S(1)} custom-call(bf16[72,512]{1,0:T(8,128)(2,1)S(1)} %get-tuple-element.56.lt_ref, bf16[72,512]{1,0:T(8,128)(2,1)S(1)} %get-tuple-element.60.rt_ref, bf16[72,512]{1,0:T(8,128)(2,1)S(1)} %get-tuple-element.55.lb_ref, bf16[72,512]{1,0:T(8,128)(2,1)S(1)} %get-tuple-element.59.rb_ref, ...), custom_call_target="tpu_custom_call" | custom-call | flops 1048576 | bytes 65536 | tf_op jit(solution)/shard_map/edge_attention/pallas_call | solution.py:353
  44.3 0.0 copy-start.6
  44.3 2.9 %edge_mlp.1.joined_ref = bf16[4,160,512]{2,1,0:T(8,128)(2,1)S(1)} custom-call(bf16[288,512]{1,0:T(8,128)(2,1)S(1)} %edge_attention.1.x_ref, bf16[288,512]{1,0:T(8,128)(2,1)S(1)} %middle_mlp.1.blk1_ref, f32[1,512]{1,0:T(1,128)S(1)} %bitcast.24, bf16[512,2048]{1,0:T(8,128)(2,1)S(1)} %copy-done, bf16[2048,512]{1,0:T(8,128)(2,1)S(1)} %copy-done.1, ...), custom_call_target="tpu_custom_call" | custom-call | flops 1048576 | bytes 65536 | tf_op jit(solution)/shard_map/edge_mlp/pallas_call | solution.py:356
  47.2 0.0 collective-permute-done.11.refs_9_
  47.2 0.6 collective-permute-done.10.refs_8_
  47.8 0.0 collective-permute-done.12.refs_4_
  47.8 0.0 collective-permute-done.13.refs_7_
  47.9 0.0 collective-permute-start.14
  47.9 1.1 %merge_own.1.own_ref = f32[16,40,128]{2,1,0:T(8,128)S(1)} custom-call(bf16[4,160,512]{2,1,0:T(8,128)(2,1)S(1)} %edge_mlp.1.joined_ref, bf16[32,2048]{1,0:T(8,128)(2,1)S(1)} %bitcast.18, bf16[32,2048]{1,0:T(8,128)(2,1)S(1)} %collective-permute-done.refs_1_, bf16[64,2048]{1,0:T(8,128)(2,1)S(1)} %constant_dynamic-update-slice_fusion.refs_2_, ...), custom_call_target="tpu_custom_call" | custom-call | flops 1048576 | bytes 65536 | tf_op jit(solution)/shard_map/merge_own/pallas_call | solution.py:362
  49.0 0.9 %collective-permute-done.14.joined_ref = bf16[4,160,512]{2,1,0:T(8,128)(2,1)S(1)} collective-permute-done((bf16[4,160,512]{2,1,0:T(8,128)(2,1)S(1)}, bf16[4,160,512]{2,1,0:T(8,128)(2,1)S(1)}, u32[]{:S(2)}, u32[]{:S(2)}) %collective-permute-start.14) | collective-permute-done | bytes 655392 | tf_op jit(solution)/shard_map/ppermute | solution.py:360
  50.0 1.1 %merge.1 = bf16[16,72,128]{2,1,0:T(8,128)(2,1)S(1)} custom-call(bf16[4,160,512]{2,1,0:T(8,128)(2,1)S(1)} %collective-permute-done.14.joined_ref, f32[16,40,128]{2,1,0:T(8,128)S(1)} %merge_own.1.own_ref, bf16[32,2048]{1,0:T(8,128)(2,1)S(1)} %bitcast.19, bf16[32,2048]{1,0:T(8,128)(2,1)S(1)} %collective-permute-done.refs_1_, ...), custom_call_target="tpu_custom_call" | custom-call | flops 1048576 | bytes 65536 | tf_op jit(solution)/shard_map/merge/pallas_call | solution.py:363
  51.1 16.0 %all_to_all.5.in_ref = bf16[16,72,128]{2,1,0:T(8,128)(2,1)S(1)} all-to-all(bf16[16,72,128]{2,1,0:T(8,128)(2,1)S(1)} %merge.1), channel_id=1, replica_groups={{0,2,4,6,8,10,12,14,16,18,20,22,24,26,28,30},{1,3,5,7,9,11,13,15,17,19,..., dimensions={0} | all-to-all | bytes 589824 | tf_op jit(solution)/shard_map/all_to_all | solution.py:371
  67.1 1.0 %unpack.1 = bf16[6,128,192]{2,1,0:T(8,128)(2,1)} custom-call(bf16[16,72,128]{2,1,0:T(8,128)(2,1)S(1)} %all_to_all.5.in_ref), custom_call_target="tpu_custom_call" | custom-call | flops 1048576 | bytes 65536 | tf_op jit(solution)/shard_map/unpack/pallas_call | solution.py:372
  (22 shorter events, 0.2 us)
Async XLA Ops:
  0.0 9.9 %collective-permute-start = (bf16[32,2048]{1,0:T(8,128)(2,1)}, bf16[32,2048]{1,0:T(8,128)(2,1)S(1)}, u32[]{:S(2)}, u32[]{:S(2)}) collective-permute-start(bf16[32,2048]{1,0:T(8,128)(2,1)} %bitcast.15), channel_id=1, source_target_pairs={{0,16},{1,17},{2,18},{3,19},{4,20},{5,21},{6,22},{7,23},{8,24},{9,... | collective-permute-start | bytes 393224 | tf_op jit(solution)/shard_map/ppermute | solution.py:319
  1.3 1.1 %copy-start.5 = (bf16[12,12,4,512]{3,2,1,0:T(4,128)(2,1)S(1)}, bf16[12,12,4,512]{3,2,1,0:T(4,128)(2,1)}, u32[]{:S(2)}) copy-start(bf16[12,12,4,512]{3,2,1,0:T(4,128)(2,1)} %tokens_hbm.1) | copy-start | bytes 1769476
  2.6 15.8 %collective-permute-start.1 = (bf16[288,512]{1,0:T(8,128)(2,1)S(1)}, bf16[288,512]{1,0:T(8,128)(2,1)S(1)}, u32[]{:S(2)}, u32[]{:S(2)}) collective-permute-start(bf16[288,512]{1,0:T(8,128)(2,1)S(1)} %get-tuple-element.32), channel_id=1, source_target_pairs={{1,0},{2,1},{3,2},{4,3},{5,4},{6,5},{7,6},{8,7},{9,8},{10,9},{11,1... | collective-permute-start | bytes 884744 | tf_op jit(solution)/shard_map/ppermute | solution.py:323
  7.8 8.6 %collective-permute-start.3 = (bf16[32,2048]{1,0:T(8,128)(2,1)}, bf16[32,2048]{1,0:T(8,128)(2,1)S(1)}, u32[]{:S(2)}, u32[]{:S(2)}) collective-permute-start(bf16[32,2048]{1,0:T(8,128)(2,1)} %bitcast.16), channel_id=1, source_target_pairs={{0,14},{1,15},{2,0},{3,1},{4,2},{5,3},{6,4},{7,5},{8,6},{9,7},{10,... | collective-permute-start | bytes 393224 | tf_op jit(solution)/shard_map/ppermute | solution.py:316
  8.7 7.8 %collective-permute-start.2 = (bf16[32,2048]{1,0:T(8,128)(2,1)}, bf16[32,2048]{1,0:T(8,128)(2,1)S(1)}, u32[]{:S(2)}, u32[]{:S(2)}) collective-permute-start(bf16[32,2048]{1,0:T(8,128)(2,1)} %bitcast.17), channel_id=1, source_target_pairs={{0,2},{1,3},{2,4},{3,5},{4,6},{5,7},{6,8},{7,9},{8,10},{9,11},{10,... | collective-permute-start | bytes 393224 | tf_op jit(solution)/shard_map/ppermute | solution.py:316
  9.9 7.8 %collective-permute-start.5 = (bf16[32,2048]{1,0:T(8,128)(2,1)S(1)}, bf16[32,2048]{1,0:T(8,128)(2,1)S(1)}, u32[]{:S(2)}, u32[]{:S(2)}) collective-permute-start(bf16[32,2048]{1,0:T(8,128)(2,1)S(1)} %collective-permute-done.refs_1_), channel_id=1, source_target_pairs={{0,14},{1,15},{2,0},{3,1},{4,2},{5,3},{6,4},{7,5},{8,6},{9,7},{10,... | collective-permute-start | bytes 393224 | tf_op jit(solution)/shard_map/ppermute | solution.py:316
  11.9 6.5 %collective-permute-start.4 = (bf16[32,2048]{1,0:T(8,128)(2,1)S(1)}, bf16[32,2048]{1,0:T(8,128)(2,1)S(1)}, u32[]{:S(2)}, u32[]{:S(2)}) collective-permute-start(bf16[32,2048]{1,0:T(8,128)(2,1)S(1)} %collective-permute-done.refs_1_), channel_id=1, source_target_pairs={{0,2},{1,3},{2,4},{3,5},{4,6},{5,7},{6,8},{7,9},{8,10},{9,11},{10,... | collective-permute-start | bytes 393224 | tf_op jit(solution)/shard_map/ppermute | solution.py:316
  11.9 1.7 %copy-start.3 = (f32[16,144,144]{2,1,0:T(8,128)S(1)}, f32[16,144,144]{2,1,0:T(8,128)}, u32[]{:S(2)}) copy-start(f32[16,144,144]{2,1,0:T(8,128)} %bias_ref) | copy-start | bytes 3981316
  13.6 15.7 %copy-start.2 = (bf16[512,1536]{1,0:T(8,128)(2,1)S(1)}, bf16[512,1536]{1,0:T(8,128)(2,1)}, u32[]{:S(2)}) copy-start(bf16[512,1536]{1,0:T(8,128)(2,1)} %wqkv_ref.3) | copy-start | bytes 4718596
  13.6 15.7 %copy-start.4 = (bf16[512,512]{1,0:T(8,128)(2,1)S(1)}, bf16[512,512]{1,0:T(8,128)(2,1)}, u32[]{:S(2)}) copy-start(bf16[512,512]{1,0:T(8,128)(2,1)} %wout_ref.3) | copy-start | bytes 1572868
  13.6 15.7 %copy-start.7 = (f32[512]{0:T(512)S(1)}, f32[512]{0:T(512)}, u32[]{:S(2)}) copy-start(f32[512]{0:T(512)} %param.11) | copy-start | bytes 6148
  18.4 16.0 %collective-permute-start.9 = (bf16[64,2048]{1,0:T(8,128)(2,1)S(1)}, bf16[64,2048]{1,0:T(8,128)(2,1)S(1)}, u32[]{:S(2)}, u32[]{:S(2)}) collective-permute-start(bf16[64,2048]{1,0:T(8,128)(2,1)S(1)} %constant_dynamic-update-slice_fusion.2.refs_5_), channel_id=1, source_target_pairs={{0,14},{1,15},{2,0},{3,1},{4,2},{5,3},{6,4},{7,5},{8,6},{9,7},{10,... | collective-permute-start | bytes 786440 | tf_op jit(solution)/shard_map/ppermute | solution.py:316
  21.5 12.8 %collective-permute-start.8 = (bf16[64,2048]{1,0:T(8,128)(2,1)S(1)}, bf16[64,2048]{1,0:T(8,128)(2,1)S(1)}, u32[]{:S(2)}, u32[]{:S(2)}) collective-permute-start(bf16[64,2048]{1,0:T(8,128)(2,1)S(1)} %constant_dynamic-update-slice_fusion.refs_2_), channel_id=1, source_target_pairs={{0,2},{1,3},{2,4},{3,5},{4,6},{5,7},{6,8},{7,9},{8,10},{9,11},{10,... | collective-permute-start | bytes 786440 | tf_op jit(solution)/shard_map/ppermute | solution.py:316
  21.7 12.7 %collective-permute-start.6 = (bf16[2,72,512]{2,1,0:T(8,128)(2,1)S(1)}, bf16[2,72,512]{2,1,0:T(8,128)(2,1)S(1)}, u32[]{:S(2)}, u32[]{:S(2)}) collective-permute-start(bf16[2,72,512]{2,1,0:T(8,128)(2,1)S(1)} %pad_maximum_fusion), channel_id=1, source_target_pairs={{0,32},{32,64},{64,96},{96,128},{128,160},{160,192},{192,224},{1,3... | collective-permute-start | bytes 442376 | tf_op jit(solution)/shard_map/ppermute | solution.py:341
  24.9 9.5 %collective-permute-start.7 = (bf16[2,72,512]{2,1,0:T(8,128)(2,1)S(1)}, bf16[2,72,512]{2,1,0:T(8,128)(2,1)S(1)}, u32[]{:S(2)}, u32[]{:S(2)}) collective-permute-start(bf16[2,72,512]{2,1,0:T(8,128)(2,1)S(1)} %pad_maximum_fusion.1), channel_id=1, source_target_pairs={{32,0},{64,32},{96,64},{128,96},{160,128},{192,160},{224,192},{33,... | collective-permute-start | bytes 442376 | tf_op jit(solution)/shard_map/ppermute | solution.py:342
  29.3 3.0 %copy-start = (bf16[512,2048]{1,0:T(8,128)(2,1)S(1)}, bf16[512,2048]{1,0:T(8,128)(2,1)}, u32[]{:S(2)}) copy-start(bf16[512,2048]{1,0:T(8,128)(2,1)} %up_ref.3) | copy-start | bytes 6291460
  29.3 3.0 %copy-start.1 = (bf16[2048,512]{1,0:T(8,128)(2,1)S(1)}, bf16[2048,512]{1,0:T(8,128)(2,1)}, u32[]{:S(2)}) copy-start(bf16[2048,512]{1,0:T(8,128)(2,1)} %down_ref.3) | copy-start | bytes 6291460
  29.3 3.0 %copy-start.9 = (f32[512]{0:T(512)S(1)}, f32[512]{0:T(512)}, u32[]{:S(2)}) copy-start(f32[512]{0:T(512)} %param.15) | copy-start | bytes 6148
  34.4 13.5 %collective-permute-start.12 = (bf16[64,2048]{1,0:T(8,128)(2,1)S(1)}, bf16[64,2048]{1,0:T(8,128)(2,1)S(1)}, u32[]{:S(2)}, u32[]{:S(2)}) collective-permute-start(bf16[64,2048]{1,0:T(8,128)(2,1)S(1)} %collective-permute-done.8.refs_3_), channel_id=1, source_target_pairs={{0,2},{1,3},{2,4},{3,5},{4,6},{5,7},{6,8},{7,9},{8,10},{9,11},{10,... | collective-permute-start | bytes 786440 | tf_op jit(solution)/shard_map/ppermute | solution.py:316
  34.5 13.4 %collective-permute-start.13 = (bf16[64,2048]{1,0:T(8,128)(2,1)S(1)}, bf16[64,2048]{1,0:T(8,128)(2,1)S(1)}, u32[]{:S(2)}, u32[]{:S(2)}) collective-permute-start(bf16[64,2048]{1,0:T(8,128)(2,1)S(1)} %collective-permute-done.9.refs_6_), channel_id=1, source_target_pairs={{0,14},{1,15},{2,0},{3,1},{4,2},{5,3},{6,4},{7,5},{8,6},{9,7},{10,... | collective-permute-start | bytes 786440 | tf_op jit(solution)/shard_map/ppermute | solution.py:316
  37.8 9.4 %collective-permute-start.11 = (bf16[32,2048]{1,0:T(8,128)(2,1)S(1)}, bf16[32,2048]{1,0:T(8,128)(2,1)S(1)}, u32[]{:S(2)}, u32[]{:S(2)}) collective-permute-start(bf16[32,2048]{1,0:T(8,128)(2,1)S(1)} %slice.23), channel_id=1, source_target_pairs={{0,12},{1,13},{2,14},{3,15},{4,0},{5,1},{6,2},{7,3},{8,4},{9,5},{1... | collective-permute-start | bytes 393224 | tf_op jit(solution)/shard_map/ppermute | solution.py:316
  39.2 8.6 %collective-permute-start.10 = (bf16[32,2048]{1,0:T(8,128)(2,1)S(1)}, bf16[32,2048]{1,0:T(8,128)(2,1)S(1)}, u32[]{:S(2)}, u32[]{:S(2)}) collective-permute-start(bf16[32,2048]{1,0:T(8,128)(2,1)S(1)} %slice.22), channel_id=1, source_target_pairs={{0,4},{1,5},{2,6},{3,7},{4,8},{5,9},{6,10},{7,11},{8,12},{9,13},{1... | collective-permute-start | bytes 393224 | tf_op jit(solution)/shard_map/ppermute | solution.py:316
  40.8 3.5 %copy-start.8 = (f32[2048]{0:T(1024)S(1)}, f32[2048]{0:T(1024)}, u32[]{:S(2)}) copy-start(f32[2048]{0:T(1024)} %param.18) | copy-start | bytes 24580
  44.3 3.6 %copy-start.6 = (bf16[2048,32]{0,1:T(8,128)(2,1)S(1)}, bf16[2048,32]{0,1:T(8,128)(2,1)}, u32[]{:S(2)}) copy-start(bf16[2048,32]{0,1:T(8,128)(2,1)} %param.19) | copy-start | bytes 393220
  47.9 2.1 %collective-permute-start.14 = (bf16[4,160,512]{2,1,0:T(8,128)(2,1)S(1)}, bf16[4,160,512]{2,1,0:T(8,128)(2,1)S(1)}, u32[]{:S(2)}, u32[]{:S(2)}) collective-permute-start(bf16[4,160,512]{2,1,0:T(8,128)(2,1)S(1)} %edge_mlp.1.joined_ref), channel_id=1, source_target_pairs={{0,1},{1,0},{2,3},{3,2},{4,5},{5,4},{6,7},{7,6},{8,9},{9,8},{10,11... | collective-permute-start | bytes 1966088 | tf_op jit(solution)/shard_map/ppermute | solution.py:360

commit v6 on v5

--- a/solution.py
+++ b/solution.py
@@ -145,7 +145,7 @@
 def feed_forward(attended, norm_mlp, up_ref, down_ref):
     normed = normalise(attended, norm_mlp).astype(BF)
     acc = attended
-    step = 512
+    step = 1024
     for c in range(0, FFN, step):
         h = dot(normed, up_ref[:, c : c + step])
         h = 0.5 * h * (1.0 + lax.erf(h * 0.7071067811865476))

time: 68.7 us -> 68.6 us (level)
  Pallas kernels: 17.6 us -> 16.9 us
  transfers between devices with their start and end apart: 15 -> 15, of which waited for: 4 -> 5; matrix products, arithmetic and copies ran while one was open for 0% -> 0% of each run, Pallas kernels for 23% -> 22%
where the time goes in v6:
time: 68.6 us; the launch traced here: 67.7 us
  starting transfers between devices  27.6 us (40%)
  Pallas kernels  16.9 us (25%)
  blocking collectives  16 us (23%)
  waiting for transfers between devices  3.91 us (6%)
  local copies, waits for them, and re-layouts  2.87 us (4%)
    all_to_all x1, blocking collectives, on_device(): lax.all_to_all(messages, 'lon', 0, 0, tiled=True, axis_index_groups=cores)  16 us
    ppermute x10, starting transfers between devices, around(): return lax.ppermute(block, 'lon', route)  13.6 us
    ppermute x1, starting transfers between devices, on_device(): lax.ppermute(right_own, 'lon', [((i + 1) % lon_count, i) for i in range(l...  5.27 us
    ppermute x1, starting transfers between devices, on_device(): lax.ppermute(top_rows, 'lat', [(i + 1, i) for i in range(lat_count - 1)])  4.35 us
    pallas_call x1, Pallas kernels, on_device(): call(edge_attention_kernel, shape((BAND, WIDTH)), [VMEM] * 11, [], 'edge_...  3.48 us
    ppermute x1, starting transfers between devices, on_device(): lax.ppermute(bottom_rows, 'lat', [(i, i + 1) for i in range(lat_count - 1)])  3.17 us
    pallas_call x1, Pallas kernels, on_device(): call(middle_attention_kernel, shape((BAND, WIDTH)), [VMEM] * 7, [], 'midd...  2.99 us
    pallas_call x1, Pallas kernels, on_device(): call(prepare_kernel, made, [VMEM], [], 'prepare')(pos_bias)  2.85 us
  transfers between devices with their start and end apart: 15, of which 5 were waited for; matrix products, arithmetic and copies ran while one was open for 0% of the time, Pallas kernels for 22%

profile of v6, /device:TPU:18, one launch (start us, length us, event | category | flops | bytes accessed | tf_op | source)
XLA Modules:
  0.0 67.7 jit_solution(10708380310047691002)
XLA Ops:
  0.0 1.3 %collective-permute-start = (bf16[32,2048]{1,0:T(8,128)(2,1)}, bf16[32,2048]{1,0:T(8,128)(2,1)S(1)}, u32[]{:S(2)}, u32[]{:S(2)}) collective-permute-start(bf16[32,2048]{1,0:T(8,128)(2,1)} %bitcast.15), channel_id=1, source_target_pairs={{0,16},{1,17},{2,18},{3,19},{4,20},{5,21},{6,22},{7,23},{8,24},{9,... | collective-permute-start | bytes 393224 | tf_op jit(solution)/shard_map/ppermute | solution.py:319
  1.3 1.1 %copy-done.5 = bf16[12,12,4,512]{3,2,1,0:T(4,128)(2,1)S(1)} copy-done((bf16[12,12,4,512]{3,2,1,0:T(4,128)(2,1)S(1)}, bf16[12,12,4,512]{3,2,1,0:T(4,128)(2,1)}, u32[]{:S(2)}) %copy-start.5) | copy-done | bytes 589848
  2.3 0.2 split.1
  2.6 5.3 %collective-permute-start.1 = (bf16[288,512]{1,0:T(8,128)(2,1)S(1)}, bf16[288,512]{1,0:T(8,128)(2,1)S(1)}, u32[]{:S(2)}, u32[]{:S(2)}) collective-permute-start(bf16[288,512]{1,0:T(8,128)(2,1)S(1)} %get-tuple-element.32), channel_id=1, source_target_pairs={{1,0},{2,1},{3,2},{4,3},{5,4},{6,5},{7,6},{8,7},{9,8},{10,9},{11,1... | collective-permute-start | bytes 884744 | tf_op jit(solution)/shard_map/ppermute | solution.py:323
  7.8 0.8 %collective-permute-start.3 = (bf16[32,2048]{1,0:T(8,128)(2,1)}, bf16[32,2048]{1,0:T(8,128)(2,1)S(1)}, u32[]{:S(2)}, u32[]{:S(2)}) collective-permute-start(bf16[32,2048]{1,0:T(8,128)(2,1)} %bitcast.16), channel_id=1, source_target_pairs={{0,14},{1,15},{2,0},{3,1},{4,2},{5,3},{6,4},{7,5},{8,6},{9,7},{10,... | collective-permute-start | bytes 393224 | tf_op jit(solution)/shard_map/ppermute | solution.py:316
  8.7 1.2 %collective-permute-start.2 = (bf16[32,2048]{1,0:T(8,128)(2,1)}, bf16[32,2048]{1,0:T(8,128)(2,1)S(1)}, u32[]{:S(2)}, u32[]{:S(2)}) collective-permute-start(bf16[32,2048]{1,0:T(8,128)(2,1)} %bitcast.17), channel_id=1, source_target_pairs={{0,2},{1,3},{2,4},{3,5},{4,6},{5,7},{6,8},{7,9},{8,10},{9,11},{10,... | collective-permute-start | bytes 393224 | tf_op jit(solution)/shard_map/ppermute | solution.py:316
  9.9 0.0 collective-permute-done.refs_1_
  9.9 2.0 %collective-permute-start.5 = (bf16[32,2048]{1,0:T(8,128)(2,1)S(1)}, bf16[32,2048]{1,0:T(8,128)(2,1)S(1)}, u32[]{:S(2)}, u32[]{:S(2)}) collective-permute-start(bf16[32,2048]{1,0:T(8,128)(2,1)S(1)} %collective-permute-done.refs_1_), channel_id=1, source_target_pairs={{0,14},{1,15},{2,0},{3,1},{4,2},{5,3},{6,4},{7,5},{8,6},{9,7},{10,... | collective-permute-start | bytes 393224 | tf_op jit(solution)/shard_map/ppermute | solution.py:316
  11.9 0.0 collective-permute-start.4
  11.9 0.0 copy-start.3
  11.9 1.7 %copy-done.3 = f32[16,144,144]{2,1,0:T(8,128)S(1)} copy-done((f32[16,144,144]{2,1,0:T(8,128)S(1)}, f32[16,144,144]{2,1,0:T(8,128)}, u32[]{:S(2)}) %copy-start.3) | copy-done | bytes 1327128
  13.6 2.8 %prepare.1 = (f32[16,144,144]{2,1,0:T(8,128)S(1)}, bf16[2,288,288]{2,1,0:T(8,128)(2,1)S(1)}, bf16[4,288,72]{2,1,0:T(8,128)(2,1)S(1)}, bf16[4,160,576]{2,1,0:T(8,128)(2,1)S(1)}) custom-call(f32[16,144,144]{2,1,0:T(8,128)S(1)} %copy-done.3), custom_call_target="tpu_custom_call" | custom-call | flops 1048576 | bytes 65536 | tf_op jit(solution)/shard_map/prepare/pallas_call | solution.py:333
  16.5 0.0 collective-permute-done.3
  16.5 0.0 collective-permute-done.2
  16.5 1.2 %collective-permute-done.5 = bf16[32,2048]{1,0:T(8,128)(2,1)S(1)} collective-permute-done((bf16[32,2048]{1,0:T(8,128)(2,1)S(1)}, bf16[32,2048]{1,0:T(8,128)(2,1)S(1)}, u32[]{:S(2)}, u32[]{:S(2)}) %collective-permute-start.5) | collective-permute-done | bytes 131104 | tf_op jit(solution)/shard_map/ppermute | solution.py:316
  17.7 0.7 collective-permute-done.4
  18.4 0.0 collective-permute-done.1.right_ref
  18.4 3.1 %collective-permute-start.9 = (bf16[64,2048]{1,0:T(8,128)(2,1)S(1)}, bf16[64,2048]{1,0:T(8,128)(2,1)S(1)}, u32[]{:S(2)}, u32[]{:S(2)}) collective-permute-start(bf16[64,2048]{1,0:T(8,128)(2,1)S(1)} %constant_dynamic-update-slice_fusion.2.refs_5_), channel_id=1, source_target_pairs={{0,14},{1,15},{2,0},{3,1},{4,2},{5,3},{6,4},{7,5},{8,6},{9,7},{10,... | collective-permute-start | bytes 786440 | tf_op jit(solution)/shard_map/ppermute | solution.py:316
  21.5 0.1 collective-permute-start.8
  21.7 3.2 %collective-permute-start.6 = (bf16[2,72,512]{2,1,0:T(8,128)(2,1)S(1)}, bf16[2,72,512]{2,1,0:T(8,128)(2,1)S(1)}, u32[]{:S(2)}, u32[]{:S(2)}) collective-permute-start(bf16[2,72,512]{2,1,0:T(8,128)(2,1)S(1)} %pad_maximum_fusion), channel_id=1, source_target_pairs={{0,32},{32,64},{64,96},{96,128},{128,160},{160,192},{192,224},{1,3... | collective-permute-start | bytes 442376 | tf_op jit(solution)/shard_map/ppermute | solution.py:341
  24.9 4.4 %collective-permute-start.7 = (bf16[2,72,512]{2,1,0:T(8,128)(2,1)S(1)}, bf16[2,72,512]{2,1,0:T(8,128)(2,1)S(1)}, u32[]{:S(2)}, u32[]{:S(2)}) collective-permute-start(bf16[2,72,512]{2,1,0:T(8,128)(2,1)S(1)} %pad_maximum_fusion.1), channel_id=1, source_target_pairs={{32,0},{64,32},{96,64},{128,96},{160,128},{192,160},{224,192},{33,... | collective-permute-start | bytes 442376 | tf_op jit(solution)/shard_map/ppermute | solution.py:342
  29.2 0.0 copy-done.2
  29.3 0.0 copy-start
  29.3 0.0 copy-start.1
  29.3 0.0 copy-start.9
  29.3 3.0 %middle_attention.1.x_ref = bf16[288,512]{1,0:T(8,128)(2,1)S(1)} custom-call(bf16[288,512]{1,0:T(8,128)(2,1)S(1)} %get-tuple-element.29.left_ref, bf16[288,512]{1,0:T(8,128)(2,1)S(1)} %collective-permute-done.1.right_ref, bf16[2,288,288]{2,1,0:T(8,128)(2,1)S(1)} %get-tuple-element.35.perm_ref, f32[1,512]{1,0:T(1,128)S(1)} %bitcast.20, ...), custom_call_target="tpu_custom_call" | custom-call | flops 1048576 | bytes 65536 | tf_op jit(solution)/shard_map/middle_attention/pallas_call | solution.py:344
  32.3 1.6 %middle_mlp.1.blk1_ref = bf16[288,512]{1,0:T(8,128)(2,1)S(1)} custom-call(bf16[288,512]{1,0:T(8,128)(2,1)S(1)} %middle_attention.1.x_ref, f32[1,512]{1,0:T(1,128)S(1)} %bitcast.23, bf16[512,2048]{1,0:T(8,128)(2,1)S(1)} %copy-done, bf16[2048,512]{1,0:T(8,128)(2,1)S(1)} %copy-done.1), custom_call_target="tpu_custom_call" | custom-call | flops 1048576 | bytes 65536 | tf_op jit(solution)/shard_map/middle_mlp/pallas_call | solution.py:347
  34.0 0.0 collective-permute-done.6.top_ref
  34.0 0.3 collective-permute-done.7.bottom_ref
  34.3 0.0 collective-permute-done.9.refs_6_
  34.3 0.0 collective-permute-done.8.refs_3_
  34.3 0.0 collective-permute-start.12
  34.3 3.3 %collective-permute-start.13 = (bf16[64,2048]{1,0:T(8,128)(2,1)S(1)}, bf16[64,2048]{1,0:T(8,128)(2,1)S(1)}, u32[]{:S(2)}, u32[]{:S(2)}) collective-permute-start(bf16[64,2048]{1,0:T(8,128)(2,1)S(1)} %collective-permute-done.9.refs_6_), channel_id=1, source_target_pairs={{0,14},{1,15},{2,0},{3,1},{4,2},{5,3},{6,4},{7,5},{8,6},{9,7},{10,... | collective-permute-start | bytes 786440 | tf_op jit(solution)/shard_map/ppermute | solution.py:316
  37.7 1.5 %collective-permute-start.11 = (bf16[32,2048]{1,0:T(8,128)(2,1)S(1)}, bf16[32,2048]{1,0:T(8,128)(2,1)S(1)}, u32[]{:S(2)}, u32[]{:S(2)}) collective-permute-start(bf16[32,2048]{1,0:T(8,128)(2,1)S(1)} %slice.23), channel_id=1, source_target_pairs={{0,12},{1,13},{2,14},{3,15},{4,0},{5,1},{6,2},{7,3},{8,4},{9,5},{1... | collective-permute-start | bytes 393224 | tf_op jit(solution)/shard_map/ppermute | solution.py:316
  39.1 1.5 %collective-permute-start.10 = (bf16[32,2048]{1,0:T(8,128)(2,1)S(1)}, bf16[32,2048]{1,0:T(8,128)(2,1)S(1)}, u32[]{:S(2)}, u32[]{:S(2)}) collective-permute-start(bf16[32,2048]{1,0:T(8,128)(2,1)S(1)} %slice.22), channel_id=1, source_target_pairs={{0,4},{1,5},{2,6},{3,7},{4,8},{5,9},{6,10},{7,11},{8,12},{9,13},{1... | collective-permute-start | bytes 393224 | tf_op jit(solution)/shard_map/ppermute | solution.py:316
  40.7 3.5 %edge_attention.1.x_ref = bf16[288,512]{1,0:T(8,128)(2,1)S(1)} custom-call(bf16[72,512]{1,0:T(8,128)(2,1)S(1)} %get-tuple-element.56.lt_ref, bf16[72,512]{1,0:T(8,128)(2,1)S(1)} %get-tuple-element.60.rt_ref, bf16[72,512]{1,0:T(8,128)(2,1)S(1)} %get-tuple-element.55.lb_ref, bf16[72,512]{1,0:T(8,128)(2,1)S(1)} %get-tuple-element.59.rb_ref, ...), custom_call_target="tpu_custom_call" | custom-call | flops 1048576 | bytes 65536 | tf_op jit(solution)/shard_map/edge_attention/pallas_call | solution.py:353
  44.2 0.0 copy-start.6
  44.2 2.5 %edge_mlp.1.joined_ref = bf16[4,160,512]{2,1,0:T(8,128)(2,1)S(1)} custom-call(bf16[288,512]{1,0:T(8,128)(2,1)S(1)} %edge_attention.1.x_ref, bf16[288,512]{1,0:T(8,128)(2,1)S(1)} %middle_mlp.1.blk1_ref, f32[1,512]{1,0:T(1,128)S(1)} %bitcast.24, bf16[512,2048]{1,0:T(8,128)(2,1)S(1)} %copy-done, bf16[2048,512]{1,0:T(8,128)(2,1)S(1)} %copy-done.1, ...), custom_call_target="tpu_custom_call" | custom-call | flops 1048576 | bytes 65536 | tf_op jit(solution)/shard_map/edge_mlp/pallas_call | solution.py:356
  46.7 0.0 collective-permute-done.11.refs_9_
  46.7 0.7 %collective-permute-done.10.refs_8_ = bf16[32,2048]{1,0:T(8,128)(2,1)S(1)} collective-permute-done((bf16[32,2048]{1,0:T(8,128)(2,1)S(1)}, bf16[32,2048]{1,0:T(8,128)(2,1)S(1)}, u32[]{:S(2)}, u32[]{:S(2)}) %collective-permute-start.10) | collective-permute-done | bytes 131104 | tf_op jit(solution)/shard_map/ppermute | solution.py:316
  47.5 0.0 collective-permute-done.12.refs_4_
  47.5 0.0 collective-permute-done.13.refs_7_
  47.5 0.0 collective-permute-start.14
  47.5 1.1 %merge_own.1.own_ref = f32[16,40,128]{2,1,0:T(8,128)S(1)} custom-call(bf16[4,160,512]{2,1,0:T(8,128)(2,1)S(1)} %edge_mlp.1.joined_ref, bf16[32,2048]{1,0:T(8,128)(2,1)S(1)} %bitcast.18, bf16[32,2048]{1,0:T(8,128)(2,1)S(1)} %collective-permute-done.refs_1_, bf16[64,2048]{1,0:T(8,128)(2,1)S(1)} %constant_dynamic-update-slice_fusion.refs_2_, ...), custom_call_target="tpu_custom_call" | custom-call | flops 1048576 | bytes 65536 | tf_op jit(solution)/shard_map/merge_own/pallas_call | solution.py:362
  48.6 0.9 %collective-permute-done.14.joined_ref = bf16[4,160,512]{2,1,0:T(8,128)(2,1)S(1)} collective-permute-done((bf16[4,160,512]{2,1,0:T(8,128)(2,1)S(1)}, bf16[4,160,512]{2,1,0:T(8,128)(2,1)S(1)}, u32[]{:S(2)}, u32[]{:S(2)}) %collective-permute-start.14) | collective-permute-done | bytes 655392 | tf_op jit(solution)/shard_map/ppermute | solution.py:360
  49.6 1.1 %merge.1 = bf16[16,72,128]{2,1,0:T(8,128)(2,1)S(1)} custom-call(bf16[4,160,512]{2,1,0:T(8,128)(2,1)S(1)} %collective-permute-done.14.joined_ref, f32[16,40,128]{2,1,0:T(8,128)S(1)} %merge_own.1.own_ref, bf16[32,2048]{1,0:T(8,128)(2,1)S(1)} %bitcast.19, bf16[32,2048]{1,0:T(8,128)(2,1)S(1)} %collective-permute-done.refs_1_, ...), custom_call_target="tpu_custom_call" | custom-call | flops 1048576 | bytes 65536 | tf_op jit(solution)/shard_map/merge/pallas_call | solution.py:363
  50.7 16.0 %all_to_all.5.in_ref = bf16[16,72,128]{2,1,0:T(8,128)(2,1)S(1)} all-to-all(bf16[16,72,128]{2,1,0:T(8,128)(2,1)S(1)} %merge.1), channel_id=1, replica_groups={{0,2,4,6,8,10,12,14,16,18,20,22,24,26,28,30},{1,3,5,7,9,11,13,15,17,19,..., dimensions={0} | all-to-all | bytes 589824 | tf_op jit(solution)/shard_map/all_to_all | solution.py:371
  66.7 1.0 %unpack.1 = bf16[6,128,192]{2,1,0:T(8,128)(2,1)} custom-call(bf16[16,72,128]{2,1,0:T(8,128)(2,1)S(1)} %all_to_all.5.in_ref), custom_call_target="tpu_custom_call" | custom-call | flops 1048576 | bytes 65536 | tf_op jit(solution)/shard_map/unpack/pallas_call | solution.py:372
  (22 shorter events, 0.2 us)
Async XLA Ops:
  0.0 9.9 %collective-permute-start = (bf16[32,2048]{1,0:T(8,128)(2,1)}, bf16[32,2048]{1,0:T(8,128)(2,1)S(1)}, u32[]{:S(2)}, u32[]{:S(2)}) collective-permute-start(bf16[32,2048]{1,0:T(8,128)(2,1)} %bitcast.15), channel_id=1, source_target_pairs={{0,16},{1,17},{2,18},{3,19},{4,20},{5,21},{6,22},{7,23},{8,24},{9,... | collective-permute-start | bytes 393224 | tf_op jit(solution)/shard_map/ppermute | solution.py:319
  1.3 1.1 %copy-start.5 = (bf16[12,12,4,512]{3,2,1,0:T(4,128)(2,1)S(1)}, bf16[12,12,4,512]{3,2,1,0:T(4,128)(2,1)}, u32[]{:S(2)}) copy-start(bf16[12,12,4,512]{3,2,1,0:T(4,128)(2,1)} %tokens_hbm.1) | copy-start | bytes 1769476
  2.6 15.8 %collective-permute-start.1 = (bf16[288,512]{1,0:T(8,128)(2,1)S(1)}, bf16[288,512]{1,0:T(8,128)(2,1)S(1)}, u32[]{:S(2)}, u32[]{:S(2)}) collective-permute-start(bf16[288,512]{1,0:T(8,128)(2,1)S(1)} %get-tuple-element.32), channel_id=1, source_target_pairs={{1,0},{2,1},{3,2},{4,3},{5,4},{6,5},{7,6},{8,7},{9,8},{10,9},{11,1... | collective-permute-start | bytes 884744 | tf_op jit(solution)/shard_map/ppermute | solution.py:323
  7.8 8.6 %collective-permute-start.3 = (bf16[32,2048]{1,0:T(8,128)(2,1)}, bf16[32,2048]{1,0:T(8,128)(2,1)S(1)}, u32[]{:S(2)}, u32[]{:S(2)}) collective-permute-start(bf16[32,2048]{1,0:T(8,128)(2,1)} %bitcast.16), channel_id=1, source_target_pairs={{0,14},{1,15},{2,0},{3,1},{4,2},{5,3},{6,4},{7,5},{8,6},{9,7},{10,... | collective-permute-start | bytes 393224 | tf_op jit(solution)/shard_map/ppermute | solution.py:316
  8.7 7.8 %collective-permute-start.2 = (bf16[32,2048]{1,0:T(8,128)(2,1)}, bf16[32,2048]{1,0:T(8,128)(2,1)S(1)}, u32[]{:S(2)}, u32[]{:S(2)}) collective-permute-start(bf16[32,2048]{1,0:T(8,128)(2,1)} %bitcast.17), channel_id=1, source_target_pairs={{0,2},{1,3},{2,4},{3,5},{4,6},{5,7},{6,8},{7,9},{8,10},{9,11},{10,... | collective-permute-start | bytes 393224 | tf_op jit(solution)/shard_map/ppermute | solution.py:316
  9.9 7.8 %collective-permute-start.5 = (bf16[32,2048]{1,0:T(8,128)(2,1)S(1)}, bf16[32,2048]{1,0:T(8,128)(2,1)S(1)}, u32[]{:S(2)}, u32[]{:S(2)}) collective-permute-start(bf16[32,2048]{1,0:T(8,128)(2,1)S(1)} %collective-permute-done.refs_1_), channel_id=1, source_target_pairs={{0,14},{1,15},{2,0},{3,1},{4,2},{5,3},{6,4},{7,5},{8,6},{9,7},{10,... | collective-permute-start | bytes 393224 | tf_op jit(solution)/shard_map/ppermute | solution.py:316
  11.9 6.5 %collective-permute-start.4 = (bf16[32,2048]{1,0:T(8,128)(2,1)S(1)}, bf16[32,2048]{1,0:T(8,128)(2,1)S(1)}, u32[]{:S(2)}, u32[]{:S(2)}) collective-permute-start(bf16[32,2048]{1,0:T(8,128)(2,1)S(1)} %collective-permute-done.refs_1_), channel_id=1, source_target_pairs={{0,2},{1,3},{2,4},{3,5},{4,6},{5,7},{6,8},{7,9},{8,10},{9,11},{10,... | collective-permute-start | bytes 393224 | tf_op jit(solution)/shard_map/ppermute | solution.py:316
  11.9 1.7 %copy-start.3 = (f32[16,144,144]{2,1,0:T(8,128)S(1)}, f32[16,144,144]{2,1,0:T(8,128)}, u32[]{:S(2)}) copy-start(f32[16,144,144]{2,1,0:T(8,128)} %bias_ref) | copy-start | bytes 3981316
  13.6 15.7 %copy-start.2 = (bf16[512,1536]{1,0:T(8,128)(2,1)S(1)}, bf16[512,1536]{1,0:T(8,128)(2,1)}, u32[]{:S(2)}) copy-start(bf16[512,1536]{1,0:T(8,128)(2,1)} %wqkv_ref.3) | copy-start | bytes 4718596
  13.6 15.7 %copy-start.4 = (bf16[512,512]{1,0:T(8,128)(2,1)S(1)}, bf16[512,512]{1,0:T(8,128)(2,1)}, u32[]{:S(2)}) copy-start(bf16[512,512]{1,0:T(8,128)(2,1)} %wout_ref.3) | copy-start | bytes 1572868
  13.6 15.7 %copy-start.7 = (f32[512]{0:T(512)S(1)}, f32[512]{0:T(512)}, u32[]{:S(2)}) copy-start(f32[512]{0:T(512)} %param.11) | copy-start | bytes 6148
  18.4 15.9 %collective-permute-start.9 = (bf16[64,2048]{1,0:T(8,128)(2,1)S(1)}, bf16[64,2048]{1,0:T(8,128)(2,1)S(1)}, u32[]{:S(2)}, u32[]{:S(2)}) collective-permute-start(bf16[64,2048]{1,0:T(8,128)(2,1)S(1)} %constant_dynamic-update-slice_fusion.2.refs_5_), channel_id=1, source_target_pairs={{0,14},{1,15},{2,0},{3,1},{4,2},{5,3},{6,4},{7,5},{8,6},{9,7},{10,... | collective-permute-start | bytes 786440 | tf_op jit(solution)/shard_map/ppermute | solution.py:316
  21.5 12.8 %collective-permute-start.8 = (bf16[64,2048]{1,0:T(8,128)(2,1)S(1)}, bf16[64,2048]{1,0:T(8,128)(2,1)S(1)}, u32[]{:S(2)}, u32[]{:S(2)}) collective-permute-start(bf16[64,2048]{1,0:T(8,128)(2,1)S(1)} %constant_dynamic-update-slice_fusion.refs_2_), channel_id=1, source_target_pairs={{0,2},{1,3},{2,4},{3,5},{4,6},{5,7},{6,8},{7,9},{8,10},{9,11},{10,... | collective-permute-start | bytes 786440 | tf_op jit(solution)/shard_map/ppermute | solution.py:316
  21.7 12.3 %collective-permute-start.6 = (bf16[2,72,512]{2,1,0:T(8,128)(2,1)S(1)}, bf16[2,72,512]{2,1,0:T(8,128)(2,1)S(1)}, u32[]{:S(2)}, u32[]{:S(2)}) collective-permute-start(bf16[2,72,512]{2,1,0:T(8,128)(2,1)S(1)} %pad_maximum_fusion), channel_id=1, source_target_pairs={{0,32},{32,64},{64,96},{96,128},{128,160},{160,192},{192,224},{1,3... | collective-permute-start | bytes 442376 | tf_op jit(solution)/shard_map/ppermute | solution.py:341
  24.9 9.4 %collective-permute-start.7 = (bf16[2,72,512]{2,1,0:T(8,128)(2,1)S(1)}, bf16[2,72,512]{2,1,0:T(8,128)(2,1)S(1)}, u32[]{:S(2)}, u32[]{:S(2)}) collective-permute-start(bf16[2,72,512]{2,1,0:T(8,128)(2,1)S(1)} %pad_maximum_fusion.1), channel_id=1, source_target_pairs={{32,0},{64,32},{96,64},{128,96},{160,128},{192,160},{224,192},{33,... | collective-permute-start | bytes 442376 | tf_op jit(solution)/shard_map/ppermute | solution.py:342
  29.3 3.0 %copy-start = (bf16[512,2048]{1,0:T(8,128)(2,1)S(1)}, bf16[512,2048]{1,0:T(8,128)(2,1)}, u32[]{:S(2)}) copy-start(bf16[512,2048]{1,0:T(8,128)(2,1)} %up_ref.3) | copy-start | bytes 6291460
  29.3 3.0 %copy-start.1 = (bf16[2048,512]{1,0:T(8,128)(2,1)S(1)}, bf16[2048,512]{1,0:T(8,128)(2,1)}, u32[]{:S(2)}) copy-start(bf16[2048,512]{1,0:T(8,128)(2,1)} %down_ref.3) | copy-start | bytes 6291460
  29.3 3.0 %copy-start.9 = (f32[512]{0:T(512)S(1)}, f32[512]{0:T(512)}, u32[]{:S(2)}) copy-start(f32[512]{0:T(512)} %param.15) | copy-start | bytes 6148
  34.3 13.1 %collective-permute-start.12 = (bf16[64,2048]{1,0:T(8,128)(2,1)S(1)}, bf16[64,2048]{1,0:T(8,128)(2,1)S(1)}, u32[]{:S(2)}, u32[]{:S(2)}) collective-permute-start(bf16[64,2048]{1,0:T(8,128)(2,1)S(1)} %collective-permute-done.8.refs_3_), channel_id=1, source_target_pairs={{0,2},{1,3},{2,4},{3,5},{4,6},{5,7},{6,8},{7,9},{8,10},{9,11},{10,... | collective-permute-start | bytes 786440 | tf_op jit(solution)/shard_map/ppermute | solution.py:316
  34.3 13.1 %collective-permute-start.13 = (bf16[64,2048]{1,0:T(8,128)(2,1)S(1)}, bf16[64,2048]{1,0:T(8,128)(2,1)S(1)}, u32[]{:S(2)}, u32[]{:S(2)}) collective-permute-start(bf16[64,2048]{1,0:T(8,128)(2,1)S(1)} %collective-permute-done.9.refs_6_), channel_id=1, source_target_pairs={{0,14},{1,15},{2,0},{3,1},{4,2},{5,3},{6,4},{7,5},{8,6},{9,7},{10,... | collective-permute-start | bytes 786440 | tf_op jit(solution)/shard_map/ppermute | solution.py:316
  37.7 9.1 %collective-permute-start.11 = (bf16[32,2048]{1,0:T(8,128)(2,1)S(1)}, bf16[32,2048]{1,0:T(8,128)(2,1)S(1)}, u32[]{:S(2)}, u32[]{:S(2)}) collective-permute-start(bf16[32,2048]{1,0:T(8,128)(2,1)S(1)} %slice.23), channel_id=1, source_target_pairs={{0,12},{1,13},{2,14},{3,15},{4,0},{5,1},{6,2},{7,3},{8,4},{9,5},{1... | collective-permute-start | bytes 393224 | tf_op jit(solution)/shard_map/ppermute | solution.py:316
  39.1 8.3 %collective-permute-start.10 = (bf16[32,2048]{1,0:T(8,128)(2,1)S(1)}, bf16[32,2048]{1,0:T(8,128)(2,1)S(1)}, u32[]{:S(2)}, u32[]{:S(2)}) collective-permute-start(bf16[32,2048]{1,0:T(8,128)(2,1)S(1)} %slice.22), channel_id=1, source_target_pairs={{0,4},{1,5},{2,6},{3,7},{4,8},{5,9},{6,10},{7,11},{8,12},{9,13},{1... | collective-permute-start | bytes 393224 | tf_op jit(solution)/shard_map/ppermute | solution.py:316
  40.7 3.5 %copy-start.8 = (f32[2048]{0:T(1024)S(1)}, f32[2048]{0:T(1024)}, u32[]{:S(2)}) copy-start(f32[2048]{0:T(1024)} %param.18) | copy-start | bytes 24580
  44.2 3.3 %copy-start.6 = (bf16[2048,32]{0,1:T(8,128)(2,1)S(1)}, bf16[2048,32]{0,1:T(8,128)(2,1)}, u32[]{:S(2)}) copy-start(bf16[2048,32]{0,1:T(8,128)(2,1)} %param.19) | copy-start | bytes 393220
  47.5 2.1 %collective-permute-start.14 = (bf16[4,160,512]{2,1,0:T(8,128)(2,1)S(1)}, bf16[4,160,512]{2,1,0:T(8,128)(2,1)S(1)}, u32[]{:S(2)}, u32[]{:S(2)}) collective-permute-start(bf16[4,160,512]{2,1,0:T(8,128)(2,1)S(1)} %edge_mlp.1.joined_ref), channel_id=1, source_target_pairs={{0,1},{1,0},{2,3},{3,2},{4,5},{5,4},{6,7},{7,6},{8,9},{9,8},{10,11... | collective-permute-start | bytes 1966088 | tf_op jit(solution)/shard_map/ppermute | solution.py:360
